TPU v7x, 32 devices: a whole 2x2x4 slice. The times are simulated.
32 devices in a mesh: slab: 8 (over z, y), batch: 4 (over x, core).
Axes of the slice: x: 2, y: 2, z: 4, core: 2. Of those that a mesh axis runs over, the one named last changes fastest.
Arguments:
- velocity_old: float32 [64, 64, 2, 3, 128], P('slab', 'batch'), may hold values from -6 to 6
- traction: bfloat16 [6144, 3, 169], P(('slab', 'batch')), may hold values from -6 to 6
- offsets: bfloat16 [6144, 3, 338], P(('slab', 'batch')), may hold values from -1 to 2
- owner_slab: int32 [6144, 1], P(('slab', 'batch')), may hold values from 0 to 7; in each aligned block of 192 rows (0 to 191, 192 to 383, ...) at most 48 rows name the same one
- anchor: int32 [6144, 3], P(('slab', 'batch')), may hold values from 1 to 253, as said below
- blocks: int32 [6144, 16], P(('slab', 'batch')), may hold values from 0 to 1023, as said below
- block_count: int32 [6144], P(('slab', 'batch')), may hold values from 8 to 16, as said below
- synthesis: bfloat16 [169, 338], replicated, may hold values from -0.5 to 0.5
- analysis: bfloat16 [169, 338], replicated, may hold values from -0.3125 to 0.3125
Outputs:
- velocity_new: float32 [64, 64, 2, 3, 128], P('slab', 'batch')
- velocity_coef: bfloat16 [6144, 3, 169], P(('slab', 'batch'))
Inputs may be any that keep to these rules, and one draw needn't show every extreme that they name: `owner_slab`: among the 192 cells of one device at most 48 name the same slab, and that bound is reached. `anchor`: in the owner's slab: first coordinate 1 to 5, second 1 to 61, third 1 to 125 within its tile of 128 points. `blocks`: the first block_count entries of a cell are distinct lines within two cells of its anchor in the first two dimensions, in its anchor's tile along the third; the remaining entries are padding with any tile number. `block_count`: some cells of every device use all 16 blocks.
All inputs are finite; a program needn't handle non-finite values.
Results may differ from a plain program's by a relative error of at most 0.012.
Values may be sent and summed in bfloat16 or wider, within the bound.
No kernel may reach another device: no remote copies, remote signals or barrier semaphores. Data moves between devices by JAX's collectives and lax.ppermute only.
A program may use at most 64 MiB of HBM per device.

v0:
```python
import math

import jax
import jax.numpy as jnp
from jax import lax
from jax.sharding import PartitionSpec as P

SWEEPS = 2
GX = 8
NY = 64
NZ = 256


kernel_width = 0.8
kernel_norm = 1.0 / (0.8 * math.sqrt(2.0 * math.pi))
coupling = 2.0


def padded_2(block, sides, width):
    for axis, dim in sides:
        count = lax.axis_size(axis)
        forward = [(i, i + 1) for i in range(count - 1)]
        backward = [(target, source) for source, target in forward]
        low = lax.ppermute(
            lax.slice_in_dim(block, block.shape[dim] - width, None, axis=dim), axis, forward
        )
        high = lax.ppermute(lax.slice_in_dim(block, 0, width, axis=dim), axis, backward)
        block = jnp.concatenate([low, block, high], axis=dim)
    return block


def kernel_value(distance):
    scaled = distance / kernel_width
    return jnp.exp(-0.5 * scaled * scaled) * kernel_norm


def stencil_weights(anchor_part, offset_part, block_part, count_part):
    layers = NZ // 128
    points = anchor_part[:, :, None].astype(jnp.float32) + offset_part.astype(jnp.float32)
    tile_x = (block_part // (NY * layers)).astype(jnp.float32)
    tile_y = (block_part // layers % NY).astype(jnp.float32)
    live_mask = (jnp.arange(block_part.shape[1])[None, :] < count_part[:, None]).astype(jnp.float32)
    weight_xy = (
        kernel_value(points[:, 0, None, :] - tile_x[:, :, None])
        * kernel_value(points[:, 1, None, :] - tile_y[:, :, None])
        * live_mask[:, :, None]
    )
    z_root = (anchor_part[:, 2] // 128 * 128).astype(jnp.float32)
    heights = z_root[:, None, None] + jnp.arange(128, dtype=jnp.float32)[None, None, :]
    weight_z = kernel_value(points[:, 2, :, None] - heights).astype(jnp.bfloat16)
    return (weight_xy, weight_z)


def neighbours(padded):
    centre = padded[1:-1, 1:-1]
    total = padded[2:, 1:-1] + padded[:-2, 1:-1] + padded[1:-1, 2:] + padded[1:-1, :-2]
    zero_edge = jnp.zeros(centre.shape[:2] + (1, centre.shape[3], 1), centre.dtype)
    after = jnp.concatenate([centre[:, :, 1:, :, :1], zero_edge], axis=2)
    before = jnp.concatenate([zero_edge, centre[:, :, :-1, :, -1:]], axis=2)
    upper = jnp.concatenate([centre[..., 1:], after], axis=-1)
    lower = jnp.concatenate([before, centre[..., :-1]], axis=-1)
    return total + upper + lower


def relax(drive, widen):
    state = drive
    for sweep_index in range(SWEEPS):
        state = (drive + coupling * neighbours(widen(state))) / (1.0 + 6.0 * coupling)
    return state


def local(
    velocity_old, traction, offsets, owner_slab, anchor, blocks, block_count, synthesis, analysis
):
    cell_total = traction.shape[0]
    slab_count = lax.axis_size("slab")
    capacity = 2 * cell_total // slab_count
    slot_total = slab_count * capacity
    destination = owner_slab[:, 0]
    member = (destination[:, None] == jnp.arange(slab_count)[None, :]).astype(jnp.int32)
    bucket_rank = jnp.sum((jnp.cumsum(member, axis=0) - member) * member, axis=1)
    slot_index = destination * capacity + bucket_rank

    def placed(values):
        empty = jnp.zeros((slot_total,) + values.shape[1:], values.dtype)
        return empty.at[slot_index].set(values)

    sent_coef, sent_offsets = (
        lax.all_to_all(placed(traction), "slab", split_axis=0, concat_axis=0, tiled=True),
        lax.all_to_all(placed(offsets), "slab", split_axis=0, concat_axis=0, tiled=True),
    )
    sent_anchor, sent_blocks, sent_count = (
        lax.all_to_all(placed(anchor), "slab", split_axis=0, concat_axis=0, tiled=True),
        lax.all_to_all(placed(blocks), "slab", split_axis=0, concat_axis=0, tiled=True),
        lax.all_to_all(placed(block_count), "slab", split_axis=0, concat_axis=0, tiled=True),
    )
    block_rows = 16
    steps_total = slot_total // block_rows

    def grouped(values):
        return values.reshape((steps_total, block_rows) + values.shape[1:])

    received = tuple(
        (
            grouped(values)
            for values in (sent_coef, sent_offsets, sent_anchor, sent_blocks, sent_count)
        )
    )
    layers = NZ // 128

    def spread_step(grid_sum, piece):
        coef_part, offset_part, anchor_part, block_part, count_part = piece
        weight_xy, weight_z = stencil_weights(anchor_part, offset_part, block_part, count_part)
        forces = jnp.einsum("ckl,lq->ckq", coef_part, synthesis, preferred_element_type=jnp.float32)
        weighted = (forces[:, None] * weight_xy[:, :, None]).astype(jnp.bfloat16)
        tile_terms = jnp.einsum(
            "cbkq,cqi->cbki", weighted, weight_z, preferred_element_type=jnp.float32
        )
        return (grid_sum.at[block_part.reshape(-1)].add(tile_terms.reshape(-1, 3, 128)), None)

    start = jnp.zeros((GX * NY * layers, 3, 128), jnp.float32)
    partial_value, ignored = lax.scan(spread_step, start, received)
    partial_value = partial_value.reshape(GX, NY, layers, 3, 128)
    drive = velocity_old + lax.psum_scatter(
        partial_value.astype(jnp.bfloat16), "batch", scatter_dimension=1, tiled=True
    ).astype(jnp.float32)

    def widen(state):
        return padded_2(state.astype(jnp.bfloat16), (("slab", 0), ("batch", 1)), 1).astype(
            state.dtype
        )

    velocity_new = relax(drive, widen)
    slab_velocity = lax.all_gather(velocity_new.astype(jnp.bfloat16), "batch", axis=1, tiled=True)
    flat_velocity = slab_velocity.reshape(-1, 3, 128)

    def sample_step(piece):
        offset_part, anchor_part, block_part, count_part = piece
        weight_xy, weight_z = stencil_weights(anchor_part, offset_part, block_part, count_part)
        gathered = flat_velocity[block_part]
        projected = jnp.einsum(
            "cbki,cqi->cbkq", gathered, weight_z, preferred_element_type=jnp.float32
        )
        return jnp.sum(projected * weight_xy[:, :, None, :], axis=1).astype(jnp.bfloat16)

    sampled = lax.map(sample_step, received[1:])
    sampled = sampled.reshape((slot_total,) + sampled.shape[2:])
    returned = lax.all_to_all(
        jnp.einsum("ckq,lq->ckl", sampled, analysis, preferred_element_type=jnp.float32).astype(
            jnp.bfloat16
        ),
        "slab",
        split_axis=0,
        concat_axis=0,
        tiled=True,
    )
    velocity_coef = returned[slot_index]
    return (velocity_new, velocity_coef)


def solution(mesh):
    in_specs = (
        P("slab", "batch", None, None, None),
        P(("slab", "batch"), None, None),
        P(("slab", "batch"), None, None),
        P(("slab", "batch"), None),
        P(("slab", "batch"), None),
        P(("slab", "batch"), None),
        P(("slab", "batch")),
        P(),
        P(),
    )
    out_specs = (P("slab", "batch", None, None, None), P(("slab", "batch"), None, None))
    return jax.shard_map(local, mesh=mesh, in_specs=in_specs, out_specs=out_specs, check_vma=False)
```

profile of v0, /device:TPU:0, one launch (start us, length us, event | category | flops | bytes accessed | tf_op | source)
XLA Modules:
  0.0 638.2 jit_solution(9693712858319888979)
XLA Ops:
  56.3 21.5 %scatter_fusion.2 = bf16[384,3,338]{2,1,0:T(4,128)(2,1)} fusion(bf16[384,3,338]{2,1,0:T(4,128)(2,1)} %broadcast_in_dim.23, s32[192]{0:T(256)S(1)} %bitcast.197, bf16[192,3,338]{2,1,0:T(4,128)(2,1)S(1)} %copy.120), kind=kCustom, calls=%fused_computation.6 | custom fusion | bytes 1168896 | tf_op jit(solution)/shard_map/scatter | solution.py:86
  90.2 19.0 %all-to-all-done.3 = bf16[384,3,338]{2,1,0:T(4,128)(2,1)S(1)} async-done(((bf16[384,3,338]{2,1,0:T(4,128)(2,1)}), bf16[384,3,338]{2,1,0:T(4,128)(2,1)S(1)}, u32[]{:S(2)}, u32[]{:S(2)}) %all-to-all-start.3) | async-done | bytes 778784 | tf_op jit(solution)/shard_map/all_to_all | solution.py:90
  110.6 309.3 %while.26 = (s32[]{:T(128)}, f32[1024,3,128]{2,1,0:T(4,128)S(1)}, s32[24,16,16]{2,1,0:T(8,128)S(1)}, bf16[24,16,3,169]{3,1,2,0:T(8,128)(2,1)}, bf16[169,338]{1,0...) while((s32[]{:T(128)}, f32[1024,3,128]{2,1,0:T(4,128)S(1)}, ...), condition=%wide.region_10.11_spmd, body=%wide.region_8.10_spmd.sunk | while | flops 77793472 | bytes 3774449 | solution.py:122
  114.9 8.3 %scatter_fusion = f32[1024,3,128]{2,1,0:T(4,128)S(1)} fusion(f32[1024,3,128]{2,1,0:T(4,128)S(1)} %get-tuple-element.553, s32[256]{0:T(256)S(1)} %bitcast.190, f32[256,3,128]{2,1,0:T(4,128)S(1)} %copy.165), kind=kCustom, calls=%fused_computation.2.clone.1 | custom fusion | flops 98304 | bytes 1180672 | tf_op jit(solution)/shard_map/while/body/eval_jaxpr/scatter-add | solution.py:119
  127.7 8.3 %scatter_fusion = f32[1024,3,128]{2,1,0:T(4,128)S(1)} fusion(f32[1024,3,128]{2,1,0:T(4,128)S(1)} %get-tuple-element.553, s32[256]{0:T(256)S(1)} %bitcast.190, f32[256,3,128]{2,1,0:T(4,128)S(1)} %copy.165), kind=kCustom, calls=%fused_computation.2.clone.1 | custom fusion | flops 98304 | bytes 1180672 | tf_op jit(solution)/shard_map/while/body/eval_jaxpr/scatter-add | solution.py:119
  140.4 8.7 %scatter_fusion = f32[1024,3,128]{2,1,0:T(4,128)S(1)} fusion(f32[1024,3,128]{2,1,0:T(4,128)S(1)} %get-tuple-element.553, s32[256]{0:T(256)S(1)} %bitcast.190, f32[256,3,128]{2,1,0:T(4,128)S(1)} %copy.165), kind=kCustom, calls=%fused_computation.2.clone.1 | custom fusion | flops 98304 | bytes 1180672 | tf_op jit(solution)/shard_map/while/body/eval_jaxpr/scatter-add | solution.py:119
  153.4 8.3 %scatter_fusion = f32[1024,3,128]{2,1,0:T(4,128)S(1)} fusion(f32[1024,3,128]{2,1,0:T(4,128)S(1)} %get-tuple-element.553, s32[256]{0:T(256)S(1)} %bitcast.190, f32[256,3,128]{2,1,0:T(4,128)S(1)} %copy.165), kind=kCustom, calls=%fused_computation.2.clone.1 | custom fusion | flops 98304 | bytes 1180672 | tf_op jit(solution)/shard_map/while/body/eval_jaxpr/scatter-add | solution.py:119
  178.9 8.6 %scatter_fusion = f32[1024,3,128]{2,1,0:T(4,128)S(1)} fusion(f32[1024,3,128]{2,1,0:T(4,128)S(1)} %get-tuple-element.553, s32[256]{0:T(256)S(1)} %bitcast.190, f32[256,3,128]{2,1,0:T(4,128)S(1)} %copy.165), kind=kCustom, calls=%fused_computation.2.clone.1 | custom fusion | flops 98304 | bytes 1180672 | tf_op jit(solution)/shard_map/while/body/eval_jaxpr/scatter-add | solution.py:119
  217.3 8.7 %scatter_fusion = f32[1024,3,128]{2,1,0:T(4,128)S(1)} fusion(f32[1024,3,128]{2,1,0:T(4,128)S(1)} %get-tuple-element.553, s32[256]{0:T(256)S(1)} %bitcast.190, f32[256,3,128]{2,1,0:T(4,128)S(1)} %copy.165), kind=kCustom, calls=%fused_computation.2.clone.1 | custom fusion | flops 98304 | bytes 1180672 | tf_op jit(solution)/shard_map/while/body/eval_jaxpr/scatter-add | solution.py:119
  230.4 8.3 %scatter_fusion = f32[1024,3,128]{2,1,0:T(4,128)S(1)} fusion(f32[1024,3,128]{2,1,0:T(4,128)S(1)} %get-tuple-element.553, s32[256]{0:T(256)S(1)} %bitcast.190, f32[256,3,128]{2,1,0:T(4,128)S(1)} %copy.165), kind=kCustom, calls=%fused_computation.2.clone.1 | custom fusion | flops 98304 | bytes 1180672 | tf_op jit(solution)/shard_map/while/body/eval_jaxpr/scatter-add | solution.py:119
  243.1 8.7 %scatter_fusion = f32[1024,3,128]{2,1,0:T(4,128)S(1)} fusion(f32[1024,3,128]{2,1,0:T(4,128)S(1)} %get-tuple-element.553, s32[256]{0:T(256)S(1)} %bitcast.190, f32[256,3,128]{2,1,0:T(4,128)S(1)} %copy.165), kind=kCustom, calls=%fused_computation.2.clone.1 | custom fusion | flops 98304 | bytes 1180672 | tf_op jit(solution)/shard_map/while/body/eval_jaxpr/scatter-add | solution.py:119
  256.2 9.1 %scatter_fusion = f32[1024,3,128]{2,1,0:T(4,128)S(1)} fusion(f32[1024,3,128]{2,1,0:T(4,128)S(1)} %get-tuple-element.553, s32[256]{0:T(256)S(1)} %bitcast.190, f32[256,3,128]{2,1,0:T(4,128)S(1)} %copy.165), kind=kCustom, calls=%fused_computation.2.clone.1 | custom fusion | flops 98304 | bytes 1180672 | tf_op jit(solution)/shard_map/while/body/eval_jaxpr/scatter-add | solution.py:119
  282.4 8.4 %scatter_fusion = f32[1024,3,128]{2,1,0:T(4,128)S(1)} fusion(f32[1024,3,128]{2,1,0:T(4,128)S(1)} %get-tuple-element.553, s32[256]{0:T(256)S(1)} %bitcast.190, f32[256,3,128]{2,1,0:T(4,128)S(1)} %copy.165), kind=kCustom, calls=%fused_computation.2.clone.1 | custom fusion | flops 98304 | bytes 1180672 | tf_op jit(solution)/shard_map/while/body/eval_jaxpr/scatter-add | solution.py:119
  295.2 9.1 %scatter_fusion = f32[1024,3,128]{2,1,0:T(4,128)S(1)} fusion(f32[1024,3,128]{2,1,0:T(4,128)S(1)} %get-tuple-element.553, s32[256]{0:T(256)S(1)} %bitcast.190, f32[256,3,128]{2,1,0:T(4,128)S(1)} %copy.165), kind=kCustom, calls=%fused_computation.2.clone.1 | custom fusion | flops 98304 | bytes 1180672 | tf_op jit(solution)/shard_map/while/body/eval_jaxpr/scatter-add | solution.py:119
  334.1 8.8 %scatter_fusion = f32[1024,3,128]{2,1,0:T(4,128)S(1)} fusion(f32[1024,3,128]{2,1,0:T(4,128)S(1)} %get-tuple-element.553, s32[256]{0:T(256)S(1)} %bitcast.190, f32[256,3,128]{2,1,0:T(4,128)S(1)} %copy.165), kind=kCustom, calls=%fused_computation.2.clone.1 | custom fusion | flops 98304 | bytes 1180672 | tf_op jit(solution)/shard_map/while/body/eval_jaxpr/scatter-add | solution.py:119
  347.3 8.3 %scatter_fusion = f32[1024,3,128]{2,1,0:T(4,128)S(1)} fusion(f32[1024,3,128]{2,1,0:T(4,128)S(1)} %get-tuple-element.553, s32[256]{0:T(256)S(1)} %bitcast.190, f32[256,3,128]{2,1,0:T(4,128)S(1)} %copy.165), kind=kCustom, calls=%fused_computation.2.clone.1 | custom fusion | flops 98304 | bytes 1180672 | tf_op jit(solution)/shard_map/while/body/eval_jaxpr/scatter-add | solution.py:119
  360.0 8.3 %scatter_fusion = f32[1024,3,128]{2,1,0:T(4,128)S(1)} fusion(f32[1024,3,128]{2,1,0:T(4,128)S(1)} %get-tuple-element.553, s32[256]{0:T(256)S(1)} %bitcast.190, f32[256,3,128]{2,1,0:T(4,128)S(1)} %copy.165), kind=kCustom, calls=%fused_computation.2.clone.1 | custom fusion | flops 98304 | bytes 1180672 | tf_op jit(solution)/shard_map/while/body/eval_jaxpr/scatter-add | solution.py:119
  372.7 8.7 %scatter_fusion = f32[1024,3,128]{2,1,0:T(4,128)S(1)} fusion(f32[1024,3,128]{2,1,0:T(4,128)S(1)} %get-tuple-element.553, s32[256]{0:T(256)S(1)} %bitcast.190, f32[256,3,128]{2,1,0:T(4,128)S(1)} %copy.165), kind=kCustom, calls=%fused_computation.2.clone.1 | custom fusion | flops 98304 | bytes 1180672 | tf_op jit(solution)/shard_map/while/body/eval_jaxpr/scatter-add | solution.py:119
  385.8 8.3 %scatter_fusion = f32[1024,3,128]{2,1,0:T(4,128)S(1)} fusion(f32[1024,3,128]{2,1,0:T(4,128)S(1)} %get-tuple-element.553, s32[256]{0:T(256)S(1)} %bitcast.190, f32[256,3,128]{2,1,0:T(4,128)S(1)} %copy.165), kind=kCustom, calls=%fused_computation.2.clone.1 | custom fusion | flops 98304 | bytes 1180672 | tf_op jit(solution)/shard_map/while/body/eval_jaxpr/scatter-add | solution.py:119
  411.2 8.7 %scatter_fusion = f32[1024,3,128]{2,1,0:T(4,128)S(1)} fusion(f32[1024,3,128]{2,1,0:T(4,128)S(1)} %get-tuple-element.553, s32[256]{0:T(256)S(1)} %bitcast.190, f32[256,3,128]{2,1,0:T(4,128)S(1)} %copy.165), kind=kCustom, calls=%fused_computation.2.clone.1 | custom fusion | flops 98304 | bytes 1180672 | tf_op jit(solution)/shard_map/while/body/eval_jaxpr/scatter-add | solution.py:119
  421.9 30.9 %reduce-scatter.2.cloned.1.call-done = bf16[8,16,2,3,128]{4,0,3,2,1:T(8,128)(2,1)} async-done(((bf16[8,64,2,3,128]{4,0,3,2,1:T(8,128)(2,1)}), bf16[8,16,2,3,128]{4,0,3,2,1:T(8,128)(2,1)}) %reduce-scatter.2.cloned.1.call-update) | async-done | bytes 196624 | tf_op jit(solution)/shard_map/reduce_scatter | solution.py:124
  488.1 9.4 %all_gather.3 = bf16[8,64,2,3,128]{4,0,3,2,1:T(8,128)(2,1)S(1)} all-gather(bf16[8,16,2,3,128]{4,0,3,2,1:T(8,128)(2,1)S(1)} %get-tuple-element.399), channel_id=1, replica_groups=mesh['slab'=8,'batch'=4] {'batch'}, dimensions={1}, use_global_device_ids=true | all-gather | bytes 983040 | tf_op jit(solution)/shard_map/all_gather | solution.py:134
  499.0 107.4 %while.27 = (s32[]{:T(128)}, bf16[24,16,3,338]{3,2,1,0:T(4,128)(2,1)}, s32[24,16,16]{2,1,0:T(8,128)S(1)}, bf16[1024,3,128]{2,1,0:T(4,128)(2,1)S(1)}, s32[24,16,3...) while((s32[]{:T(128)}, ...), condition=%wide.region_14.15_spmd, body=%wide.region_12.14_spmd.sunk | while | flops 72195744 | bytes 1725229 | solution.py:146
  616.5 11.0 %all-to-all-done.5 = bf16[8,2,12168]{2,1,0:T(2,128)(2,1)S(1)} async-done(((bf16[8,2,12168]{2,1,0:T(2,128)(2,1)}), bf16[8,2,12168]{2,1,0:T(2,128)(2,1)S(1)}, u32[]{:S(2)}, u32[]{:S(2)}) %all-to-all-start.5) | async-done | bytes 389408 | tf_op jit(solution)/shard_map/all_to_all | solution.py:148
  (881 shorter events, 382.8 us)
Async XLA Ops:
  7.2 599.3 %copy-start = (bf16[169,338]{1,0:T(8,128)(2,1)S(1)}, bf16[169,338]{1,0:T(8,128)(2,1)}, u32[]{:S(2)}) copy-start(bf16[169,338]{1,0:T(8,128)(2,1)} %param.21) | copy-start | bytes 342736
  12.3 13.7 %all-to-all-start.4 = ((s32[8,48,1]{1,2,0:T(1,128)}), s32[8,48,1]{1,2,0:T(1,128)S(1)}, u32[]{:S(2)}, u32[]{:S(2)}) async-start(s32[8,48,1]{1,2,0:T(1,128)} %all_to_all.33), calls=%async_computation.4 | async-start | bytes 8192 | tf_op jit(solution)/shard_map/all_to_all | solution.py:95
  25.9 9.8 %all-to-all-start.2 = ((s32[8,1,144]{2,1,0:T(1,128)}), s32[8,1,144]{2,1,0:T(1,128)S(1)}, u32[]{:S(2)}, u32[]{:S(2)}) async-start(s32[8,1,144]{2,1,0:T(1,128)} %reshape.641), calls=%async_computation.2 | async-start | bytes 16384 | tf_op jit(solution)/shard_map/all_to_all | solution.py:93
  35.7 13.0 %all-to-all-start = ((s32[8,1,768]{2,1,0:T(1,128)}), s32[8,1,768]{2,1,0:T(1,128)S(1)}, u32[]{:S(2)}, u32[]{:S(2)}) async-start(s32[8,1,768]{2,1,0:T(1,128)} %reshape.637), calls=%async_computation | async-start | bytes 49152 | tf_op jit(solution)/shard_map/all_to_all | solution.py:94
  40.3 14.3 %copy-start.4 = (bf16[192,3,338]{2,0,1:T(8,128)(2,1)S(1)}, bf16[192,3,338]{2,0,1:T(8,128)(2,1)}, u32[]{:S(2)}) copy-start(bf16[192,3,338]{2,0,1:T(8,128)(2,1)} %param.15) | copy-start | bytes 1168132
  48.7 29.2 %all-to-all-start.1 = ((bf16[8,2,12168]{2,1,0:T(2,128)(2,1)}), bf16[8,2,12168]{2,1,0:T(2,128)(2,1)S(1)}, u32[]{:S(2)}, u32[]{:S(2)}) async-start(bf16[8,2,12168]{2,1,0:T(2,128)(2,1)} %reshape.639), calls=%async_computation.1 | async-start | bytes 786432 | tf_op jit(solution)/shard_map/all_to_all | solution.py:89
  77.9 31.3 %all-to-all-start.3 = ((bf16[384,3,338]{2,1,0:T(4,128)(2,1)}), bf16[384,3,338]{2,1,0:T(4,128)(2,1)S(1)}, u32[]{:S(2)}, u32[]{:S(2)}) async-start(bf16[384,3,338]{2,1,0:T(4,128)(2,1)} %scatter_fusion.2), calls=%async_computation.3 | async-start | bytes 2359296 | tf_op jit(solution)/shard_map/all_to_all | solution.py:90
  83.8 369.0 %reduce-scatter.2.cloned.1.call-start = ((), (), s32[]{:S(2)}) async-start(), calls=%async_computation.7 | async-start | bytes 983040 | tf_op jit(solution)/shard_map/reduce_scatter | solution.py:124
  109.3 1.3 copy-start.2
  419.9 32.9 %copy-start.1 = (f32[8,16,2,3,128]{4,2,3,1,0:T(2,128)S(1)}, f32[8,16,2,3,128]{4,2,3,1,0:T(2,128)}, u32[]{:S(2)}) copy-start(f32[8,16,2,3,128]{4,2,3,1,0:T(2,128)} %param.13) | copy-start | bytes 1179652
  454.0 15.2 %copy-start.3 = (bf16[8,16,2,3,128]{4,0,3,2,1:T(8,128)(2,1)S(1)}, bf16[8,16,2,3,128]{4,0,3,2,1:T(8,128)(2,1)}, u32[]{:S(2)}) copy-start(bf16[8,16,2,3,128]{4,0,3,2,1:T(8,128)(2,1)} %reduce-scatter.2.cloned.1.call-done) | copy-start | bytes 589828
  454.1 5.1 collective-permute-start
  457.4 6.0 collective-permute-start.1
  463.5 2.8 collective-permute-start.2
  464.8 3.9 collective-permute-start.3
  469.8 6.0 collective-permute-start.4
  474.0 6.0 collective-permute-start.5
  480.1 4.3 collective-permute-start.6
  483.1 4.0 collective-permute-start.7
  610.9 16.6 %all-to-all-start.5 = ((bf16[8,2,12168]{2,1,0:T(2,128)(2,1)}), bf16[8,2,12168]{2,1,0:T(2,128)(2,1)S(1)}, u32[]{:S(2)}, u32[]{:S(2)}) async-start(bf16[8,2,12168]{2,1,0:T(2,128)(2,1)} %reshape.643), calls=%async_computation.6 | async-start | bytes 786432 | tf_op jit(solution)/shard_map/all_to_all | solution.py:148
Sparse Core Ops, SparseCore 0:
  422.0 30.7 reduce-scatter.1
where the time goes:
time: 645 us; the launch traced here: 638 us
  other arithmetic  276 us (43%)
  local copies, waits for them, and re-layouts  109 us (17%)
  matrix products  95.1 us (15%)
  waiting for transfers between devices  82.8 us (13%)
  starting transfers between devices  47.8 us (7%)
  between operations  14.4 us (2%)
  blocking collectives  9.44 us (1%)
    scatter-add x24, other arithmetic, spread_step(): grid_sum.at[block_part.reshape(-1)].add(tile_terms.reshape(-1, 3, 128))  204 us
    add x48, other arithmetic, stencil_weights(): anchor_part[:, :, None].astype(jnp.float32)  40.7 us
    dot_general x24, matrix products, spread_step(): jnp.einsum('cbkq,cqi->cbki', weighted, weight_z, preferred_element_type=j...  40.2 us
    dot_general x24, matrix products, sample_step(): jnp.einsum('cbki,cqi->cbkq', gathered, weight_z, preferred_element_type=j...  32.1 us
    scatter x5, local copies, waits for them, and re-layouts, placed(): return empty.at[slot_index].set(values)  31.2 us
    reduce_scatter x1, waiting for transfers between devices, local(): lax.psum_scatter(partial_value.astype(jnp.bfloat16), 'batch', scatter_dim...  30.9 us
    gather x24, local copies, waits for them, and re-layouts, sample_step(): gathered = flat_velocity[block_part]  23.6 us
    dot_general x24, matrix products, spread_step(): jnp.einsum('ckl,lq->ckq', coef_part, synthesis, preferred_element_type=jn...  21.1 us
  transfers between devices with their start and end apart: 15, of which 11 were waited for; matrix products, arithmetic and copies ran while one was open for 7% of the time, Pallas kernels for 0%

commit v1 on v0

v1 whole, which is shorter than its diff:
```python
import math

import jax
import jax.numpy as jnp
from jax import lax
from jax.experimental import pallas as pl
from jax.experimental.pallas import tpu as pltpu
from jax.sharding import PartitionSpec as P

SWEEPS = 2
TILE = 128
GROUP = 8
DEAD = 64.0

kernel_width = 0.8
kernel_norm = 1.0 / (0.8 * math.sqrt(2.0 * math.pi))
coupling = 2.0
scale = math.sqrt(0.5 / math.log(2.0)) / kernel_width
norm_bits = math.log2(kernel_norm)

f32 = jnp.float32
bf16 = jnp.bfloat16


def round_up(value, step):
    return -(-value // step) * step


def iota(shape, dim):
    return lax.broadcasted_iota(jnp.int32, shape, dim)


def one_hot(mask):
    return jnp.where(mask, 1.0, 0.0).astype(bf16)


def dot(a, b, ca=1, cb=0):
    return lax.dot_general(a, b, (((ca,), (cb,)), ((), ())), preferred_element_type=f32)


def vmem(count=1):
    return [pl.BlockSpec(memory_space=pltpu.VMEM)] * count


def smem(count=1):
    return [pl.BlockSpec(memory_space=pltpu.SMEM)] * count


params = pltpu.CompilerParams(vmem_limit_bytes=48 * 1024 * 1024)


class Sizes:
    def __init__(self, terms, points, stencil):
        self.terms, self.points, self.stencil = terms, points, stencil
        self.qw = round_up(points, TILE)
        self.cw = round_up(3 * terms, TILE)
        self.width = 3 * self.qw + self.cw
        self.mt = points // TILE * TILE
        self.mo = points - self.mt
        self.meta = 2 * stencil + 4
        self.rows = round_up(self.meta, 8)


def place_terms(sz, k):
    shape = (sz.cw, sz.terms)
    return one_hot(iota(shape, 0) == iota(shape, 1) + k * sz.terms)


def pack_kernel(sz, slabs, cap, ny, layers, owner, anchor, blocks, count, trac, offs, send, slot_out, rec):
    cells = owner.shape[1]
    slots = slabs * cap
    own = owner[...]
    member = one_hot(own == iota((slabs, cells), 0))
    before = one_hot(iota((cells, cells), 0) < iota((cells, cells), 1))
    rank = jnp.sum(member.astype(f32) * dot(member, before), axis=0, keepdims=True)
    slot = own * cap + rank.astype(jnp.int32)
    slot_out[...] = slot
    place = one_hot(slot == iota((slots, cells), 0))

    tile = blocks[...].astype(f32)
    anchors = anchor[...].astype(f32)
    tile_x = jnp.floor((tile + 0.5) * (1.0 / (ny * layers)))
    tile_y = jnp.floor((tile + 0.5) * (1.0 / layers)) - tile_x * ny
    live = iota(tile.shape, 0) < count[...]
    dx = jnp.where(live, tile_x - anchors[0:1], DEAD)
    dy = jnp.where(live, tile_y - anchors[1:2], DEAD)

    rec[...] = jnp.zeros(rec.shape, bf16)
    for k in range(3):
        rec[:, k * sz.qw : k * sz.qw + sz.points] = offs[k]
    base = sz.mo
    meta = jnp.zeros((cells, TILE), f32)
    ones = jnp.ones((1, cells), f32)
    for part in (dx, dy, anchors, ones):
        shape = (part.shape[0], TILE)
        where = one_hot(iota(shape, 1) == iota(shape, 0) + base)
        meta = meta + dot(part.astype(bf16), where, 0, 0)
        base += part.shape[0]
    rec[:, sz.mt : sz.mt + TILE] = rec[:, sz.mt : sz.mt + TILE] + meta.astype(bf16)
    coef = jnp.zeros((cells, sz.cw), f32)
    for k in range(3):
        coef = coef + dot(trac[k], place_terms(sz, k), 0, 1)
    rec[:, 3 * sz.qw :] = coef.astype(bf16)
    send[...] = dot(place, rec[...]).astype(bf16)


def meta_table(sz, recv):
    shape = (sz.rows, TILE)
    pick = one_hot((iota(shape, 1) == iota(shape, 0) + sz.mo) & (iota(shape, 0) < sz.meta))
    return dot(pick, recv[:, sz.mt : sz.mt + TILE], 1, 1)


def height_weights(pz_row):
    heights = iota((TILE, TILE), 0).astype(f32) * scale
    away = jnp.broadcast_to(pz_row, (TILE, TILE)) - heights
    return jnp.exp2(norm_bits - away * away).astype(bf16)


def line_weights(ox_row, oy_row, dx, dy):
    ex = ox_row - dx
    ey = oy_row - dy
    return jnp.exp2(2.0 * norm_bits - ex * ex - ey * ey)


def column_group(sz, cols, g):
    per = TILE // GROUP
    wide = cols[g // per]
    return pltpu.roll(wide, (TILE - GROUP * (g % per)) % TILE, 1)


def spread_kernel(
    sz, gx, ny, nyb, layers, where, recv, synthesis, vold,
    keep, send, points, cols, rows_out,
    grid, forces, expand, terms, rows_v, rows_s, sem,
):
    slots = recv.shape[0]
    planes = 3 * layers
    table = meta_table(sz, recv)
    expand[...] = jnp.zeros(expand.shape, bf16)
    for k in range(3):
        expand[:, k * sz.qw : k * sz.qw + sz.points] = dot(place_terms(sz, k), synthesis[...]).astype(bf16)
    dense = recv[:, : 3 * sz.qw].astype(f32)
    forces[...] = dot(recv[:, 3 * sz.qw :], expand[...])

    stencil = sz.stencil
    dx, dy = table[:stencil], table[stencil : 2 * stencil]
    ax, ay, az = (table[2 * stencil + d : 2 * stencil + d + 1] for d in range(3))
    layer = jnp.floor((az + 0.5) * (1.0 / TILE))
    line = ((ax + dx) * planes + layer) * ny + ay + dy
    line = jnp.where((dx < 0.5 * DEAD) & (ax > 0.5), line, float(gx * planes * ny))
    rows_v[...] = line.astype(jnp.int32)
    copy = pltpu.make_async_copy(rows_v, rows_s, sem)
    copy.start()
    rows_out[...] = rows_v[...]
    for t in range(slots // TILE):
        cols[t] = table[: 2 * stencil, t * TILE : (t + 1) * TILE] * scale

    at = sz.mo + 2 * stencil + 2
    az_col = dense[:, sz.mt + at : sz.mt + at + 1]
    az_col = az_col - TILE * jnp.floor((az_col + 0.5) * (1.0 / TILE))
    points[:, : 2 * sz.qw] = dense[:, : 2 * sz.qw] * scale
    points[:, 2 * sz.qw :] = (dense[:, 2 * sz.qw : 3 * sz.qw] + az_col) * scale

    grid[...] = jnp.zeros(grid.shape, f32)
    y_at = pl.multiple_of(where[1] * nyb, 8)
    for x in range(gx):
        for r in range(planes):
            grid[pl.ds((x * planes + r) * ny + y_at, nyb), :] = vold[pl.ds(x * nyb * planes + r, nyb, stride=planes), :]
    copy.wait()

    def step(g, carry):
        first = pl.multiple_of(g * GROUP, GROUP)
        pts = points[pl.ds(first, GROUP), :]
        frc = forces[pl.ds(first, GROUP), :]
        col = column_group(sz, cols, g)
        for u in range(GROUP):
            cx, cy = col[:stencil, u : u + 1], col[stencil:, u : u + 1]
            total_terms = jnp.zeros((3 * stencil, TILE), f32)
            for t in range(0, sz.qw, TILE):
                w = line_weights(pts[u : u + 1, t : t + TILE], pts[u : u + 1, sz.qw + t : sz.qw + t + TILE], cx, cy)
                weighted = jnp.concatenate(
                    [(frc[u : u + 1, k * sz.qw + t : k * sz.qw + t + TILE] * w).astype(bf16) for k in range(3)], axis=0
                )
                wz = height_weights(pts[u : u + 1, 2 * sz.qw + t : 2 * sz.qw + t + TILE])
                total_terms = total_terms + dot(weighted, wz, 1, 1)
            terms[u] = total_terms
        for u in range(GROUP):
            lines = [rows_s[j, first + u] for j in range(stencil)]
            spots = [pl.ds(line, 3, stride=layers * ny) for line in lines]
            sums = [grid[spots[j], :] + terms[u, pl.ds(j, 3, stride=stencil), :] for j in range(stencil)]
            for j in range(stencil):
                grid[spots[j], :] = sums[j]
        return carry

    lax.fori_loop(0, slots // GROUP, step, 0)

    half = ny // 2
    mine = where[1] % 2
    for p in range(gx * planes):
        keep[p * half : (p + 1) * half] = grid[pl.ds(pl.multiple_of(p * ny + mine * half, 8), half), :].astype(bf16)
        send[p * half : (p + 1) * half] = grid[pl.ds(pl.multiple_of(p * ny + (1 - mine) * half, 8), half), :].astype(bf16)


def sample_kernel(
    sz, gx, ny, nyb, layers, slabs, where, rows_s, own, other, points, cols, analysis,
    vnew, back,
    drive, state, last, expand, gathered, piece, sampled,
):
    planes = 3 * layers
    half = ny // 2
    pad = 8
    wide = gx + 2 * SWEEPS
    edge = jnp.zeros((pad, TILE), f32)
    mine = where[1] % 2

    def load(p, carry):
        for ref, part in ((own, mine), (other, 1 - mine)):
            rows = ref[pl.ds(pl.multiple_of(p * half, 16), half), :].astype(f32)
            drive[p, pl.ds(pl.multiple_of(pad + part * half, 8), half), :] = rows
        for ref in (drive, state):
            ref[p, 0:pad] = edge
            ref[p, pad + ny :] = edge
        return carry

    lax.fori_loop(0, wide * planes, load, 0)

    last_lane = iota((ny, TILE), 1) == TILE - 1
    first_lane = iota((ny, TILE), 1) == 0
    zero = jnp.zeros((ny, TILE), f32)
    inner = pl.ds(pad, ny)

    def sweep(source, p, store):
        for k in range(3):
            centre = [source[(p * 3 + k) * layers + l, inner] for l in range(layers)]
            ahead = [pltpu.roll(c, TILE - 1, 1) for c in centre]
            behind = [pltpu.roll(c, 1, 1) for c in centre]
            for l in range(layers):
                at = (p * 3 + k) * layers + l
                upper = jnp.where(last_lane, ahead[l + 1] if l + 1 < layers else zero, ahead[l])
                lower = jnp.where(first_lane, behind[l - 1] if l else zero, behind[l])
                around = source[at - planes, inner] + source[at + planes, inner]
                around = around + source[at, pl.ds(pad - 1, ny)] + source[at, pl.ds(pad + 1, ny)]
                around = around + upper + lower
                store(at, (drive[at, inner] + coupling * around) * (1.0 / (1.0 + 6.0 * coupling)))

    def first_sweep(p, carry):
        inside = ((p >= SWEEPS) | (where[0] > 0)) & ((p < gx + SWEEPS) | (where[0] < slabs - 1))
        factor = inside.astype(f32)

        def store(at, value):
            state[at, inner] = value * factor

        sweep(drive, p, store)
        return carry

    lax.fori_loop(1, wide - 1, first_sweep, 0)

    def second_sweep(p, carry):
        def store(at, value):
            last[pl.ds(pl.multiple_of((at - SWEEPS * planes) * ny, 8), ny), :] = value

        sweep(state, p, store)
        return carry

    lax.fori_loop(SWEEPS, gx + SWEEPS, second_sweep, 0)
    last[gx * planes * ny :] = jnp.zeros((last.shape[0] - gx * planes * ny, TILE), f32)

    y_at = pl.multiple_of(where[1] * nyb, 8)
    for x in range(gx):
        for r in range(planes):
            vnew[pl.ds(x * nyb * planes + r, nyb, stride=planes), :] = last[pl.ds((x * planes + r) * ny + y_at, nyb), :]

    stencil = sz.stencil
    slots = points.shape[0]

    def step(g, carry):
        first = pl.multiple_of(g * GROUP, GROUP)
        for u in range(GROUP):
            for j in range(stencil):
                spot = pl.ds(rows_s[j, first + u], 3, stride=layers * ny)
                gathered[u, pl.ds(j, 3, stride=stencil), :] = last[spot, :]
        pts = points[pl.ds(first, GROUP), :]
        col = column_group(sz, cols, g)
        for u in range(GROUP):
            cx, cy = col[:stencil, u : u + 1], col[stencil:, u : u + 1]
            tiles = gathered[u].astype(bf16)
            for t in range(0, sz.qw, TILE):
                w = line_weights(pts[u : u + 1, t : t + TILE], pts[u : u + 1, sz.qw + t : sz.qw + t + TILE], cx, cy)
                wz = height_weights(pts[u : u + 1, 2 * sz.qw + t : 2 * sz.qw + t + TILE])
                projected = dot(tiles, wz)
                for k in range(3):
                    part = jnp.sum(projected[k * stencil : (k + 1) * stencil] * w, axis=0, keepdims=True)
                    piece[u : u + 1, k * sz.qw + t : k * sz.qw + t + TILE] = part
        sampled[pl.ds(first, GROUP), :] = piece[...]
        return carry

    lax.fori_loop(0, slots // GROUP, step, 0)

    expand[...] = jnp.zeros(expand.shape, bf16)
    for k in range(3):
        expand[:, k * sz.qw : k * sz.qw + sz.points] = dot(place_terms(sz, k), analysis[...]).astype(bf16)
    back[...] = dot(sampled[...].astype(bf16), expand[...], 1, 1).astype(bf16)


def unpack_kernel(sz, slot, back, out):
    cells, slots = slot.shape[1], back.shape[0]
    place = one_hot(slot[...] == iota((slots, cells), 0))
    coef = dot(place, back[...], 0, 0).astype(bf16)
    for k in range(3):
        shape = (sz.terms, sz.cw)
        pick = one_hot(iota(shape, 1) == iota(shape, 0) + k * sz.terms)
        out[k] = dot(pick, coef, 1, 1).astype(bf16)


def local(
    velocity_old, traction, offsets, owner_slab, anchor, blocks, block_count, synthesis, analysis
):
    cells, _, terms = traction.shape
    gx, nyb, layers = velocity_old.shape[:3]
    slabs, batches = lax.axis_size("slab"), lax.axis_size("batch")
    ny = nyb * batches
    planes = 3 * layers
    cap = 2 * cells // slabs
    slots = slabs * cap
    stencil = blocks.shape[1]
    sz = Sizes(terms, offsets.shape[2], stencil)
    where = jnp.stack([lax.axis_index("slab"), lax.axis_index("batch")]).astype(jnp.int32)

    def shape(dims, dtype):
        return jax.ShapeDtypeStruct(dims, dtype)

    send, slot = pl.pallas_call(
        lambda *refs: pack_kernel(sz, slabs, cap, ny, layers, *refs),
        out_shape=(shape((slots, sz.width), bf16), shape((1, cells), jnp.int32)),
        in_specs=vmem(6),
        out_specs=vmem(2),
        scratch_shapes=[pltpu.VMEM((cells, sz.width), bf16)],
        compiler_params=params,
        name="pack",
    )(
        owner_slab.T,
        anchor.T,
        blocks.T,
        block_count.reshape(1, cells),
        traction.transpose(1, 2, 0),
        offsets.transpose(1, 0, 2),
    )
    recv = lax.all_to_all(send, "slab", split_axis=0, concat_axis=0, tiled=True)

    half = ny // 2
    dump = 3 * layers * ny
    old_rows = velocity_old.transpose(0, 1, 3, 2, 4).reshape(-1, TILE)
    keep, send_half, points, cols, rows = pl.pallas_call(
        lambda *refs: spread_kernel(sz, gx, ny, nyb, layers, *refs),
        out_shape=(
            shape((gx * planes * half, TILE), bf16),
            shape((gx * planes * half, TILE), bf16),
            shape((slots, 3 * sz.qw), f32),
            shape((slots // TILE, 2 * stencil, TILE), f32),
            shape((stencil, slots), jnp.int32),
        ),
        in_specs=smem(1) + vmem(3),
        out_specs=vmem(5),
        scratch_shapes=[
            pltpu.VMEM((gx * planes * ny + dump, TILE), f32),
            pltpu.VMEM((slots, 3 * sz.qw), f32),
            pltpu.VMEM((sz.cw, 3 * sz.qw), bf16),
            pltpu.VMEM((GROUP, 3 * stencil, TILE), f32),
            pltpu.VMEM((stencil, slots), jnp.int32),
            pltpu.SMEM((stencil, slots), jnp.int32),
            pltpu.SemaphoreType.DMA,
        ],
        compiler_params=params,
        name="spread",
    )(where, recv, synthesis, old_rows)

    def pairs(bit):
        return [(i, i ^ bit) for i in range(batches)]

    def add(a, b):
        return (a.astype(f32) + b.astype(f32)).astype(bf16)

    mine = add(keep, lax.ppermute(send_half, "batch", pairs(1)))
    bit = 2
    while bit < batches:
        mine = add(mine, lax.ppermute(mine, "batch", pairs(bit)))
        bit *= 2
    halo = SWEEPS * planes * half
    up = [(i, i + 1) for i in range(slabs - 1)]
    down = [(i + 1, i) for i in range(slabs - 1)]
    low = lax.ppermute(mine[-halo:], "slab", up)
    high = lax.ppermute(mine[:halo], "slab", down)
    mine = jnp.concatenate([low, mine, high], axis=0)
    other = lax.ppermute(mine, "batch", pairs(1))

    wide = gx + 2 * SWEEPS
    vnew, back = pl.pallas_call(
        lambda *refs: sample_kernel(sz, gx, ny, nyb, layers, slabs, *refs),
        out_shape=(
            shape((gx * nyb * planes, TILE), f32),
            shape((slots, sz.cw), bf16),
        ),
        in_specs=smem(2) + vmem(5),
        out_specs=vmem(2),
        scratch_shapes=[
            pltpu.VMEM((wide * planes, ny + 16, TILE), f32),
            pltpu.VMEM((wide * planes, ny + 16, TILE), f32),
            pltpu.VMEM((gx * planes * ny + dump, TILE), f32),
            pltpu.VMEM((sz.cw, 3 * sz.qw), bf16),
            pltpu.VMEM((GROUP, 3 * stencil, TILE), f32),
            pltpu.VMEM((GROUP, 3 * sz.qw), f32),
            pltpu.VMEM((slots, 3 * sz.qw), f32),
        ],
        compiler_params=params,
        name="sample",
    )(where, rows, mine, other, points, cols, analysis)
    velocity_new = vnew.reshape(gx, nyb, 3, layers, TILE).transpose(0, 1, 3, 2, 4)

    returned = lax.all_to_all(back, "slab", split_axis=0, concat_axis=0, tiled=True)
    coef = pl.pallas_call(
        lambda *refs: unpack_kernel(sz, *refs),
        out_shape=shape((3, terms, cells), bf16),
        in_specs=vmem(2),
        out_specs=vmem(1)[0],
        compiler_params=params,
        name="unpack",
    )(slot, returned)
    return velocity_new, coef.transpose(2, 0, 1)


def solution(mesh):
    in_specs = (
        P("slab", "batch", None, None, None),
        P(("slab", "batch"), None, None),
        P(("slab", "batch"), None, None),
        P(("slab", "batch"), None),
        P(("slab", "batch"), None),
        P(("slab", "batch"), None),
        P(("slab", "batch")),
        P(),
        P(),
    )
    out_specs = (P("slab", "batch", None, None, None), P(("slab", "batch"), None, None))
    return jax.shard_map(local, mesh=mesh, in_specs=in_specs, out_specs=out_specs, check_vma=False)
```

time: 645 us -> 176 us (0.27)
  other arithmetic: 276 us -> 0.32 us
  local copies, waits for them, and re-layouts: 109 us -> 4.75 us
  matrix products: 95.1 us -> 0 us
  Pallas kernels: 0 us -> 91.2 us
  starting transfers between devices: 47.8 us -> 13.2 us
  waiting for transfers between devices: 82.8 us -> 49.2 us
  between operations: 14.4 us -> 0.73 us
  blocking collectives: 9.44 us -> 16 us
    scatter-add x24 -> x0, other arithmetic: 204 us -> none  [spread_step(): grid_sum.at[block_part.reshape(-1)].add(tile_terms.reshape(-1, 3, 128))]
    dot_general x73 -> x0, matrix products: 95.1 us -> none  [the longest x24 40.2 us: spread_step(): jnp.einsum('cbkq,cqi->cbki', weighted, weight_z, preferred_element_type=j...]
    pallas_call x0 -> x4, Pallas kernels: none -> 91.2 us  [the longest x1 47.4 us: local(): pl.pallas_call(lambda *refs: spread_kernel(sz, gx, ny, nyb, layers, *refs...]
    add x96 -> x0, other arithmetic: 44.2 us -> none  [the longest x48 40.7 us: stencil_weights(): anchor_part[:, :, None].astype(jnp.float32)]
    scatter x5 -> x0, local copies, waits for them, and re-layouts: 31.2 us -> none  [placed(): return empty.at[slot_index].set(values)]
    reduce_scatter x1 -> x0, waiting for transfers between devices: 30.9 us -> none  [local(): lax.psum_scatter(partial_value.astype(jnp.bfloat16), 'batch', scatter_dim...]
    gather x25 -> x0, local copies, waits for them, and re-layouts: 24.6 us -> none  [the longest x24 23.6 us: sample_step(): gathered = flat_velocity[block_part]]
    all_to_all x6 -> x1, starting transfers between devices: 30.4 us -> 7.41 us  [local(): recv = lax.all_to_all(send, 'slab', split_axis=0, concat_axis=0, tiled=True)]
  transfers between devices with their start and end apart: 15 -> 6, of which waited for: 11 -> 6; matrix products, arithmetic and copies ran while one was open for 7% -> 0% of each run, Pallas kernels for 0% -> 0%
where the time goes in v1:
time: 176 us; the launch traced here: 175 us
  Pallas kernels  91.2 us (52%)
  waiting for transfers between devices  49.2 us (28%)
  blocking collectives  16 us (9%)
  starting transfers between devices  13.2 us (8%)
  local copies, waits for them, and re-layouts  4.75 us (3%)
    pallas_call x1, Pallas kernels, local(): pl.pallas_call(lambda *refs: spread_kernel(sz, gx, ny, nyb, layers, *refs...  47.4 us
    pallas_call x1, Pallas kernels, local(): pl.pallas_call(lambda *refs: sample_kernel(sz, gx, ny, nyb, layers, slabs...  40.5 us
    all_to_all x1, waiting for transfers between devices, local(): recv = lax.all_to_all(send, 'slab', split_axis=0, concat_axis=0, tiled=True)  30.6 us
    all_to_all x1, blocking collectives, local(): lax.all_to_all(back, 'slab', split_axis=0, concat_axis=0, tiled=True)  16 us
    ppermute x1, waiting for transfers between devices, local(): mine = add(mine, lax.ppermute(mine, 'batch', pairs(bit)))  9.64 us
    all_to_all x1, starting transfers between devices, local(): recv = lax.all_to_all(send, 'slab', split_axis=0, concat_axis=0, tiled=True)  7.41 us
    unnamed x18, local copies, waits for them, and re-layouts  4.73 us
    ppermute x1, waiting for transfers between devices, local(): high = lax.ppermute(mine[:halo], 'slab', down)  4.32 us
  transfers between devices with their start and end apart: 6, of which 6 were waited for; matrix products, arithmetic and copies ran while one was open for 0% of the time, Pallas kernels for 0%

profile of v1, /device:TPU:0, one launch (start us, length us, event | category | flops | bytes accessed | tf_op | source)
XLA Modules:
  0.0 175.4 jit_solution(10201333800014067805)
XLA Ops:
  0.6 1.0 copy-done
  1.6 1.0 copy-done.2
  2.6 0.7 copy-done.5
  3.3 0.7 copy-done.6
  4.0 0.7 copy-done.7
  4.7 0.7 copy-done.8
  5.4 2.0 %pack.1 = (bf16[384,1664]{1,0:T(8,128)(2,1)}, s32[1,192]{1,0:T(1,128)S(1)}) custom-call(s32[1,192]{1,0:T(1,128)S(1)} %bitcast.27, s32[3,192]{1,0:T(4,128)S(1)} %bitcast.26, s32[16,192]{1,0:T(8,128)S(1)} %bitcast.25, s32[1,192]{1,0:T(1,128)S(1)} %bitcast.28, bf16[3,169,192]{2,1,0:T(8,128)(2,1)S(1)} %bitcast.24, bf16[3,192,338]{2,1,0:T(8,128)(2,1)S(1)} %bitcast.21), custom_call_target="tpu_custom_call" | custom-call | tf_op jit(solution)/shard_map/pack/pallas_call | solution.py:332
  7.3 7.4 %all-to-all-start = ((bf16[8,48,1664]{2,1,0:T(8,128)(2,1)}), bf16[8,48,1664]{2,1,0:T(8,128)(2,1)S(1)}, u32[]{:S(2)}, u32[]{:S(2)}) async-start(bf16[8,48,1664]{2,1,0:T(8,128)(2,1)} %bitcast.8), calls=%async_computation | async-start | bytes 2555904 | tf_op jit(solution)/shard_map/all_to_all | solution.py:348
  14.7 0.1 pad_add_fusion.refs_0_
  14.8 30.6 %all-to-all-done = bf16[8,48,1664]{2,1,0:T(8,128)(2,1)S(1)} async-done(((bf16[8,48,1664]{2,1,0:T(8,128)(2,1)}), bf16[8,48,1664]{2,1,0:T(8,128)(2,1)S(1)}, u32[]{:S(2)}, u32[]{:S(2)}) %all-to-all-start) | async-done | bytes 1277984 | tf_op jit(solution)/shard_map/all_to_all | solution.py:348
  45.4 47.4 %spread.1 = (bf16[1536,128]{1,0:T(8,128)(2,1)S(1)}, bf16[1536,128]{1,0:T(8,128)(2,1)S(1)}, f32[384,1152]{1,0:T(8,128)S(1)}, f32[3,32,128]{2,1,0:T(8,128)S(1)}, s32[16,384]{1,0:T(8,128)S(1)}) custom-call(s32[2]{0:T(128)S(1)} %pad_add_fusion.refs_0_, bf16[384,1664]{1,0:T(8,128)(2,1)S(1)} %bitcast.19, bf16[169,338]{1,0:T(8,128)(2,1)S(1)} %copy-done.3, ...), custom_call_target="tpu_custom_call" | custom-call | tf_op jit(solution)/shard_map/spread/pallas_call | solution.py:353
  92.9 1.7 collective-permute-done
  94.6 0.1 add_convert_fusion.1
  94.7 1.6 collective-permute-start.1
  96.3 9.6 %collective-permute-done.1 = bf16[1536,128]{1,0:T(8,128)(2,1)S(1)} collective-permute-done((bf16[1536,128]{1,0:T(8,128)(2,1)S(1)}, bf16[1536,128]{1,0:T(8,128)(2,1)S(1)}, u32[]{:S(2)}, u32[]{:S(2)}) %collective-permute-start.1) | collective-permute-done | bytes 393248 | tf_op jit(solution)/shard_map/ppermute | solution.py:386
  105.9 0.1 add_convert_fusion
  106.1 2.8 %collective-permute-start.2 = (bf16[384,128]{1,0:T(8,128)(2,1)S(1)}, bf16[384,128]{1,0:T(8,128)(2,1)S(1)}, u32[]{:S(2)}, u32[]{:S(2)}) collective-permute-start(bf16[384,128]{1,0:T(8,128)(2,1)S(1)} %get-tuple-element.20), channel_id=1, source_target_pairs={{0,4},{4,8},{8,12},{12,16},{16,20},{20,24},{24,28},{1,5},{5,9},{9,... | collective-permute-start | bytes 294920 | tf_op jit(solution)/shard_map/ppermute | solution.py:391
  108.9 1.3 collective-permute-start.3
  110.2 0.9 collective-permute-done.2
  111.1 4.3 %collective-permute-done.3 = bf16[384,128]{1,0:T(8,128)(2,1)S(1)} collective-permute-done((bf16[384,128]{1,0:T(8,128)(2,1)S(1)}, bf16[384,128]{1,0:T(8,128)(2,1)S(1)}, u32[]{:S(2)}, u32[]{:S(2)}) %collective-permute-start.3) | collective-permute-done | bytes 98336 | tf_op jit(solution)/shard_map/ppermute | solution.py:392
  115.5 2.0 %collective-permute-done.4.refs_3_ = bf16[2304,128]{1,0:T(8,128)(2,1)S(1)} collective-permute-done((bf16[2304,128]{1,0:T(8,128)(2,1)S(1)}, bf16[2304,128]{1,0:T(8,128)(2,1)S(1)}, u32[]{:S(2)}, u32[]{:S(2)}) %collective-permute-start.4) | collective-permute-done | bytes 589856 | tf_op jit(solution)/shard_map/ppermute | solution.py:394
  117.5 40.5 %sample.1 = (f32[768,128]{1,0:T(8,128)}, bf16[384,512]{1,0:T(8,128)(2,1)S(1)}) custom-call(s32[2]{0:T(128)S(1)} %pad_add_fusion.refs_0_, s32[16,384]{1,0:T(8,128)S(1)} %get-tuple-element.12.refs_1_, bf16[2304,128]{1,0:T(8,128)(2,1)S(1)} %pad_maximum_fusion.refs_2_, bf16[2304,128]{1,0:T(8,128)(2,1)S(1)} %collective-permute-done.4.refs_3_, ...), custom_call_target="tpu_custom_call" | custom-call | tf_op jit(solution)/shard_map/sample/pallas_call | solution.py:397
  158.0 16.0 %all_to_all.22 = bf16[8,48,512]{2,1,0:T(8,128)(2,1)S(1)} all-to-all(bf16[8,48,512]{2,1,0:T(8,128)(2,1)S(1)} %bitcast.22), channel_id=1, replica_groups=mesh['slab'=8,'batch'=4] {'slab'}, dimensions={0} | all-to-all | bytes 786432 | tf_op jit(solution)/shard_map/all_to_all | solution.py:419
  174.1 1.3 unpack.1
  (16 shorter events, 0.2 us)
Async XLA Ops:
  0.6 1.0 copy-start
  1.6 1.0 copy-start.2
  2.6 0.7 copy-start.5
  3.3 0.7 copy-start.6
  4.0 0.7 copy-start.7
  4.7 0.7 copy-start.8
  7.3 38.1 %copy-start.1 = (f32[8,16,2,3,128]{4,2,3,1,0:T(2,128)S(1)}, f32[8,16,2,3,128]{4,2,3,1,0:T(2,128)}, u32[]{:S(2)}) copy-start(f32[8,16,2,3,128]{4,2,3,1,0:T(2,128)} %param.9) | copy-start | bytes 1179652
  7.3 38.1 %copy-start.3 = (bf16[169,338]{1,0:T(8,128)(2,1)S(1)}, bf16[169,338]{1,0:T(8,128)(2,1)}, u32[]{:S(2)}) copy-start(bf16[169,338]{1,0:T(8,128)(2,1)} %refs_2_.1) | copy-start | bytes 342736
  7.3 38.1 %all-to-all-start = ((bf16[8,48,1664]{2,1,0:T(8,128)(2,1)}), bf16[8,48,1664]{2,1,0:T(8,128)(2,1)S(1)}, u32[]{:S(2)}, u32[]{:S(2)}) async-start(bf16[8,48,1664]{2,1,0:T(8,128)(2,1)} %bitcast.8), calls=%async_computation | async-start | bytes 2555904 | tf_op jit(solution)/shard_map/all_to_all | solution.py:348
  92.8 1.8 %collective-permute-start = (bf16[1536,128]{1,0:T(8,128)(2,1)S(1)}, bf16[1536,128]{1,0:T(8,128)(2,1)S(1)}, u32[]{:S(2)}, u32[]{:S(2)}) collective-permute-start(bf16[1536,128]{1,0:T(8,128)(2,1)S(1)} %get-tuple-element.14), channel_id=1, source_target_pairs={{0,1},{1,0},{2,3},{3,2},{4,5},{5,4},{6,7},{7,6},{8,9},{9,8},{10,11... | collective-permute-start | bytes 1179656 | tf_op jit(solution)/shard_map/ppermute | solution.py:383
  94.7 22.8 %copy-start.4 = (bf16[169,338]{1,0:T(8,128)(2,1)S(1)}, bf16[169,338]{1,0:T(8,128)(2,1)}, u32[]{:S(2)}) copy-start(bf16[169,338]{1,0:T(8,128)(2,1)} %refs_6_.1) | copy-start | bytes 342736
  94.7 11.2 %collective-permute-start.1 = (bf16[1536,128]{1,0:T(8,128)(2,1)S(1)}, bf16[1536,128]{1,0:T(8,128)(2,1)S(1)}, u32[]{:S(2)}, u32[]{:S(2)}) collective-permute-start(bf16[1536,128]{1,0:T(8,128)(2,1)S(1)} %add_convert_fusion.1), channel_id=1, source_target_pairs={{0,2},{1,3},{2,0},{3,1},{4,6},{5,7},{6,4},{7,5},{8,10},{9,11},{10,... | collective-permute-start | bytes 1179656 | tf_op jit(solution)/shard_map/ppermute | solution.py:386
  106.1 5.0 %collective-permute-start.2 = (bf16[384,128]{1,0:T(8,128)(2,1)S(1)}, bf16[384,128]{1,0:T(8,128)(2,1)S(1)}, u32[]{:S(2)}, u32[]{:S(2)}) collective-permute-start(bf16[384,128]{1,0:T(8,128)(2,1)S(1)} %get-tuple-element.20), channel_id=1, source_target_pairs={{0,4},{4,8},{8,12},{12,16},{16,20},{20,24},{24,28},{1,5},{5,9},{9,... | collective-permute-start | bytes 294920 | tf_op jit(solution)/shard_map/ppermute | solution.py:391
  108.9 6.5 %collective-permute-start.3 = (bf16[384,128]{1,0:T(8,128)(2,1)S(1)}, bf16[384,128]{1,0:T(8,128)(2,1)S(1)}, u32[]{:S(2)}, u32[]{:S(2)}) collective-permute-start(bf16[384,128]{1,0:T(8,128)(2,1)S(1)} %get-tuple-element.21), channel_id=1, source_target_pairs={{4,0},{8,4},{12,8},{16,12},{20,16},{24,20},{28,24},{5,1},{9,5},{13... | collective-permute-start | bytes 294920 | tf_op jit(solution)/shard_map/ppermute | solution.py:392
  115.4 2.1 %collective-permute-start.4 = (bf16[2304,128]{1,0:T(8,128)(2,1)S(1)}, bf16[2304,128]{1,0:T(8,128)(2,1)S(1)}, u32[]{:S(2)}, u32[]{:S(2)}) collective-permute-start(bf16[2304,128]{1,0:T(8,128)(2,1)S(1)} %pad_maximum_fusion.refs_2_), channel_id=1, source_target_pairs={{0,1},{1,0},{2,3},{3,2},{4,5},{5,4},{6,7},{7,6},{8,9},{9,8},{10,11... | collective-permute-start | bytes 1769480 | tf_op jit(solution)/shard_map/ppermute | solution.py:394

commit v2 on v1

v2 whole, which is shorter than its diff:
```python
import math

import jax
import jax.numpy as jnp
from jax import lax
from jax.experimental import pallas as pl
from jax.experimental.pallas import tpu as pltpu
from jax.sharding import PartitionSpec as P

SWEEPS = 2
TILE = 128
GROUP = 8
MXU_LANES = 256
UNROLL = 6
DEAD = 64.0
MIDDLE = 64.0

kernel_width = 0.8
kernel_norm = 1.0 / (0.8 * math.sqrt(2.0 * math.pi))
coupling = 2.0
square = 0.5 / (math.log(2.0) * kernel_width * kernel_width)
norm_bits = math.log2(kernel_norm)

f32 = jnp.float32
bf16 = jnp.bfloat16


def round_up(value, step):
    return -(-value // step) * step


def iota(shape, dim):
    return lax.broadcasted_iota(jnp.int32, shape, dim)


def one_hot(mask):
    return jnp.where(mask, 1.0, 0.0).astype(bf16)


def dot(a, b, ca=1, cb=0):
    return lax.dot_general(a, b, (((ca,), (cb,)), ((), ())), preferred_element_type=f32)


def vmem(count=1):
    return [pl.BlockSpec(memory_space=pltpu.VMEM)] * count


def smem(count=1):
    return [pl.BlockSpec(memory_space=pltpu.SMEM)] * count


params = pltpu.CompilerParams(vmem_limit_bytes=12 * 1024 * 1024)


class Sizes:
    def __init__(self, terms, points, stencil):
        self.terms, self.points, self.stencil = terms, points, stencil
        self.qw = round_up(points, TILE)
        self.cw = round_up(3 * terms, TILE)
        self.width = 3 * self.qw + self.cw
        self.mt = points // TILE * TILE
        self.mo = points - self.mt
        self.meta = 2 * stencil + 3
        self.rows = round_up(self.meta, 8)


def place_terms(sz, k):
    shape = (sz.cw, sz.terms)
    return one_hot(iota(shape, 0) == iota(shape, 1) + k * sz.terms)


def pieces(value, count):
    out = []
    for _ in range(count):
        part = value.astype(bf16).astype(f32)
        out.append(part)
        value = value - part
    return out


def pack_kernel(sz, slabs, cap, chunks, pairwise, ny, layers, *refs):
    where, owner, anchor, blocks, count, trac, offs = refs[:7]
    send, slot_out, rec = refs[7 : 7 + chunks], refs[7 + chunks], refs[8 + chunks]
    cells = owner.shape[1]
    slots = slabs * cap
    own = owner[...]
    member = one_hot(own == iota((slabs, cells), 0))
    before = one_hot(iota((cells, cells), 0) < iota((cells, cells), 1))
    rank = jnp.sum(member.astype(f32) * dot(member, before), axis=0, keepdims=True)
    if pairwise:
        slot = (own ^ where[0]) * cap + rank.astype(jnp.int32)
    else:
        part = cap // chunks
        chunk = jnp.floor((rank + 0.5) * (1.0 / part))
        slot = (chunk * (slabs * part - part) + rank).astype(jnp.int32) + own * part
    slot_out[...] = slot
    place = one_hot(slot == iota((slots, cells), 0))

    tile = blocks[...].astype(f32)
    anchors = anchor[...].astype(f32)
    tile_x = jnp.floor((tile + 0.5) * (1.0 / (ny * layers)))
    tile_y = jnp.floor((tile + 0.5) * (1.0 / layers)) - tile_x * ny
    live = iota(tile.shape, 0) < count[...]
    dx = jnp.where(live, tile_x - anchors[0:1], DEAD)
    dy = jnp.where(live, tile_y - anchors[1:2], DEAD)

    rec[...] = jnp.zeros(rec.shape, bf16)
    for k in range(3):
        rec[:, k * sz.qw : k * sz.qw + sz.points] = offs[k]
    base = sz.mo
    meta = jnp.zeros((cells, TILE), f32)
    for row in (dx, dy, anchors):
        shape = (row.shape[0], TILE)
        where = one_hot(iota(shape, 1) == iota(shape, 0) + base)
        meta = meta + dot(row.astype(bf16), where, 0, 0)
        base += row.shape[0]
    rec[:, sz.mt : sz.mt + TILE] = rec[:, sz.mt : sz.mt + TILE] + meta.astype(bf16)
    coef = jnp.zeros((cells, sz.cw), f32)
    for k in range(3):
        coef = coef + dot(trac[k], place_terms(sz, k), 0, 1)
    rec[:, 3 * sz.qw :] = coef.astype(bf16)
    size = slots // chunks
    for c in range(chunks):
        send[c][...] = dot(place[c * size : (c + 1) * size], rec[...]).astype(bf16)


def load_records(sz, recv, points, lines):
    stencil = sz.stencil
    base = 0
    shape = (TILE, TILE)
    for part in recv:
        slots = part.shape[0]
        points[base : base + slots] = part[:, : 3 * sz.qw].astype(f32)
        meta = part[:, sz.mt : sz.mt + TILE]
        az = dot(meta, one_hot(iota(shape, 0) == sz.mo + 2 * stencil + 2))
        height = az - TILE * jnp.floor((az + 0.5) * (1.0 / TILE)) - MIDDLE
        for t in range(2 * sz.qw, 3 * sz.qw, TILE):
            points[base : base + slots, t : t + TILE] = points[base : base + slots, t : t + TILE] + height
        groups = slots // GROUP
        merge = one_hot(iota((groups, slots), 0) == iota((groups, slots), 1) // GROUP)
        mine = iota((slots, TILE), 0) % GROUP == iota((slots, TILE), 1) // stencil
        for d in range(2):
            spread = one_hot(iota(shape, 0) == iota(shape, 1) % stencil + sz.mo + d * stencil)
            lines[d, base // GROUP : base // GROUP + groups] = dot(
                merge, jnp.where(mine, dot(meta, spread), 0.0).astype(bf16)
            )
        base += slots


def height_table(shape, dim):
    cell, height = iota(shape, dim) // TILE, iota(shape, dim) % TILE
    kind, mine = iota(shape, 1 - dim) // GROUP, iota(shape, 1 - dim) % GROUP == cell
    m = height.astype(f32) - MIDDLE
    minus = pieces(-square * m * m, 3)
    value = jnp.where(kind < 3, m, jnp.where(kind < 6, 1.0, 0.0))
    for i in range(3):
        value = jnp.where(kind == 6 + i, minus[i], value)
    return jnp.where(mine, value, 0.0).astype(bf16)


def stack_rows(rows, like):
    rows = rows + [jnp.zeros_like(like)] * (TILE // GROUP - len(rows))
    return jnp.concatenate(rows, axis=0).astype(bf16)


def line_weights(sz, g, points, lines, w_ref):
    first = pl.multiple_of(g * GROUP, GROUP)
    pts = points[pl.ds(first, GROUP), : 2 * sz.qw]
    ox, oy = pts[:, : sz.qw], pts[:, sz.qw :]
    steps = [lines[d, pl.ds(g, 1), :] for d in range(2)]
    mine = iota((GROUP, TILE), 0) == iota((GROUP, TILE), 1) // sz.stencil
    dx, dy, norm = (jnp.where(mine, value, 0.0) for value in (*steps, steps[0] * steps[0] + steps[1] * steps[1]))
    unit = jnp.where(mine, 1.0, 0.0)
    left = stack_rows([dx, dx, dy, dy, unit, unit, norm, norm], dx)
    rows = pieces(2.0 * square * ox, 2) + pieces(2.0 * square * oy, 2)
    rows = rows + pieces(2.0 * norm_bits - square * (ox * ox + oy * oy), 2)
    rows = rows + pieces(jnp.full_like(ox, -square), 2)
    w_ref[...] = jnp.exp2(dot(left, stack_rows(rows, ox), 0, 0))


def height_factors(oz):
    rows = pieces(2.0 * square * oz, 3) + pieces(norm_bits - square * oz * oz, 3) + [jnp.ones_like(oz)] * 3
    return stack_rows(rows, oz)


def basis_kernel(sz, synthesis, analysis, spread_out, sample_out, spread_table, sample_table):
    for basis, out in ((synthesis, spread_out), (analysis, sample_out)):
        out[...] = jnp.zeros(out.shape, bf16)
        for k in range(3):
            out[:, k * sz.qw : k * sz.qw + sz.points] = dot(place_terms(sz, k), basis[...]).astype(bf16)
    spread_table[...] = height_table(spread_table.shape, 1)
    sample_table[...] = height_table(sample_table.shape, 0)


def in_turn(*works):
    works = list(works)
    while works:
        works = [work for work in works if next(work, works) is not works]


def run_groups(count, prepare, use, slots):
    in_turn(prepare(0, *slots[0]))
    turns = next(t for t in (UNROLL, 4, 2, 1) if count % t == 0)

    def step(h, carry):
        for i in range(turns):
            g = turns * h + i
            if turns % 2:
                in_turn(use(g, *slots[0]))
                in_turn(prepare(g + 1, *slots[0]))
            else:
                in_turn(prepare(g + 1, *slots[(i + 1) % 2]), use(g, *slots[i % 2]))
        return carry

    lax.fori_loop(0, count // turns, step, 0)


def stencil_rows(sz, gx, ny, layers, meta):
    stencil, planes = sz.stencil, 3 * layers
    shape = (TILE, TILE)
    source, lane = iota(shape, 0) - sz.mo, iota(shape, 1)
    dx, dy = (dot(meta, one_hot((source == lane + d * stencil) & (lane < stencil))) for d in range(2))
    ax, ay, az = (dot(meta, one_hot(source == 2 * stencil + d)) for d in range(3))
    layer = jnp.floor((az + 0.5) * (1.0 / TILE))
    line = ((ax + dx) * ny + ay + dy) * planes + layer
    line = jnp.where((dx < 0.5 * DEAD) & (ax > 0.5), line, float(gx * planes * ny))
    return line


def spread_kernel(sz, gx, ny, nyb, layers, parts, begin, end, *refs):
    where, recv, (expand, table, start), refs = refs[0], refs[1 : 1 + parts], refs[1 + parts : 4 + parts], refs[4 + parts :]
    grid, rows_out = refs[0], refs[1 : 1 + parts]
    if end:
        keep, send = refs[1 + parts : 3 + parts]
    points, lines, forces, w0, wz0, w1, wz1, terms, rows_s, sem = refs[(3 if end else 1) + parts :]
    slots = points.shape[0]
    planes = 3 * layers
    stencil = sz.stencil
    count = slots // GROUP

    copies = []
    for i, part in enumerate(recv):
        size = part.shape[0]
        meta = part[:, sz.mt : sz.mt + TILE]
        rows_out[i][...] = stencil_rows(sz, gx, ny, layers, meta).astype(jnp.int32)
        copies.append(pltpu.make_async_copy(rows_out[i], rows_s.at[pl.ds(i * size, size)], sem.at[i]))
        copies[-1].start()
    load_records(sz, recv, points, lines)
    base = 0
    for part in recv:
        size = part.shape[0]
        forces[base : base + size] = dot(part[:, 3 * sz.qw :], expand[...])
        base += size
    if begin:
        grid[...] = jnp.zeros(grid.shape, f32)
        size = nyb * planes
        for x in range(gx):
            grid[pl.ds(pl.multiple_of(x * ny * planes + where[1] * size, 8), size), :] = start[x * size : (x + 1) * size]
    for copy in copies:
        copy.wait()

    def prepare(g, w_ref, wz_ref):
        g = jnp.minimum(g, count - 1)
        line_weights(sz, g, points, lines, w_ref)
        oz = points[pl.ds(pl.multiple_of(g * GROUP, GROUP), GROUP), 2 * sz.qw :]
        left = jnp.transpose(height_factors(oz))
        yield
        for u in range(0, GROUP * TILE, 2 * TILE):
            for t in range(0, sz.qw, TILE):
                exponents = dot(left[t : t + TILE], table[:, u : u + 2 * TILE])
                wz_ref[t : t + TILE, u : u + 2 * TILE] = jnp.exp2(exponents).astype(bf16)
                yield

    def use(g, w_ref, wz_ref):
        first = pl.multiple_of(g * GROUP, GROUP)
        frc = forces[pl.ds(first, GROUP), :]
        for u in range(GROUP):
            w = w_ref[u * stencil : (u + 1) * stencil]
            weighted = [(frc[u : u + 1, k * sz.qw : (k + 1) * sz.qw] * w).astype(bf16) for k in range(3)]
            sums = dot(jnp.concatenate(weighted, axis=0), wz_ref[:, u * TILE : (u + 1) * TILE])
            for k in range(3):
                for j in range(0, stencil, 8):
                    terms[u, pl.ds(4 * j + k, 8, stride=4), :] = sums[k * stencil + j : k * stencil + j + 8]
            yield
            spots = [pl.ds(rows_s[first + u, j], 3, stride=layers) for j in range(stencil)]
            sums = [grid[spots[j], :] + terms[u, 4 * j : 4 * j + 3] for j in range(stencil)]
            for j in range(stencil):
                grid[spots[j], :] = sums[j]

    run_groups(count, prepare, use, ((w0, wz0), (w1, wz1)))

    if end:
        half = ny // 2 * planes
        mine = where[1] % 2
        for x in range(gx):
            for ref, part in ((keep, mine), (send, 1 - mine)):
                rows = grid[pl.ds(pl.multiple_of((2 * x + part) * half, 8), half), :]
                ref[x * half : (x + 1) * half] = rows.astype(bf16)


def relax(gx, ny, layers, slabs, where, own, other, drive, state, last):
    planes = 3 * layers
    rows = ny * planes
    half = rows // 2
    pad = (drive.shape[1] - rows) // 2
    wide = gx + 2 * SWEEPS
    edge = jnp.zeros((pad, TILE), f32)
    mine = where[1] % 2

    def load(p, carry):
        for ref, part in ((own, mine), (other, 1 - mine)):
            values = ref[pl.ds(pl.multiple_of(p * half, 16), half), :].astype(f32)
            drive[p, pl.ds(pl.multiple_of(pad + part * half, 8), half), :] = values
        for ref in (drive, state):
            ref[p, 0:pad] = edge
            ref[p, pad + rows :] = edge
        return carry

    lax.fori_loop(0, wide, load, 0)

    size = 8 * planes
    lane = iota((size, TILE), 1)
    layer = iota((size, TILE), 0) % layers
    last_lane, first_lane = lane == TILE - 1, lane == 0
    above = jnp.where(layer < layers - 1, 1.0, 0.0)
    below = jnp.where(layer > 0, 1.0, 0.0)

    def sweep(source, p, store):
        for at in range(0, rows, size):
            def near(step):
                return source[p, pl.ds(pad + at + step, size), :]

            upper = pltpu.roll(jnp.where(first_lane, near(1) * above, near(0)), TILE - 1, 1)
            lower = pltpu.roll(jnp.where(last_lane, near(-1) * below, near(0)), 1, 1)
            around = source[p - 1, pl.ds(pad + at, size), :] + source[p + 1, pl.ds(pad + at, size), :]
            around = around + near(planes) + near(-planes) + upper + lower
            centre = drive[p, pl.ds(pad + at, size), :]
            store(p, at, (centre + coupling * around) * (1.0 / (1.0 + 6.0 * coupling)))

    def first_sweep(p, carry):
        inside = ((p >= SWEEPS) | (where[0] > 0)) & ((p < gx + SWEEPS) | (where[0] < slabs - 1))
        factor = inside.astype(f32)

        def store(p, at, value):
            state[p, pl.ds(pad + at, size), :] = value * factor

        sweep(drive, p, store)
        return carry

    lax.fori_loop(1, wide - 1, first_sweep, 0)

    def second_sweep(p, carry):
        def store(p, at, value):
            last[pl.ds(pl.multiple_of((p - SWEEPS) * rows + at, 8), size), :] = value

        sweep(state, p, store)
        return carry

    lax.fori_loop(SWEEPS, gx + SWEEPS, second_sweep, 0)
    last[gx * rows :] = jnp.zeros((last.shape[0] - gx * rows, TILE), f32)


def sample_kernel(sz, gx, ny, nyb, layers, slabs, parts, begin, *refs):
    lines_in, recv, (expand, table), refs = refs[:parts], refs[parts : 2 * parts], refs[2 * parts : 2 + 2 * parts], refs[2 + 2 * parts :]
    if begin:
        where, own, other, last, vnew = refs[:5]
        back, (drive, state), refs = refs[5 : 5 + parts], refs[5 + parts : 7 + parts], refs[7 + parts :]
    else:
        last, back, refs = refs[0], refs[1 : 1 + parts], refs[1 + parts :]
    points, lines, w0, wz0, w1, wz1, gathered, products, sampled, rows_s, sem = refs
    copies = []
    for i, part in enumerate(lines_in):
        size = part.shape[0]
        copies.append(pltpu.make_async_copy(part, rows_s.at[pl.ds(i * size, size)], sem.at[i]))
        copies[-1].start()
    stencil = sz.stencil
    slots = points.shape[0]
    count = slots // GROUP
    planes = 3 * layers
    load_records(sz, recv, points, lines)
    if begin:
        relax(gx, ny, layers, slabs, where, own, other, drive, state, last)
        size = nyb * planes
        for x in range(gx):
            at = pl.multiple_of(x * ny * planes + where[1] * size, 8)
            vnew[x * size : (x + 1) * size] = last[pl.ds(at, size), :]
    shape = (3 * GROUP, 3 * GROUP * stencil)
    cell, part = iota(shape, 1) // (3 * stencil), iota(shape, 1) // stencil % 3
    adds = one_hot(iota(shape, 0) == part * GROUP + cell)

    for copy in copies:
        copy.wait()
    cut = sz.qw // MXU_LANES * MXU_LANES
    heights = (iota((TILE, TILE), 0).astype(f32) - MIDDLE) * math.sqrt(square)

    def prepare(g, w_ref, wz_ref):
        g = jnp.minimum(g, count - 1)
        line_weights(sz, g, points, lines, w_ref)
        oz = points[pl.ds(pl.multiple_of(g * GROUP, GROUP), GROUP), 2 * sz.qw :]
        right = height_factors(oz[:, :cut]) if cut else None
        rest = oz[:, cut:] * math.sqrt(square)
        yield
        for u in range(GROUP):
            if cut:
                exponents = dot(table[u * TILE : (u + 1) * TILE], right)
                wz_ref[u * TILE : (u + 1) * TILE, :cut] = jnp.exp2(exponents).astype(bf16)
            for t in range(cut, sz.qw, TILE):
                away = rest[u : u + 1, t - cut : t - cut + TILE] - heights
                value = jnp.exp2(norm_bits - away * away).astype(bf16)
                wz_ref[u * TILE : (u + 1) * TILE, t : t + TILE] = value
            yield

    def use(g, w_ref, wz_ref):
        first = pl.multiple_of(g * GROUP, GROUP)
        for u in range(GROUP):
            for j in range(stencil):
                spot = pl.ds(rows_s[first + u, j], 3, stride=layers)
                gathered[u, 4 * j : 4 * j + 3] = last[spot, :]
        for u in range(GROUP):
            tiles = [
                gathered[u, pl.ds(4 * j + k, 8, stride=4), :] for k in range(3) for j in range(0, stencil, 8)
            ]
            projected = dot(jnp.concatenate(tiles, axis=0).astype(bf16), wz_ref[u * TILE : (u + 1) * TILE])
            w = w_ref[u * stencil : (u + 1) * stencil]
            for k in range(3):
                at = (u * 3 + k) * stencil
                products[at : at + stencil] = (projected[k * stencil : (k + 1) * stencil] * w).astype(bf16)
            yield
        values = dot(adds, products[...])
        for k in range(3):
            sampled[pl.ds(first, GROUP), k * sz.qw : (k + 1) * sz.qw] = values[k * GROUP : (k + 1) * GROUP]

    run_groups(count, prepare, use, ((w0, wz0), (w1, wz1)))
    base = 0
    for ref in back:
        size = ref.shape[0]
        ref[...] = dot(sampled[base : base + size].astype(bf16), expand[...], 1, 1).astype(bf16)
        base += size


def unpack_kernel(sz, *refs):
    slot, out = refs[0], refs[-1]
    parts = refs[1:-1]
    cells, size = slot.shape[1], parts[0].shape[0]
    coef = jnp.zeros((cells, sz.cw), f32)
    for c, back in enumerate(parts):
        place = one_hot(slot[...] == iota((size, cells), 0) + c * size)
        coef = coef + dot(place, back[...], 0, 0)
    coef = coef.astype(bf16)
    for k in range(3):
        shape = (sz.terms, sz.cw)
        pick = one_hot(iota(shape, 1) == iota(shape, 0) + k * sz.terms)
        out[k] = dot(pick, coef, 1, 1).astype(bf16)


def local(
    velocity_old, traction, offsets, owner_slab, anchor, blocks, block_count, synthesis, analysis
):
    cells, _, terms = traction.shape
    gx, nyb, layers = velocity_old.shape[:3]
    slabs, batches = lax.axis_size("slab"), lax.axis_size("batch")
    ny = nyb * batches
    planes = 3 * layers
    cap = 2 * cells // slabs
    stencil = blocks.shape[1]
    sz = Sizes(terms, offsets.shape[2], stencil)
    where = jnp.stack([lax.axis_index("slab"), lax.axis_index("batch")]).astype(jnp.int32)
    half = ny // 2
    grid_rows = gx * ny * planes + 8 * planes

    pairwise = cap % 16 == 0 and slabs & (slabs - 1) == 0
    if pairwise:
        chunks, size = slabs, cap
        stages = [list(range(min(4, slabs)))] + ([list(range(4, slabs))] if slabs > 4 else [])
        back_stages = [list(range(4, slabs)), list(range(1, min(4, slabs))), [0]]
        back_stages = [stage for stage in back_stages if stage]
    else:
        chunks = next(c for c in (3, 2, 1) if cap % c == 0 and slabs * (cap // c) % 16 == 0)
        size = slabs * cap // chunks
        stages = back_stages = [[c] for c in range(chunks)]

    def exchange(value, p):
        if not pairwise:
            return lax.all_to_all(value, "slab", split_axis=0, concat_axis=0, tiled=True)
        return lax.ppermute(value, "slab", [(i, i ^ p) for i in range(slabs)]) if p else value

    def shape(dims, dtype):
        return jax.ShapeDtypeStruct(dims, dtype)

    def whole(dims):
        return pl.BlockSpec(dims, lambda i: (0,) * len(dims))

    packed = [
        owner_slab.T,
        anchor.T,
        blocks.T,
        block_count.reshape(1, cells),
        traction.transpose(1, 2, 0),
        offsets.transpose(1, 0, 2),
    ]
    send = pl.pallas_call(
        lambda *refs: pack_kernel(sz, slabs, cap, chunks, pairwise, ny, layers, *refs),
        grid=(1,),
        out_shape=[shape((size, sz.width), bf16)] * chunks + [shape((1, cells), jnp.int32)],
        in_specs=smem(1) + [whole(value.shape) for value in packed],
        out_specs=[whole((size, sz.width))] * chunks + [whole((1, cells))],
        scratch_shapes=[pltpu.VMEM((cells, sz.width), bf16)],
        compiler_params=pltpu.CompilerParams(vmem_limit_bytes=60 * 1024 * 1024),
        name="pack",
    )(where, *packed)
    slot = send[chunks]
    recv = [exchange(send[p], p) for p in range(chunks)]

    expand_shape = shape((sz.cw, 3 * sz.qw), bf16)
    spread_basis, sample_basis, spread_table, sample_table = pl.pallas_call(
        lambda *refs: basis_kernel(sz, *refs),
        out_shape=[expand_shape, expand_shape, shape((TILE, GROUP * TILE), bf16), shape((GROUP * TILE, TILE), bf16)],
        in_specs=vmem(2),
        out_specs=vmem(4),
        compiler_params=params,
        name="basis",
    )(synthesis, analysis)

    grid_shape = shape((grid_rows, TILE), f32)
    half_shape = shape((gx * planes * half, TILE), bf16)
    weights_xy = pltpu.VMEM((GROUP * stencil, sz.qw), f32)
    terms_shape = pltpu.VMEM((GROUP, 4 * stencil, TILE), f32)
    grid = velocity_old.transpose(0, 1, 3, 2, 4).reshape(-1, TILE)
    rows = {}
    for stage in stages:
        parts = len(stage)
        slots = parts * size
        begin, end = stage is stages[0], stage is stages[-1]
        points = [pltpu.VMEM((slots, 3 * sz.qw), f32), pltpu.VMEM((2, slots // GROUP, TILE), f32)]
        out = pl.pallas_call(
            lambda *refs: spread_kernel(sz, gx, ny, nyb, layers, parts, begin, end, *refs),
            out_shape=[
                grid_shape,
            ]
            + [shape((size, TILE), jnp.int32)] * parts
            + [half_shape] * (2 * end),
            in_specs=smem(1) + vmem(parts + 3),
            out_specs=vmem(1 + parts + 2 * end),
            scratch_shapes=points
            + [pltpu.VMEM((slots, 3 * sz.qw), f32)]
            + [weights_xy, pltpu.VMEM((sz.qw, GROUP * TILE), bf16)] * 2
            + [terms_shape, pltpu.SMEM((slots, TILE), jnp.int32), pltpu.SemaphoreType.DMA((parts,))],
            input_output_aliases={} if begin else {3 + parts: 0},
            compiler_params=params,
            cost_estimate=pl.CostEstimate(flops=100_000_000 * slots, bytes_accessed=4_000_000, transcendentals=0),
            name="spread",
        )(where, *(recv[p] for p in stage), spread_basis, spread_table, grid)
        grid = out[0]
        rows.update(zip(stage, out[1 : 1 + parts]))
    keep, send_half = out[-2:]

    def pairs(bit):
        return [(i, i ^ bit) for i in range(batches)]

    def add(a, b):
        return (a.astype(f32) + b.astype(f32)).astype(bf16)

    mine = add(keep, lax.ppermute(send_half, "batch", pairs(1)))
    bit = 2
    while bit < batches:
        mine = add(mine, lax.ppermute(mine, "batch", pairs(bit)))
        bit *= 2
    halo = SWEEPS * planes * half
    up = [(i, i + 1) for i in range(slabs - 1)]
    down = [(i + 1, i) for i in range(slabs - 1)]
    low = lax.ppermute(mine[-halo:], "slab", up)
    high = lax.ppermute(mine[:halo], "slab", down)
    mine = jnp.concatenate([low, mine, high], axis=0)
    other = lax.ppermute(mine, "batch", pairs(1))

    wide = gx + 2 * SWEEPS
    padded = pltpu.VMEM((wide, planes * ny + 16, TILE), f32)
    returned = [None] * chunks
    for stage in back_stages:
        parts = len(stage)
        slots = parts * size
        begin = stage is back_stages[0]
        out = pl.pallas_call(
            lambda *refs: sample_kernel(sz, gx, ny, nyb, layers, slabs, parts, begin, *refs),
            out_shape=([grid_shape, shape((gx * nyb * planes, TILE), f32)] if begin else [])
            + [shape((size, sz.cw), bf16)] * parts,
            in_specs=vmem(2 * parts + 2) + (smem(1) + vmem(2) if begin else vmem(1)),
            out_specs=vmem(2 * begin + parts),
            scratch_shapes=([padded, padded] if begin else [])
            + [pltpu.VMEM((slots, 3 * sz.qw), f32), pltpu.VMEM((2, slots // GROUP, TILE), f32)]
            + [weights_xy, pltpu.VMEM((GROUP * TILE, sz.qw), bf16)] * 2
            + [terms_shape]
            + [pltpu.VMEM((3 * GROUP * stencil, sz.qw), bf16), pltpu.VMEM((slots, 3 * sz.qw), f32)]
            + [pltpu.SMEM((slots, TILE), jnp.int32), pltpu.SemaphoreType.DMA((parts,))],
            compiler_params=params,
            cost_estimate=pl.CostEstimate(flops=50_000_000 * slots, bytes_accessed=4_000_000, transcendentals=0),
            name="sample",
        )(*(rows[p] for p in stage), *(recv[p] for p in stage), sample_basis, sample_table, *((where, mine, other) if begin else (grid,)))
        if begin:
            grid, vnew = out[:2]
        for p, back in zip(stage, out[2 * begin :]):
            returned[p] = exchange(back, p)
    velocity_new = vnew.reshape(gx, nyb, 3, layers, TILE).transpose(0, 1, 3, 2, 4)

    coef = pl.pallas_call(
        lambda *refs: unpack_kernel(sz, *refs),
        out_shape=shape((3, terms, cells), bf16),
        in_specs=vmem(1 + chunks),
        out_specs=vmem(1)[0],
        compiler_params=params,
        name="unpack",
    )(slot, *returned)
    return velocity_new, coef.transpose(2, 0, 1)


def solution(mesh):
    in_specs = (
        P("slab", "batch", None, None, None),
        P(("slab", "batch"), None, None),
        P(("slab", "batch"), None, None),
        P(("slab", "batch"), None),
        P(("slab", "batch"), None),
        P(("slab", "batch"), None),
        P(("slab", "batch")),
        P(),
        P(),
    )
    out_specs = (P("slab", "batch", None, None, None), P(("slab", "batch"), None, None))
    return jax.shard_map(local, mesh=mesh, in_specs=in_specs, out_specs=out_specs, check_vma=False)
```

time: 176 us -> 130 us (0.74)
  waiting for transfers between devices: 49.2 us -> 19.4 us
  Pallas kernels: 91.2 us -> 71.7 us
  starting transfers between devices: 13.2 us -> 32.3 us
  blocking collectives: 16 us -> 0 us
    all_to_all x1 -> x0, waiting for transfers between devices: 30.6 us -> none  [local(): recv = lax.all_to_all(send, 'slab', split_axis=0, concat_axis=0, tiled=True)]
    ppermute x0 -> x14, starting transfers between devices: none -> 24.6 us  [exchange(): lax.ppermute(value, 'slab', [(i, i ^ p) for i in range(slabs)])]
    all_to_all x1 -> x0, blocking collectives: 16 us -> none  [local(): lax.all_to_all(back, 'slab', split_axis=0, concat_axis=0, tiled=True)]
    pallas_call x2 -> x4, Pallas kernels: 49.3 us -> 35.3 us  [the longest x2 30.6 us: local(): pl.pallas_call(lambda *refs: spread_kernel(sz, gx, ny, nyb, layers, parts...]
    all_to_all x1 -> x0, starting transfers between devices: 7.41 us -> none  [local(): recv = lax.all_to_all(send, 'slab', split_axis=0, concat_axis=0, tiled=True)]
    pallas_call x1 -> x3, Pallas kernels: 40.5 us -> 34.8 us  [local(): pl.pallas_call(lambda *refs: sample_kernel(sz, gx, ny, nyb, layers, slabs...]
    ppermute x1, starting transfers between devices: 2.79 us -> 4.57 us  [local(): low = lax.ppermute(mine[-halo:], 'slab', up)]
    unnamed x18 -> x16, local copies, waits for them, and re-layouts: 4.73 us -> 4.33 us
  transfers between devices with their start and end apart: 6 -> 19, of which waited for: 6 -> 7; matrix products, arithmetic and copies ran while one was open for 0% -> 0% of each run, Pallas kernels for 0% -> 26%
where the time goes in v2:
time: 130 us; the launch traced here: 129 us
  Pallas kernels  71.7 us (55%)
  starting transfers between devices  32.3 us (25%)
  waiting for transfers between devices  19.4 us (15%)
  local copies, waits for them, and re-layouts  4.34 us (3%)
    pallas_call x3, Pallas kernels, local(): pl.pallas_call(lambda *refs: sample_kernel(sz, gx, ny, nyb, layers, slabs...  34.8 us
    pallas_call x2, Pallas kernels, local(): pl.pallas_call(lambda *refs: spread_kernel(sz, gx, ny, nyb, layers, parts...  30.6 us
    ppermute x14, starting transfers between devices, exchange(): lax.ppermute(value, 'slab', [(i, i ^ p) for i in range(slabs)])  24.6 us
    ppermute x1, waiting for transfers between devices, local(): mine = add(mine, lax.ppermute(mine, 'batch', pairs(bit)))  9.47 us
    ppermute x1, starting transfers between devices, local(): low = lax.ppermute(mine[-halo:], 'slab', up)  4.57 us
    ppermute x1, waiting for transfers between devices, local(): high = lax.ppermute(mine[:halo], 'slab', down)  4.5 us
    unnamed x16, local copies, waits for them, and re-layouts  4.33 us
    pallas_call x1, Pallas kernels, local(): pl.pallas_call(lambda *refs: pack_kernel(sz, slabs, cap, chunks, pairwise...  3.37 us
  transfers between devices with their start and end apart: 19, of which 7 were waited for; matrix products, arithmetic and copies ran while one was open for 0% of the time, Pallas kernels for 26%

profile of v2, /device:TPU:0, one launch (start us, length us, event | category | flops | bytes accessed | tf_op | source)
XLA Modules:
  0.0 129.4 jit_solution(13783494318324565559)
XLA Ops:
  1.2 3.4 %pack.1 = (bf16[48,1664]{1,0:T(8,128)(2,1)}, bf16[48,1664]{1,0:T(8,128)(2,1)}, bf16[48,1664]{1,0:T(8,128)(2,1)}, bf16[48,1664]{1,0:T(8,128)(2,1)}, bf16[48,1664]...) custom-call(s32[2]{0:T(128)} %pad_add_fusion.refs_0_.refs_10_, ...), custom_call_target="tpu_custom_call" | custom-call | tf_op jit(solution)/shard_map/pack/pallas_call | solution.py:501
  4.6 3.0 %collective-permute-start.4 = (bf16[48,1664]{1,0:T(8,128)(2,1)}, bf16[48,1664]{1,0:T(8,128)(2,1)S(1)}, u32[]{:S(2)}, u32[]{:S(2)}) collective-permute-start(bf16[48,1664]{1,0:T(8,128)(2,1)} %get-tuple-element.42), channel_id=1, source_target_pairs={{0,4},{4,0},{8,12},{12,8},{16,20},{20,16},{24,28},{28,24},{1,5},{5... | collective-permute-start | bytes 479240 | tf_op jit(solution)/shard_map/ppermute | solution.py:485
  7.5 1.6 %collective-permute-start.5 = (bf16[48,1664]{1,0:T(8,128)(2,1)}, bf16[48,1664]{1,0:T(8,128)(2,1)S(1)}, u32[]{:S(2)}, u32[]{:S(2)}) collective-permute-start(bf16[48,1664]{1,0:T(8,128)(2,1)} %get-tuple-element.43), channel_id=1, source_target_pairs={{0,8},{4,12},{8,0},{12,4},{16,24},{20,28},{24,16},{28,20},{1,9},{5... | collective-permute-start | bytes 479240 | tf_op jit(solution)/shard_map/ppermute | solution.py:485
  9.1 3.0 %collective-permute-start = (bf16[48,1664]{1,0:T(8,128)(2,1)}, bf16[48,1664]{1,0:T(8,128)(2,1)S(1)}, u32[]{:S(2)}, u32[]{:S(2)}) collective-permute-start(bf16[48,1664]{1,0:T(8,128)(2,1)} %get-tuple-element.35), channel_id=1, source_target_pairs={{0,16},{4,20},{8,24},{12,28},{16,0},{20,4},{24,8},{28,12},{1,17},{... | collective-permute-start | bytes 479240 | tf_op jit(solution)/shard_map/ppermute | solution.py:485
  12.1 1.3 collective-permute-start.1
  15.2 1.3 basis.1
  16.5 3.7 %collective-permute-start.2 = (bf16[48,1664]{1,0:T(8,128)(2,1)}, bf16[48,1664]{1,0:T(8,128)(2,1)S(1)}, u32[]{:S(2)}, u32[]{:S(2)}) collective-permute-start(bf16[48,1664]{1,0:T(8,128)(2,1)} %get-tuple-element.37), channel_id=1, source_target_pairs={{0,24},{4,28},{8,16},{12,20},{16,8},{20,12},{24,0},{28,4},{1,25},{... | collective-permute-start | bytes 479240 | tf_op jit(solution)/shard_map/ppermute | solution.py:485
  24.4 16.0 %spread.2 = (f32[3120,128]{1,0:T(8,128)S(1)}, s32[48,128]{1,0:T(8,128)S(1)}, s32[48,128]{1,0:T(8,128)S(1)}, s32[48,128]{1,0:T(8,128)S(1)}, s32[48,128]{1,0:T(8,128)S(1)}) custom-call(s32[2]{0:T(128)S(1)} %copy-done.3, bf16[48,1664]{1,0:T(8,128)(2,1)S(1)} %copy-done.6, bf16[48,1664]{1,0:T(8,128)(2,1)S(1)} %collective-permute-done.4.refs_2_.refs_3_, ...), custom_call_target="tpu_custom_call" | custom-call | flops 19200000000 | bytes 4000000 | tf_op jit(solution)/shard_map/spread/pallas_call | solution.py:535
  40.4 14.7 %spread.3 = (f32[3120,128]{1,0:T(8,128)S(1)}, s32[48,128]{1,0:T(8,128)S(1)}, s32[48,128]{1,0:T(8,128)S(1)}, s32[48,128]{1,0:T(8,128)S(1)}, s32[48,128]{1,0:T(8,1...) custom-call(s32[2]{0:T(128)S(1)} %copy-done.3, ...), custom_call_target="tpu_custom_call", output_to_operand_aliasing={{0}: (7, {})} | custom-call | flops 19200000000 | bytes 4000000 | tf_op jit(solution)/shard_map/spread/pallas_call | solution.py:535
  55.2 1.7 %collective-permute-done.7 = bf16[1536,128]{1,0:T(8,128)(2,1)S(1)} collective-permute-done((bf16[1536,128]{1,0:T(8,128)(2,1)S(1)}, bf16[1536,128]{1,0:T(8,128)(2,1)S(1)}, u32[]{:S(2)}, u32[]{:S(2)}) %collective-permute-start.7) | collective-permute-done | bytes 393248 | tf_op jit(solution)/shard_map/ppermute | solution.py:563
  57.0 1.8 %collective-permute-start.8 = (bf16[1536,128]{1,0:T(8,128)(2,1)S(1)}, bf16[1536,128]{1,0:T(8,128)(2,1)S(1)}, u32[]{:S(2)}, u32[]{:S(2)}) collective-permute-start(bf16[1536,128]{1,0:T(8,128)(2,1)S(1)} %add_convert_fusion.1), channel_id=1, source_target_pairs={{0,2},{1,3},{2,0},{3,1},{4,6},{5,7},{6,4},{7,5},{8,10},{9,11},{10,... | collective-permute-start | bytes 1179656 | tf_op jit(solution)/shard_map/ppermute | solution.py:566
  58.8 9.5 %collective-permute-done.8 = bf16[1536,128]{1,0:T(8,128)(2,1)S(1)} collective-permute-done((bf16[1536,128]{1,0:T(8,128)(2,1)S(1)}, bf16[1536,128]{1,0:T(8,128)(2,1)S(1)}, u32[]{:S(2)}, u32[]{:S(2)}) %collective-permute-start.8) | collective-permute-done | bytes 393248 | tf_op jit(solution)/shard_map/ppermute | solution.py:566
  68.4 4.6 %collective-permute-start.9 = (bf16[384,128]{1,0:T(8,128)(2,1)S(1)}, bf16[384,128]{1,0:T(8,128)(2,1)S(1)}, u32[]{:S(2)}, u32[]{:S(2)}) collective-permute-start(bf16[384,128]{1,0:T(8,128)(2,1)S(1)} %get-tuple-element.68), channel_id=1, source_target_pairs={{0,4},{4,8},{8,12},{12,16},{16,20},{20,24},{24,28},{1,5},{5,9},{9,... | collective-permute-start | bytes 294920 | tf_op jit(solution)/shard_map/ppermute | solution.py:571
  73.0 1.3 collective-permute-start.10
  75.0 4.5 %collective-permute-done.10 = bf16[384,128]{1,0:T(8,128)(2,1)S(1)} collective-permute-done((bf16[384,128]{1,0:T(8,128)(2,1)S(1)}, bf16[384,128]{1,0:T(8,128)(2,1)S(1)}, u32[]{:S(2)}, u32[]{:S(2)}) %collective-permute-start.10) | collective-permute-done | bytes 98336 | tf_op jit(solution)/shard_map/ppermute | solution.py:572
  79.6 2.0 %collective-permute-done.11.refs_12_ = bf16[2304,128]{1,0:T(8,128)(2,1)S(1)} collective-permute-done((bf16[2304,128]{1,0:T(8,128)(2,1)S(1)}, bf16[2304,128]{1,0:T(8,128)(2,1)S(1)}, u32[]{:S(2)}, u32[]{:S(2)}) %collective-permute-start.11) | collective-permute-done | bytes 589856 | tf_op jit(solution)/shard_map/ppermute | solution.py:574
  81.6 18.6 %sample.3 = (f32[3120,128]{1,0:T(8,128)S(1)}, f32[768,128]{1,0:T(8,128)}, bf16[48,512]{1,0:T(8,128)(2,1)S(1)}, bf16[48,512]{1,0:T(8,128)(2,1)S(1)}, bf16[48,512]...) custom-call(s32[48,128]{1,0:T(8,128)S(1)} %get-tuple-element.46.refs_0_, s32[48,128]{1,0:T(8,128)S(1)} %get-tuple-element.47.refs_1_, ...), custom_call_target="tpu_custom_call" | custom-call | flops 9600000000 | bytes 4000000 | tf_op jit(solution)/shard_map/sample/pallas_call | solution.py:583
  101.4 2.2 %collective-permute-start.16 = (bf16[48,512]{1,0:T(8,128)(2,1)S(1)}, bf16[48,512]{1,0:T(8,128)(2,1)S(1)}, u32[]{:S(2)}, u32[]{:S(2)}) collective-permute-start(bf16[48,512]{1,0:T(8,128)(2,1)S(1)} %get-tuple-element.65), channel_id=1, source_target_pairs={{0,20},{4,16},{8,28},{12,24},{16,4},{20,0},{24,12},{28,8},{1,21},{... | collective-permute-start | bytes 147464 | tf_op jit(solution)/shard_map/ppermute | solution.py:485
  103.6 1.9 %collective-permute-start.17 = (bf16[48,512]{1,0:T(8,128)(2,1)S(1)}, bf16[48,512]{1,0:T(8,128)(2,1)S(1)}, u32[]{:S(2)}, u32[]{:S(2)}) collective-permute-start(bf16[48,512]{1,0:T(8,128)(2,1)S(1)} %get-tuple-element.66), channel_id=1, source_target_pairs={{0,24},{4,28},{8,16},{12,20},{16,8},{20,12},{24,0},{28,4},{1,25},{... | collective-permute-start | bytes 147464 | tf_op jit(solution)/shard_map/ppermute | solution.py:485
  105.5 2.5 %collective-permute-start.18 = (bf16[48,512]{1,0:T(8,128)(2,1)S(1)}, bf16[48,512]{1,0:T(8,128)(2,1)S(1)}, u32[]{:S(2)}, u32[]{:S(2)}) collective-permute-start(bf16[48,512]{1,0:T(8,128)(2,1)S(1)} %get-tuple-element.67), channel_id=1, source_target_pairs={{0,28},{4,24},{8,20},{12,16},{16,12},{20,8},{24,4},{28,0},{1,29},{... | collective-permute-start | bytes 147464 | tf_op jit(solution)/shard_map/ppermute | solution.py:485
  108.0 11.7 %sample.5 = (bf16[48,512]{1,0:T(8,128)(2,1)S(1)}, bf16[48,512]{1,0:T(8,128)(2,1)S(1)}, bf16[48,512]{1,0:T(8,128)(2,1)S(1)}) custom-call(s32[48,128]{1,0:T(8,128)S(1)} %get-tuple-element.58.refs_0_, s32[48,128]{1,0:T(8,128)S(1)} %get-tuple-element.59.refs_1_, s32[48,128]{1,0:T(8,128)S(1)} %get-tuple-element.60.refs_2_, ...), custom_call_target="tpu_custom_call" | custom-call | flops 7200000000 | bytes 4000000 | tf_op jit(solution)/shard_map/sample/pallas_call | solution.py:583
  121.2 2.0 %collective-permute-start.14 = (bf16[48,512]{1,0:T(8,128)(2,1)S(1)}, bf16[48,512]{1,0:T(8,128)(2,1)S(1)}, u32[]{:S(2)}, u32[]{:S(2)}) collective-permute-start(bf16[48,512]{1,0:T(8,128)(2,1)S(1)} %get-tuple-element.63), channel_id=1, source_target_pairs={{0,12},{4,8},{8,4},{12,0},{16,28},{20,24},{24,20},{28,16},{1,13},{... | collective-permute-start | bytes 147464 | tf_op jit(solution)/shard_map/ppermute | solution.py:485
  123.2 4.5 %sample.4.refs_1_ = bf16[48,512]{1,0:T(8,128)(2,1)S(1)} custom-call(s32[48,128]{1,0:T(8,128)S(1)} %get-tuple-element.56.refs_0_, bf16[48,1664]{1,0:T(8,128)(2,1)S(1)} %copy-done.7, bf16[512,1152]{1,0:T(8,128)(2,1)S(1)} %get-tuple-element.50.refs_8_.refs_2_.refs_6_, bf16[1024,128]{1,0:T(8,128)(2,1)S(1)} %get-tuple-element.51.refs_9_.refs_3_.refs_7_, ...), custom_call_target="tpu_custom_call" | custom-call | flops 2400000000 | bytes 4000000 | tf_op jit(solution)/shard_map/sample/pallas_call | solution.py:583
  127.8 1.6 %unpack.1 = bf16[3,169,192]{2,1,0:T(8,128)(2,1)} custom-call(s32[1,192]{1,0:T(1,128)S(1)} %copy-done.2, bf16[48,512]{1,0:T(8,128)(2,1)S(1)} %sample.4.refs_1_, bf16[48,512]{1,0:T(8,128)(2,1)S(1)} %collective-permute-done.12.refs_2_, bf16[48,512]{1,0:T(8,128)(2,1)S(1)} %collective-permute-done.13.refs_3_, ...), custom_call_target="tpu_custom_call" | custom-call | tf_op jit(solution)/shard_map/unpack/pallas_call | solution.py:605
  (43 shorter events, 10.6 us)
Async XLA Ops:
  4.6 11.9 %collective-permute-start.4 = (bf16[48,1664]{1,0:T(8,128)(2,1)}, bf16[48,1664]{1,0:T(8,128)(2,1)S(1)}, u32[]{:S(2)}, u32[]{:S(2)}) collective-permute-start(bf16[48,1664]{1,0:T(8,128)(2,1)} %get-tuple-element.42), channel_id=1, source_target_pairs={{0,4},{4,0},{8,12},{12,8},{16,20},{20,16},{24,28},{28,24},{1,5},{5... | collective-permute-start | bytes 479240 | tf_op jit(solution)/shard_map/ppermute | solution.py:485
  7.5 13.3 %collective-permute-start.5 = (bf16[48,1664]{1,0:T(8,128)(2,1)}, bf16[48,1664]{1,0:T(8,128)(2,1)S(1)}, u32[]{:S(2)}, u32[]{:S(2)}) collective-permute-start(bf16[48,1664]{1,0:T(8,128)(2,1)} %get-tuple-element.43), channel_id=1, source_target_pairs={{0,8},{4,12},{8,0},{12,4},{16,24},{20,28},{24,16},{28,20},{1,9},{5... | collective-permute-start | bytes 479240 | tf_op jit(solution)/shard_map/ppermute | solution.py:485
  9.1 12.8 %collective-permute-start.6 = (bf16[48,1664]{1,0:T(8,128)(2,1)}, bf16[48,1664]{1,0:T(8,128)(2,1)S(1)}, u32[]{:S(2)}, u32[]{:S(2)}) collective-permute-start(bf16[48,1664]{1,0:T(8,128)(2,1)} %get-tuple-element.44), channel_id=1, source_target_pairs={{0,12},{4,8},{8,4},{12,0},{16,28},{20,24},{24,20},{28,16},{1,13},{... | collective-permute-start | bytes 479240 | tf_op jit(solution)/shard_map/ppermute | solution.py:485
  9.1 31.3 %collective-permute-start = (bf16[48,1664]{1,0:T(8,128)(2,1)}, bf16[48,1664]{1,0:T(8,128)(2,1)S(1)}, u32[]{:S(2)}, u32[]{:S(2)}) collective-permute-start(bf16[48,1664]{1,0:T(8,128)(2,1)} %get-tuple-element.35), channel_id=1, source_target_pairs={{0,16},{4,20},{8,24},{12,28},{16,0},{20,4},{24,8},{28,12},{1,17},{... | collective-permute-start | bytes 479240 | tf_op jit(solution)/shard_map/ppermute | solution.py:485
  12.1 28.3 %collective-permute-start.1 = (bf16[48,1664]{1,0:T(8,128)(2,1)}, bf16[48,1664]{1,0:T(8,128)(2,1)S(1)}, u32[]{:S(2)}, u32[]{:S(2)}) collective-permute-start(bf16[48,1664]{1,0:T(8,128)(2,1)} %get-tuple-element.36), channel_id=1, source_target_pairs={{0,20},{4,16},{8,28},{12,24},{16,4},{20,0},{24,12},{28,8},{1,21},{... | collective-permute-start | bytes 479240 | tf_op jit(solution)/shard_map/ppermute | solution.py:485
  16.5 23.9 %collective-permute-start.2 = (bf16[48,1664]{1,0:T(8,128)(2,1)}, bf16[48,1664]{1,0:T(8,128)(2,1)S(1)}, u32[]{:S(2)}, u32[]{:S(2)}) collective-permute-start(bf16[48,1664]{1,0:T(8,128)(2,1)} %get-tuple-element.37), channel_id=1, source_target_pairs={{0,24},{4,28},{8,16},{12,20},{16,8},{20,12},{24,0},{28,4},{1,25},{... | collective-permute-start | bytes 479240 | tf_op jit(solution)/shard_map/ppermute | solution.py:485
  20.9 19.6 %collective-permute-start.3 = (bf16[48,1664]{1,0:T(8,128)(2,1)}, bf16[48,1664]{1,0:T(8,128)(2,1)S(1)}, u32[]{:S(2)}, u32[]{:S(2)}) collective-permute-start(bf16[48,1664]{1,0:T(8,128)(2,1)} %get-tuple-element.38), channel_id=1, source_target_pairs={{0,28},{4,24},{8,20},{12,16},{16,12},{20,8},{24,4},{28,0},{1,29},{... | collective-permute-start | bytes 479240 | tf_op jit(solution)/shard_map/ppermute | solution.py:485
  22.5 1.0 copy-start.5
  23.5 0.9 copy-start.6
  55.1 1.8 %collective-permute-start.7 = (bf16[1536,128]{1,0:T(8,128)(2,1)S(1)}, bf16[1536,128]{1,0:T(8,128)(2,1)S(1)}, u32[]{:S(2)}, u32[]{:S(2)}) collective-permute-start(bf16[1536,128]{1,0:T(8,128)(2,1)S(1)} %get-tuple-element.53), channel_id=1, source_target_pairs={{0,1},{1,0},{2,3},{3,2},{4,5},{5,4},{6,7},{7,6},{8,9},{9,8},{10,11... | collective-permute-start | bytes 1179656 | tf_op jit(solution)/shard_map/ppermute | solution.py:563
  57.0 24.6 %copy-start.4 = (s32[2]{0:T(128)S(1)}, s32[2]{0:T(128)}, u32[]{:S(2)}) copy-start(s32[2]{0:T(128)} %pad_add_fusion.refs_0_.refs_10_) | copy-start | bytes 28
  57.0 11.2 %collective-permute-start.8 = (bf16[1536,128]{1,0:T(8,128)(2,1)S(1)}, bf16[1536,128]{1,0:T(8,128)(2,1)S(1)}, u32[]{:S(2)}, u32[]{:S(2)}) collective-permute-start(bf16[1536,128]{1,0:T(8,128)(2,1)S(1)} %add_convert_fusion.1), channel_id=1, source_target_pairs={{0,2},{1,3},{2,0},{3,1},{4,6},{5,7},{6,4},{7,5},{8,10},{9,11},{10,... | collective-permute-start | bytes 1179656 | tf_op jit(solution)/shard_map/ppermute | solution.py:566
  68.4 6.6 %collective-permute-start.9 = (bf16[384,128]{1,0:T(8,128)(2,1)S(1)}, bf16[384,128]{1,0:T(8,128)(2,1)S(1)}, u32[]{:S(2)}, u32[]{:S(2)}) collective-permute-start(bf16[384,128]{1,0:T(8,128)(2,1)S(1)} %get-tuple-element.68), channel_id=1, source_target_pairs={{0,4},{4,8},{8,12},{12,16},{16,20},{20,24},{24,28},{1,5},{5,9},{9,... | collective-permute-start | bytes 294920 | tf_op jit(solution)/shard_map/ppermute | solution.py:571
  73.0 6.5 %collective-permute-start.10 = (bf16[384,128]{1,0:T(8,128)(2,1)S(1)}, bf16[384,128]{1,0:T(8,128)(2,1)S(1)}, u32[]{:S(2)}, u32[]{:S(2)}) collective-permute-start(bf16[384,128]{1,0:T(8,128)(2,1)S(1)} %get-tuple-element.69), channel_id=1, source_target_pairs={{4,0},{8,4},{12,8},{16,12},{20,16},{24,20},{28,24},{5,1},{9,5},{13... | collective-permute-start | bytes 294920 | tf_op jit(solution)/shard_map/ppermute | solution.py:572
  79.5 2.1 %collective-permute-start.11 = (bf16[2304,128]{1,0:T(8,128)(2,1)S(1)}, bf16[2304,128]{1,0:T(8,128)(2,1)S(1)}, u32[]{:S(2)}, u32[]{:S(2)}) collective-permute-start(bf16[2304,128]{1,0:T(8,128)(2,1)S(1)} %pad_maximum_fusion.refs_11_), channel_id=1, source_target_pairs={{0,1},{1,0},{2,3},{3,2},{4,5},{5,4},{6,7},{7,6},{8,9},{9,8},{10,11... | collective-permute-start | bytes 1769480 | tf_op jit(solution)/shard_map/ppermute | solution.py:574
  100.2 20.5 %collective-permute-start.15 = (bf16[48,512]{1,0:T(8,128)(2,1)S(1)}, bf16[48,512]{1,0:T(8,128)(2,1)S(1)}, u32[]{:S(2)}, u32[]{:S(2)}) collective-permute-start(bf16[48,512]{1,0:T(8,128)(2,1)S(1)} %get-tuple-element.64), channel_id=1, source_target_pairs={{0,16},{4,20},{8,24},{12,28},{16,0},{20,4},{24,8},{28,12},{1,17},{... | collective-permute-start | bytes 147464 | tf_op jit(solution)/shard_map/ppermute | solution.py:485
  101.4 19.8 %collective-permute-start.16 = (bf16[48,512]{1,0:T(8,128)(2,1)S(1)}, bf16[48,512]{1,0:T(8,128)(2,1)S(1)}, u32[]{:S(2)}, u32[]{:S(2)}) collective-permute-start(bf16[48,512]{1,0:T(8,128)(2,1)S(1)} %get-tuple-element.65), channel_id=1, source_target_pairs={{0,20},{4,16},{8,28},{12,24},{16,4},{20,0},{24,12},{28,8},{1,21},{... | collective-permute-start | bytes 147464 | tf_op jit(solution)/shard_map/ppermute | solution.py:485
  103.6 24.1 %collective-permute-start.17 = (bf16[48,512]{1,0:T(8,128)(2,1)S(1)}, bf16[48,512]{1,0:T(8,128)(2,1)S(1)}, u32[]{:S(2)}, u32[]{:S(2)}) collective-permute-start(bf16[48,512]{1,0:T(8,128)(2,1)S(1)} %get-tuple-element.66), channel_id=1, source_target_pairs={{0,24},{4,28},{8,16},{12,20},{16,8},{20,12},{24,0},{28,4},{1,25},{... | collective-permute-start | bytes 147464 | tf_op jit(solution)/shard_map/ppermute | solution.py:485
  105.5 22.3 %collective-permute-start.18 = (bf16[48,512]{1,0:T(8,128)(2,1)S(1)}, bf16[48,512]{1,0:T(8,128)(2,1)S(1)}, u32[]{:S(2)}, u32[]{:S(2)}) collective-permute-start(bf16[48,512]{1,0:T(8,128)(2,1)S(1)} %get-tuple-element.67), channel_id=1, source_target_pairs={{0,28},{4,24},{8,20},{12,16},{16,12},{20,8},{24,4},{28,0},{1,29},{... | collective-permute-start | bytes 147464 | tf_op jit(solution)/shard_map/ppermute | solution.py:485
  108.0 15.3 %copy-start.7 = (bf16[48,1664]{1,0:T(8,128)(2,1)S(1)}, bf16[48,1664]{1,0:T(8,128)(2,1)}, u32[]{:S(2)}) copy-start(bf16[48,1664]{1,0:T(8,128)(2,1)} %get-tuple-element.41.refs_1_) | copy-start | bytes 479236
  119.7 8.1 %collective-permute-start.12 = (bf16[48,512]{1,0:T(8,128)(2,1)S(1)}, bf16[48,512]{1,0:T(8,128)(2,1)S(1)}, u32[]{:S(2)}, u32[]{:S(2)}) collective-permute-start(bf16[48,512]{1,0:T(8,128)(2,1)S(1)} %get-tuple-element.61), channel_id=1, source_target_pairs={{0,4},{4,0},{8,12},{12,8},{16,20},{20,16},{24,28},{28,24},{1,5},{5... | collective-permute-start | bytes 147464 | tf_op jit(solution)/shard_map/ppermute | solution.py:485
  120.7 7.0 %collective-permute-start.13 = (bf16[48,512]{1,0:T(8,128)(2,1)S(1)}, bf16[48,512]{1,0:T(8,128)(2,1)S(1)}, u32[]{:S(2)}, u32[]{:S(2)}) collective-permute-start(bf16[48,512]{1,0:T(8,128)(2,1)S(1)} %get-tuple-element.62), channel_id=1, source_target_pairs={{0,8},{4,12},{8,0},{12,4},{16,24},{20,28},{24,16},{28,20},{1,9},{5... | collective-permute-start | bytes 147464 | tf_op jit(solution)/shard_map/ppermute | solution.py:485
  121.2 6.5 %collective-permute-start.14 = (bf16[48,512]{1,0:T(8,128)(2,1)S(1)}, bf16[48,512]{1,0:T(8,128)(2,1)S(1)}, u32[]{:S(2)}, u32[]{:S(2)}) collective-permute-start(bf16[48,512]{1,0:T(8,128)(2,1)S(1)} %get-tuple-element.63), channel_id=1, source_target_pairs={{0,12},{4,8},{8,4},{12,0},{16,28},{20,24},{24,20},{28,16},{1,13},{... | collective-permute-start | bytes 147464 | tf_op jit(solution)/shard_map/ppermute | solution.py:485
  123.2 4.5 %copy-start.2 = (s32[1,192]{1,0:T(1,128)S(1)}, s32[1,192]{1,0:T(1,128)}, u32[]{:S(2)}) copy-start(s32[1,192]{1,0:T(1,128)} %get-tuple-element.55.refs_0_) | copy-start | bytes 2308
  (3 other events, 2.4 us)

commit v3 on v2

--- a/solution.py
+++ b/solution.py
@@ -43,10 +43,6 @@
 
 def vmem(count=1):
     return [pl.BlockSpec(memory_space=pltpu.VMEM)] * count
-
-
-def smem(count=1):
-    return [pl.BlockSpec(memory_space=pltpu.SMEM)] * count
 
 
 params = pltpu.CompilerParams(vmem_limit_bytes=12 * 1024 * 1024)
@@ -79,8 +75,8 @@
 
 
 def pack_kernel(sz, slabs, cap, chunks, pairwise, ny, layers, *refs):
-    where, owner, anchor, blocks, count, trac, offs = refs[:7]
-    send, slot_out, rec = refs[7 : 7 + chunks], refs[7 + chunks], refs[8 + chunks]
+    owner, anchor, blocks, count, trac, offs = refs[:6]
+    send, slot_out, rec = refs[6 : 6 + chunks], refs[6 + chunks], refs[7 + chunks]
     cells = owner.shape[1]
     slots = slabs * cap
     own = owner[...]
@@ -88,7 +84,7 @@
     before = one_hot(iota((cells, cells), 0) < iota((cells, cells), 1))
     rank = jnp.sum(member.astype(f32) * dot(member, before), axis=0, keepdims=True)
     if pairwise:
-        slot = (own ^ where[0]) * cap + rank.astype(jnp.int32)
+        slot = (own ^ lax.axis_index("slab")) * cap + rank.astype(jnp.int32)
     else:
         part = cap // chunks
         chunk = jnp.floor((rank + 0.5) * (1.0 / part))
@@ -228,7 +224,7 @@
 
 
 def spread_kernel(sz, gx, ny, nyb, layers, parts, begin, end, *refs):
-    where, recv, (expand, table, start), refs = refs[0], refs[1 : 1 + parts], refs[1 + parts : 4 + parts], refs[4 + parts :]
+    recv, (expand, table, start), refs = refs[:parts], refs[parts : 3 + parts], refs[3 + parts :]
     grid, rows_out = refs[0], refs[1 : 1 + parts]
     if end:
         keep, send = refs[1 + parts : 3 + parts]
@@ -255,7 +251,7 @@
         grid[...] = jnp.zeros(grid.shape, f32)
         size = nyb * planes
         for x in range(gx):
-            grid[pl.ds(pl.multiple_of(x * ny * planes + where[1] * size, 8), size), :] = start[x * size : (x + 1) * size]
+            grid[pl.ds(pl.multiple_of(x * ny * planes + lax.axis_index("batch") * size, 8), size), :] = start[x * size : (x + 1) * size]
     for copy in copies:
         copy.wait()
 
@@ -291,21 +287,21 @@
 
     if end:
         half = ny // 2 * planes
-        mine = where[1] % 2
+        mine = lax.axis_index("batch") % 2
         for x in range(gx):
             for ref, part in ((keep, mine), (send, 1 - mine)):
                 rows = grid[pl.ds(pl.multiple_of((2 * x + part) * half, 8), half), :]
                 ref[x * half : (x + 1) * half] = rows.astype(bf16)
 
 
-def relax(gx, ny, layers, slabs, where, own, other, drive, state, last):
+def relax(gx, ny, layers, slabs, own, other, drive, state, last):
     planes = 3 * layers
     rows = ny * planes
     half = rows // 2
     pad = (drive.shape[1] - rows) // 2
     wide = gx + 2 * SWEEPS
     edge = jnp.zeros((pad, TILE), f32)
-    mine = where[1] % 2
+    mine = lax.axis_index("batch") % 2
 
     def load(p, carry):
         for ref, part in ((own, mine), (other, 1 - mine)):
@@ -338,7 +334,7 @@
             store(p, at, (centre + coupling * around) * (1.0 / (1.0 + 6.0 * coupling)))
 
     def first_sweep(p, carry):
-        inside = ((p >= SWEEPS) | (where[0] > 0)) & ((p < gx + SWEEPS) | (where[0] < slabs - 1))
+        inside = ((p >= SWEEPS) | (lax.axis_index("slab") > 0)) & ((p < gx + SWEEPS) | (lax.axis_index("slab") < slabs - 1))
         factor = inside.astype(f32)
 
         def store(p, at, value):
@@ -363,8 +359,8 @@
 def sample_kernel(sz, gx, ny, nyb, layers, slabs, parts, begin, *refs):
     lines_in, recv, (expand, table), refs = refs[:parts], refs[parts : 2 * parts], refs[2 * parts : 2 + 2 * parts], refs[2 + 2 * parts :]
     if begin:
-        where, own, other, last, vnew = refs[:5]
-        back, (drive, state), refs = refs[5 : 5 + parts], refs[5 + parts : 7 + parts], refs[7 + parts :]
+        own, other, last, vnew = refs[:4]
+        back, (drive, state), refs = refs[4 : 4 + parts], refs[4 + parts : 6 + parts], refs[6 + parts :]
     else:
         last, back, refs = refs[0], refs[1 : 1 + parts], refs[1 + parts :]
     points, lines, w0, wz0, w1, wz1, gathered, products, sampled, rows_s, sem = refs
@@ -379,10 +375,10 @@
     planes = 3 * layers
     load_records(sz, recv, points, lines)
     if begin:
-        relax(gx, ny, layers, slabs, where, own, other, drive, state, last)
+        relax(gx, ny, layers, slabs, own, other, drive, state, last)
         size = nyb * planes
         for x in range(gx):
-            at = pl.multiple_of(x * ny * planes + where[1] * size, 8)
+            at = pl.multiple_of(x * ny * planes + lax.axis_index("batch") * size, 8)
             vnew[x * size : (x + 1) * size] = last[pl.ds(at, size), :]
     shape = (3 * GROUP, 3 * GROUP * stencil)
     cell, part = iota(shape, 1) // (3 * stencil), iota(shape, 1) // stencil % 3
@@ -464,7 +460,6 @@
     cap = 2 * cells // slabs
     stencil = blocks.shape[1]
     sz = Sizes(terms, offsets.shape[2], stencil)
-    where = jnp.stack([lax.axis_index("slab"), lax.axis_index("batch")]).astype(jnp.int32)
     half = ny // 2
     grid_rows = gx * ny * planes + 8 * planes
 
@@ -502,12 +497,12 @@
         lambda *refs: pack_kernel(sz, slabs, cap, chunks, pairwise, ny, layers, *refs),
         grid=(1,),
         out_shape=[shape((size, sz.width), bf16)] * chunks + [shape((1, cells), jnp.int32)],
-        in_specs=smem(1) + [whole(value.shape) for value in packed],
+        in_specs=[whole(value.shape) for value in packed],
         out_specs=[whole((size, sz.width))] * chunks + [whole((1, cells))],
         scratch_shapes=[pltpu.VMEM((cells, sz.width), bf16)],
         compiler_params=pltpu.CompilerParams(vmem_limit_bytes=60 * 1024 * 1024),
         name="pack",
-    )(where, *packed)
+    )(*packed)
     slot = send[chunks]
     recv = [exchange(send[p], p) for p in range(chunks)]
 
@@ -539,17 +534,17 @@
             ]
             + [shape((size, TILE), jnp.int32)] * parts
             + [half_shape] * (2 * end),
-            in_specs=smem(1) + vmem(parts + 3),
+            in_specs=vmem(parts + 3),
             out_specs=vmem(1 + parts + 2 * end),
             scratch_shapes=points
             + [pltpu.VMEM((slots, 3 * sz.qw), f32)]
             + [weights_xy, pltpu.VMEM((sz.qw, GROUP * TILE), bf16)] * 2
             + [terms_shape, pltpu.SMEM((slots, TILE), jnp.int32), pltpu.SemaphoreType.DMA((parts,))],
-            input_output_aliases={} if begin else {3 + parts: 0},
+            input_output_aliases={} if begin else {2 + parts: 0},
             compiler_params=params,
             cost_estimate=pl.CostEstimate(flops=100_000_000 * slots, bytes_accessed=4_000_000, transcendentals=0),
             name="spread",
-        )(where, *(recv[p] for p in stage), spread_basis, spread_table, grid)
+        )(*(recv[p] for p in stage), spread_basis, spread_table, grid)
         grid = out[0]
         rows.update(zip(stage, out[1 : 1 + parts]))
     keep, send_half = out[-2:]
@@ -561,16 +556,18 @@
         return (a.astype(f32) + b.astype(f32)).astype(bf16)
 
     mine = add(keep, lax.ppermute(send_half, "batch", pairs(1)))
+    halo = SWEEPS * planes * half
+    low = lax.ppermute(mine[-halo:], "slab", [(i, i + 1) for i in range(slabs - 1)])
+    high = lax.ppermute(mine[:halo], "slab", [(i + 1, i) for i in range(slabs - 1)])
+    edges = jnp.concatenate([low, high], axis=0)
     bit = 2
     while bit < batches:
-        mine = add(mine, lax.ppermute(mine, "batch", pairs(bit)))
+        got = lax.ppermute(mine, "batch", pairs(bit))
+        edges, got = lax.optimization_barrier((edges, got))
+        mine = add(mine, got)
+        edges = add(edges, lax.ppermute(edges, "batch", pairs(bit)))
         bit *= 2
-    halo = SWEEPS * planes * half
-    up = [(i, i + 1) for i in range(slabs - 1)]
-    down = [(i + 1, i) for i in range(slabs - 1)]
-    low = lax.ppermute(mine[-halo:], "slab", up)
-    high = lax.ppermute(mine[:halo], "slab", down)
-    mine = jnp.concatenate([low, mine, high], axis=0)
+    mine = jnp.concatenate([edges[:halo], mine, edges[halo:]], axis=0)
     other = lax.ppermute(mine, "batch", pairs(1))
 
     wide = gx + 2 * SWEEPS
@@ -584,7 +581,7 @@
             lambda *refs: sample_kernel(sz, gx, ny, nyb, layers, slabs, parts, begin, *refs),
             out_shape=([grid_shape, shape((gx * nyb * planes, TILE), f32)] if begin else [])
             + [shape((size, sz.cw), bf16)] * parts,
-            in_specs=vmem(2 * parts + 2) + (smem(1) + vmem(2) if begin else vmem(1)),
+            in_specs=vmem(2 * parts + 2) + vmem(2 if begin else 1),
             out_specs=vmem(2 * begin + parts),
             scratch_shapes=([padded, padded] if begin else [])
             + [pltpu.VMEM((slots, 3 * sz.qw), f32), pltpu.VMEM((2, slots // GROUP, TILE), f32)]
@@ -595,7 +592,7 @@
             compiler_params=params,
             cost_estimate=pl.CostEstimate(flops=50_000_000 * slots, bytes_accessed=4_000_000, transcendentals=0),
             name="sample",
-        )(*(rows[p] for p in stage), *(recv[p] for p in stage), sample_basis, sample_table, *((where, mine, other) if begin else (grid,)))
+        )(*(rows[p] for p in stage), *(recv[p] for p in stage), sample_basis, sample_table, *((mine, other) if begin else (grid,)))
         if begin:
             grid, vnew = out[:2]
         for p, back in zip(stage, out[2 * begin :]):

time: 130 us -> 124 us (0.954)
  waiting for transfers between devices: 19.4 us -> 14.9 us
    ppermute x3 -> x4, waiting for transfers between devices: 14.7 us -> 10.2 us  [the longest x1 4.98 us: local(): edges = add(edges, lax.ppermute(edges, 'batch', pairs(bit)))]
    ppermute x3 -> x4, starting transfers between devices: 7.62 us -> 8.26 us  [the longest x1 4.56 us: local(): lax.ppermute(mine[-halo:], 'slab', [(i, i + 1) for i in range(slabs - 1)])]
    unnamed x16 -> x12, local copies, waits for them, and re-layouts: 4.33 us -> 3.73 us
  transfers between devices with their start and end apart: 19 -> 20, of which waited for: 7 -> 7; matrix products, arithmetic and copies ran while one was open for 0% -> 0% of each run, Pallas kernels for 26% -> 27%
where the time goes in v3:
time: 124 us
  Pallas kernels  70.4 us (57%)
  starting transfers between devices  33.3 us (27%)
  waiting for transfers between devices  14.9 us (12%)
  local copies, waits for them, and re-layouts  3.76 us (3%)
    pallas_call x3, Pallas kernels, local(): pl.pallas_call(lambda *refs: sample_kernel(sz, gx, ny, nyb, layers, slabs...  34.4 us
    pallas_call x2, Pallas kernels, local(): pl.pallas_call(lambda *refs: spread_kernel(sz, gx, ny, nyb, layers, parts...  29.8 us
    ppermute x14, starting transfers between devices, exchange(): lax.ppermute(value, 'slab', [(i, i ^ p) for i in range(slabs)])  24.9 us
    ppermute x1, waiting for transfers between devices, local(): edges = add(edges, lax.ppermute(edges, 'batch', pairs(bit)))  4.98 us
    ppermute x1, starting transfers between devices, local(): lax.ppermute(mine[-halo:], 'slab', [(i, i + 1) for i in range(slabs - 1)])  4.56 us
    ppermute x1, waiting for transfers between devices, local(): lax.ppermute(mine[:halo], 'slab', [(i + 1, i) for i in range(slabs - 1)])  4.32 us
    unnamed x12, local copies, waits for them, and re-layouts  3.73 us
    pallas_call x1, Pallas kernels, local(): pl.pallas_call(lambda *refs: pack_kernel(sz, slabs, cap, chunks, pairwise...  3.37 us
  transfers between devices with their start and end apart: 20, of which 7 were waited for; matrix products, arithmetic and copies ran while one was open for 0% of the time, Pallas kernels for 27%

profile of v3, /device:TPU:0, one launch (start us, length us, event | category | flops | bytes accessed | tf_op | source)
XLA Modules:
  0.0 123.5 jit_solution(8891694925971947737)
XLA Ops:
  0.6 3.4 %pack.1 = (bf16[48,1664]{1,0:T(8,128)(2,1)}, bf16[48,1664]{1,0:T(8,128)(2,1)}, bf16[48,1664]{1,0:T(8,128)(2,1)}, bf16[48,1664]{1,0:T(8,128)(2,1)}, bf16[48,1664]...) custom-call(s32[1,192]{1,0:T(1,128)} %bitcast.19, ...), custom_call_target="tpu_custom_call" | custom-call | tf_op jit(solution)/shard_map/pack/pallas_call | solution.py:496
  4.0 3.0 %collective-permute-start.4 = (bf16[48,1664]{1,0:T(8,128)(2,1)}, bf16[48,1664]{1,0:T(8,128)(2,1)S(1)}, u32[]{:S(2)}, u32[]{:S(2)}) collective-permute-start(bf16[48,1664]{1,0:T(8,128)(2,1)} %get-tuple-element.44), channel_id=1, source_target_pairs={{0,4},{4,0},{8,12},{12,8},{16,20},{20,16},{24,28},{28,24},{1,5},{5... | collective-permute-start | bytes 479240 | tf_op jit(solution)/shard_map/ppermute | solution.py:480
  7.0 1.6 %collective-permute-start.5 = (bf16[48,1664]{1,0:T(8,128)(2,1)}, bf16[48,1664]{1,0:T(8,128)(2,1)S(1)}, u32[]{:S(2)}, u32[]{:S(2)}) collective-permute-start(bf16[48,1664]{1,0:T(8,128)(2,1)} %get-tuple-element.45), channel_id=1, source_target_pairs={{0,8},{4,12},{8,0},{12,4},{16,24},{20,28},{24,16},{28,20},{1,9},{5... | collective-permute-start | bytes 479240 | tf_op jit(solution)/shard_map/ppermute | solution.py:480
  8.5 3.0 %collective-permute-start = (bf16[48,1664]{1,0:T(8,128)(2,1)}, bf16[48,1664]{1,0:T(8,128)(2,1)S(1)}, u32[]{:S(2)}, u32[]{:S(2)}) collective-permute-start(bf16[48,1664]{1,0:T(8,128)(2,1)} %get-tuple-element.37), channel_id=1, source_target_pairs={{0,16},{4,20},{8,24},{12,28},{16,0},{20,4},{24,8},{28,12},{1,17},{... | collective-permute-start | bytes 479240 | tf_op jit(solution)/shard_map/ppermute | solution.py:480
  11.5 1.3 %collective-permute-start.1 = (bf16[48,1664]{1,0:T(8,128)(2,1)}, bf16[48,1664]{1,0:T(8,128)(2,1)S(1)}, u32[]{:S(2)}, u32[]{:S(2)}) collective-permute-start(bf16[48,1664]{1,0:T(8,128)(2,1)} %get-tuple-element.38), channel_id=1, source_target_pairs={{0,20},{4,16},{8,28},{12,24},{16,4},{20,0},{24,12},{28,8},{1,21},{... | collective-permute-start | bytes 479240 | tf_op jit(solution)/shard_map/ppermute | solution.py:480
  15.9 3.7 %collective-permute-start.2 = (bf16[48,1664]{1,0:T(8,128)(2,1)}, bf16[48,1664]{1,0:T(8,128)(2,1)S(1)}, u32[]{:S(2)}, u32[]{:S(2)}) collective-permute-start(bf16[48,1664]{1,0:T(8,128)(2,1)} %get-tuple-element.39), channel_id=1, source_target_pairs={{0,24},{4,28},{8,16},{12,20},{16,8},{20,12},{24,0},{28,4},{1,25},{... | collective-permute-start | bytes 479240 | tf_op jit(solution)/shard_map/ppermute | solution.py:480
  23.2 15.5 %spread.2 = (f32[3120,128]{1,0:T(8,128)S(1)}, s32[48,128]{1,0:T(8,128)S(1)}, s32[48,128]{1,0:T(8,128)S(1)}, s32[48,128]{1,0:T(8,128)S(1)}, s32[48,128]{1,0:T(8,128)S(1)}) custom-call(bf16[48,1664]{1,0:T(8,128)(2,1)S(1)} %copy-done.4, bf16[48,1664]{1,0:T(8,128)(2,1)S(1)} %collective-permute-done.4.refs_1_.refs_3_, ...), custom_call_target="tpu_custom_call" | custom-call | flops 19200000000 | bytes 4000000 | tf_op jit(solution)/shard_map/spread/pallas_call | solution.py:530
  38.8 14.2 %spread.3 = (f32[3120,128]{1,0:T(8,128)S(1)}, s32[48,128]{1,0:T(8,128)S(1)}, s32[48,128]{1,0:T(8,128)S(1)}, s32[48,128]{1,0:T(8,128)S(1)}, s32[48,128]{1,0:T(8,1...) custom-call(bf16[48,1664]{1,0:T(8,128)(2,1)S(1)} %collective-permute-done.r, ...), custom_call_target="tpu_custom_call", output_to_operand_aliasing={{0}: (6, {})} | custom-call | flops 19200000000 | bytes 4000000 | tf_op jit(solution)/shard_map/spread/pallas_call | solution.py:530
  53.2 1.7 %collective-permute-done.7 = bf16[1536,128]{1,0:T(8,128)(2,1)S(1)} collective-permute-done((bf16[1536,128]{1,0:T(8,128)(2,1)S(1)}, bf16[1536,128]{1,0:T(8,128)(2,1)S(1)}, u32[]{:S(2)}, u32[]{:S(2)}) %collective-permute-start.7) | collective-permute-done | bytes 393248 | tf_op jit(solution)/shard_map/ppermute | solution.py:558
  55.0 1.8 %collective-permute-start.10 = (bf16[1536,128]{1,0:T(8,128)(2,1)S(1)}, bf16[1536,128]{1,0:T(8,128)(2,1)S(1)}, u32[]{:S(2)}, u32[]{:S(2)}) collective-permute-start(bf16[1536,128]{1,0:T(8,128)(2,1)S(1)} %add_convert_fusion.1), channel_id=1, source_target_pairs={{0,2},{1,3},{2,0},{3,1},{4,6},{5,7},{6,4},{7,5},{8,10},{9,11},{10,... | collective-permute-start | bytes 1179656 | tf_op jit(solution)/shard_map/ppermute | solution.py:565
  56.8 4.6 %collective-permute-start.8 = (bf16[384,128]{1,0:T(8,128)(2,1)S(1)}, bf16[384,128]{1,0:T(8,128)(2,1)S(1)}, u32[]{:S(2)}, u32[]{:S(2)}) collective-permute-start(bf16[384,128]{1,0:T(8,128)(2,1)S(1)} %get-tuple-element.72), channel_id=1, source_target_pairs={{0,4},{4,8},{8,12},{12,16},{16,20},{20,24},{24,28},{1,5},{5,9},{9,... | collective-permute-start | bytes 294920 | tf_op jit(solution)/shard_map/ppermute | solution.py:560
  61.3 1.3 %collective-permute-start.9 = (bf16[384,128]{1,0:T(8,128)(2,1)S(1)}, bf16[384,128]{1,0:T(8,128)(2,1)S(1)}, u32[]{:S(2)}, u32[]{:S(2)}) collective-permute-start(bf16[384,128]{1,0:T(8,128)(2,1)S(1)} %get-tuple-element.73), channel_id=1, source_target_pairs={{4,0},{8,4},{12,8},{16,12},{20,16},{24,20},{28,24},{5,1},{9,5},{13... | collective-permute-start | bytes 294920 | tf_op jit(solution)/shard_map/ppermute | solution.py:561
  63.5 4.3 %collective-permute-done.9 = bf16[384,128]{1,0:T(8,128)(2,1)S(1)} collective-permute-done((bf16[384,128]{1,0:T(8,128)(2,1)S(1)}, bf16[384,128]{1,0:T(8,128)(2,1)S(1)}, u32[]{:S(2)}, u32[]{:S(2)}) %collective-permute-start.9) | collective-permute-done | bytes 98336 | tf_op jit(solution)/shard_map/ppermute | solution.py:561
  68.6 5.0 %collective-permute-done.11 = bf16[768,128]{1,0:T(8,128)(2,1)S(1)} collective-permute-done((bf16[768,128]{1,0:T(8,128)(2,1)S(1)}, bf16[768,128]{1,0:T(8,128)(2,1)S(1)}, u32[]{:S(2)}, u32[]{:S(2)}) %collective-permute-start.11) | collective-permute-done | bytes 196640 | tf_op jit(solution)/shard_map/ppermute | solution.py:568
  73.8 2.0 %collective-permute-done.12.refs_11_ = bf16[2304,128]{1,0:T(8,128)(2,1)S(1)} collective-permute-done((bf16[2304,128]{1,0:T(8,128)(2,1)S(1)}, bf16[2304,128]{1,0:T(8,128)(2,1)S(1)}, u32[]{:S(2)}, u32[]{:S(2)}) %collective-permute-start.12) | collective-permute-done | bytes 589856 | tf_op jit(solution)/shard_map/ppermute | solution.py:571
  75.8 18.1 %sample.3 = (f32[3120,128]{1,0:T(8,128)S(1)}, f32[768,128]{1,0:T(8,128)}, bf16[48,512]{1,0:T(8,128)(2,1)S(1)}, bf16[48,512]{1,0:T(8,128)(2,1)S(1)}, bf16[48,512]...) custom-call(s32[48,128]{1,0:T(8,128)S(1)} %get-tuple-element.48.refs_0_, s32[48,128]{1,0:T(8,128)S(1)} %get-tuple-element.49.refs_1_, ...), custom_call_target="tpu_custom_call" | custom-call | flops 9600000000 | bytes 4000000 | tf_op jit(solution)/shard_map/sample/pallas_call | solution.py:580
  93.9 3.3 %collective-permute-start.16 = (bf16[48,512]{1,0:T(8,128)(2,1)S(1)}, bf16[48,512]{1,0:T(8,128)(2,1)S(1)}, u32[]{:S(2)}, u32[]{:S(2)}) collective-permute-start(bf16[48,512]{1,0:T(8,128)(2,1)S(1)} %get-tuple-element.68), channel_id=1, source_target_pairs={{0,16},{4,20},{8,24},{12,28},{16,0},{20,4},{24,8},{28,12},{1,17},{... | collective-permute-start | bytes 147464 | tf_op jit(solution)/shard_map/ppermute | solution.py:480
  98.2 2.0 %collective-permute-start.18 = (bf16[48,512]{1,0:T(8,128)(2,1)S(1)}, bf16[48,512]{1,0:T(8,128)(2,1)S(1)}, u32[]{:S(2)}, u32[]{:S(2)}) collective-permute-start(bf16[48,512]{1,0:T(8,128)(2,1)S(1)} %get-tuple-element.70), channel_id=1, source_target_pairs={{0,24},{4,28},{8,16},{12,20},{16,8},{20,12},{24,0},{28,4},{1,25},{... | collective-permute-start | bytes 147464 | tf_op jit(solution)/shard_map/ppermute | solution.py:480
  100.2 1.8 %collective-permute-start.19 = (bf16[48,512]{1,0:T(8,128)(2,1)S(1)}, bf16[48,512]{1,0:T(8,128)(2,1)S(1)}, u32[]{:S(2)}, u32[]{:S(2)}) collective-permute-start(bf16[48,512]{1,0:T(8,128)(2,1)S(1)} %get-tuple-element.71), channel_id=1, source_target_pairs={{0,28},{4,24},{8,20},{12,16},{16,12},{20,8},{24,4},{28,0},{1,29},{... | collective-permute-start | bytes 147464 | tf_op jit(solution)/shard_map/ppermute | solution.py:480
  102.0 11.7 %sample.5 = (bf16[48,512]{1,0:T(8,128)(2,1)S(1)}, bf16[48,512]{1,0:T(8,128)(2,1)S(1)}, bf16[48,512]{1,0:T(8,128)(2,1)S(1)}) custom-call(s32[48,128]{1,0:T(8,128)S(1)} %get-tuple-element.62.refs_0_, s32[48,128]{1,0:T(8,128)S(1)} %get-tuple-element.63.refs_1_, s32[48,128]{1,0:T(8,128)S(1)} %get-tuple-element.64.refs_2_, ...), custom_call_target="tpu_custom_call" | custom-call | flops 7200000000 | bytes 4000000 | tf_op jit(solution)/shard_map/sample/pallas_call | solution.py:580
  113.8 1.5 %collective-permute-start.13 = (bf16[48,512]{1,0:T(8,128)(2,1)S(1)}, bf16[48,512]{1,0:T(8,128)(2,1)S(1)}, u32[]{:S(2)}, u32[]{:S(2)}) collective-permute-start(bf16[48,512]{1,0:T(8,128)(2,1)S(1)} %get-tuple-element.65), channel_id=1, source_target_pairs={{0,4},{4,0},{8,12},{12,8},{16,20},{20,16},{24,28},{28,24},{1,5},{5... | collective-permute-start | bytes 147464 | tf_op jit(solution)/shard_map/ppermute | solution.py:480
  116.0 1.3 %collective-permute-start.15 = (bf16[48,512]{1,0:T(8,128)(2,1)S(1)}, bf16[48,512]{1,0:T(8,128)(2,1)S(1)}, u32[]{:S(2)}, u32[]{:S(2)}) collective-permute-start(bf16[48,512]{1,0:T(8,128)(2,1)S(1)} %get-tuple-element.67), channel_id=1, source_target_pairs={{0,12},{4,8},{8,4},{12,0},{16,28},{20,24},{24,20},{28,16},{1,13},{... | collective-permute-start | bytes 147464 | tf_op jit(solution)/shard_map/ppermute | solution.py:480
  117.3 4.5 %sample.4.refs_1_ = bf16[48,512]{1,0:T(8,128)(2,1)S(1)} custom-call(s32[48,128]{1,0:T(8,128)S(1)} %get-tuple-element.60.refs_0_, bf16[48,1664]{1,0:T(8,128)(2,1)S(1)} %copy-done.5, bf16[512,1152]{1,0:T(8,128)(2,1)S(1)} %get-tuple-element.52.refs_8_.refs_2_.refs_6_, bf16[1024,128]{1,0:T(8,128)(2,1)S(1)} %get-tuple-element.53.refs_9_.refs_3_.refs_7_, ...), custom_call_target="tpu_custom_call" | custom-call | flops 2400000000 | bytes 4000000 | tf_op jit(solution)/shard_map/sample/pallas_call | solution.py:580
  121.9 1.6 %unpack.1 = bf16[3,169,192]{2,1,0:T(8,128)(2,1)} custom-call(s32[1,192]{1,0:T(1,128)S(1)} %copy-done.2, bf16[48,512]{1,0:T(8,128)(2,1)S(1)} %sample.4.refs_1_, bf16[48,512]{1,0:T(8,128)(2,1)S(1)} %collective-permute-done.13.refs_2_, bf16[48,512]{1,0:T(8,128)(2,1)S(1)} %collective-permute-done.14.refs_3_, ...), custom_call_target="tpu_custom_call" | custom-call | tf_op jit(solution)/shard_map/unpack/pallas_call | solution.py:602
  (43 shorter events, 10.5 us)
Async XLA Ops:
  4.0 11.9 %collective-permute-start.4 = (bf16[48,1664]{1,0:T(8,128)(2,1)}, bf16[48,1664]{1,0:T(8,128)(2,1)S(1)}, u32[]{:S(2)}, u32[]{:S(2)}) collective-permute-start(bf16[48,1664]{1,0:T(8,128)(2,1)} %get-tuple-element.44), channel_id=1, source_target_pairs={{0,4},{4,0},{8,12},{12,8},{16,20},{20,16},{24,28},{28,24},{1,5},{5... | collective-permute-start | bytes 479240 | tf_op jit(solution)/shard_map/ppermute | solution.py:480
  7.0 13.3 %collective-permute-start.5 = (bf16[48,1664]{1,0:T(8,128)(2,1)}, bf16[48,1664]{1,0:T(8,128)(2,1)S(1)}, u32[]{:S(2)}, u32[]{:S(2)}) collective-permute-start(bf16[48,1664]{1,0:T(8,128)(2,1)} %get-tuple-element.45), channel_id=1, source_target_pairs={{0,8},{4,12},{8,0},{12,4},{16,24},{20,28},{24,16},{28,20},{1,9},{5... | collective-permute-start | bytes 479240 | tf_op jit(solution)/shard_map/ppermute | solution.py:480
  8.5 12.8 %collective-permute-start.6 = (bf16[48,1664]{1,0:T(8,128)(2,1)}, bf16[48,1664]{1,0:T(8,128)(2,1)S(1)}, u32[]{:S(2)}, u32[]{:S(2)}) collective-permute-start(bf16[48,1664]{1,0:T(8,128)(2,1)} %get-tuple-element.46), channel_id=1, source_target_pairs={{0,12},{4,8},{8,4},{12,0},{16,28},{20,24},{24,20},{28,16},{1,13},{... | collective-permute-start | bytes 479240 | tf_op jit(solution)/shard_map/ppermute | solution.py:480
  8.5 30.2 %collective-permute-start = (bf16[48,1664]{1,0:T(8,128)(2,1)}, bf16[48,1664]{1,0:T(8,128)(2,1)S(1)}, u32[]{:S(2)}, u32[]{:S(2)}) collective-permute-start(bf16[48,1664]{1,0:T(8,128)(2,1)} %get-tuple-element.37), channel_id=1, source_target_pairs={{0,16},{4,20},{8,24},{12,28},{16,0},{20,4},{24,8},{28,12},{1,17},{... | collective-permute-start | bytes 479240 | tf_op jit(solution)/shard_map/ppermute | solution.py:480
  11.5 27.3 %collective-permute-start.1 = (bf16[48,1664]{1,0:T(8,128)(2,1)}, bf16[48,1664]{1,0:T(8,128)(2,1)S(1)}, u32[]{:S(2)}, u32[]{:S(2)}) collective-permute-start(bf16[48,1664]{1,0:T(8,128)(2,1)} %get-tuple-element.38), channel_id=1, source_target_pairs={{0,20},{4,16},{8,28},{12,24},{16,4},{20,0},{24,12},{28,8},{1,21},{... | collective-permute-start | bytes 479240 | tf_op jit(solution)/shard_map/ppermute | solution.py:480
  15.9 22.9 %collective-permute-start.2 = (bf16[48,1664]{1,0:T(8,128)(2,1)}, bf16[48,1664]{1,0:T(8,128)(2,1)S(1)}, u32[]{:S(2)}, u32[]{:S(2)}) collective-permute-start(bf16[48,1664]{1,0:T(8,128)(2,1)} %get-tuple-element.39), channel_id=1, source_target_pairs={{0,24},{4,28},{8,16},{12,20},{16,8},{20,12},{24,0},{28,4},{1,25},{... | collective-permute-start | bytes 479240 | tf_op jit(solution)/shard_map/ppermute | solution.py:480
  20.3 18.5 %collective-permute-start.3 = (bf16[48,1664]{1,0:T(8,128)(2,1)}, bf16[48,1664]{1,0:T(8,128)(2,1)S(1)}, u32[]{:S(2)}, u32[]{:S(2)}) collective-permute-start(bf16[48,1664]{1,0:T(8,128)(2,1)} %get-tuple-element.40), channel_id=1, source_target_pairs={{0,28},{4,24},{8,20},{12,16},{16,12},{20,8},{24,4},{28,0},{1,29},{... | collective-permute-start | bytes 479240 | tf_op jit(solution)/shard_map/ppermute | solution.py:480
  21.3 1.0 copy-start.3
  22.3 0.9 copy-start.4
  53.1 1.8 %collective-permute-start.7 = (bf16[1536,128]{1,0:T(8,128)(2,1)S(1)}, bf16[1536,128]{1,0:T(8,128)(2,1)S(1)}, u32[]{:S(2)}, u32[]{:S(2)}) collective-permute-start(bf16[1536,128]{1,0:T(8,128)(2,1)S(1)} %get-tuple-element.55), channel_id=1, source_target_pairs={{0,1},{1,0},{2,3},{3,2},{4,5},{5,4},{6,7},{7,6},{8,9},{9,8},{10,11... | collective-permute-start | bytes 1179656 | tf_op jit(solution)/shard_map/ppermute | solution.py:558
  55.0 12.9 %collective-permute-start.10 = (bf16[1536,128]{1,0:T(8,128)(2,1)S(1)}, bf16[1536,128]{1,0:T(8,128)(2,1)S(1)}, u32[]{:S(2)}, u32[]{:S(2)}) collective-permute-start(bf16[1536,128]{1,0:T(8,128)(2,1)S(1)} %add_convert_fusion.1), channel_id=1, source_target_pairs={{0,2},{1,3},{2,0},{3,1},{4,6},{5,7},{6,4},{7,5},{8,10},{9,11},{10,... | collective-permute-start | bytes 1179656 | tf_op jit(solution)/shard_map/ppermute | solution.py:565
  56.8 6.8 %collective-permute-start.8 = (bf16[384,128]{1,0:T(8,128)(2,1)S(1)}, bf16[384,128]{1,0:T(8,128)(2,1)S(1)}, u32[]{:S(2)}, u32[]{:S(2)}) collective-permute-start(bf16[384,128]{1,0:T(8,128)(2,1)S(1)} %get-tuple-element.72), channel_id=1, source_target_pairs={{0,4},{4,8},{8,12},{12,16},{16,20},{20,24},{24,28},{1,5},{5,9},{9,... | collective-permute-start | bytes 294920 | tf_op jit(solution)/shard_map/ppermute | solution.py:560
  61.3 6.5 %collective-permute-start.9 = (bf16[384,128]{1,0:T(8,128)(2,1)S(1)}, bf16[384,128]{1,0:T(8,128)(2,1)S(1)}, u32[]{:S(2)}, u32[]{:S(2)}) collective-permute-start(bf16[384,128]{1,0:T(8,128)(2,1)S(1)} %get-tuple-element.73), channel_id=1, source_target_pairs={{4,0},{8,4},{12,8},{16,12},{20,16},{24,20},{28,24},{5,1},{9,5},{13... | collective-permute-start | bytes 294920 | tf_op jit(solution)/shard_map/ppermute | solution.py:561
  67.9 5.7 %collective-permute-start.11 = (bf16[768,128]{1,0:T(8,128)(2,1)S(1)}, bf16[768,128]{1,0:T(8,128)(2,1)S(1)}, u32[]{:S(2)}, u32[]{:S(2)}) collective-permute-start(bf16[768,128]{1,0:T(8,128)(2,1)S(1)} %pad_maximum_fusion.1), channel_id=1, source_target_pairs={{0,2},{1,3},{2,0},{3,1},{4,6},{5,7},{6,4},{7,5},{8,10},{9,11},{10,... | collective-permute-start | bytes 589832 | tf_op jit(solution)/shard_map/ppermute | solution.py:568
  73.7 2.1 %collective-permute-start.12 = (bf16[2304,128]{1,0:T(8,128)(2,1)S(1)}, bf16[2304,128]{1,0:T(8,128)(2,1)S(1)}, u32[]{:S(2)}, u32[]{:S(2)}) collective-permute-start(bf16[2304,128]{1,0:T(8,128)(2,1)S(1)} %pad_maximum_fusion.refs_10_), channel_id=1, source_target_pairs={{0,1},{1,0},{2,3},{3,2},{4,5},{5,4},{6,7},{7,6},{8,9},{9,8},{10,11... | collective-permute-start | bytes 1769480 | tf_op jit(solution)/shard_map/ppermute | solution.py:571
  93.9 21.3 %collective-permute-start.16 = (bf16[48,512]{1,0:T(8,128)(2,1)S(1)}, bf16[48,512]{1,0:T(8,128)(2,1)S(1)}, u32[]{:S(2)}, u32[]{:S(2)}) collective-permute-start(bf16[48,512]{1,0:T(8,128)(2,1)S(1)} %get-tuple-element.68), channel_id=1, source_target_pairs={{0,16},{4,20},{8,24},{12,28},{16,0},{20,4},{24,8},{28,12},{1,17},{... | collective-permute-start | bytes 147464 | tf_op jit(solution)/shard_map/ppermute | solution.py:480
  97.2 18.8 %collective-permute-start.17 = (bf16[48,512]{1,0:T(8,128)(2,1)S(1)}, bf16[48,512]{1,0:T(8,128)(2,1)S(1)}, u32[]{:S(2)}, u32[]{:S(2)}) collective-permute-start(bf16[48,512]{1,0:T(8,128)(2,1)S(1)} %get-tuple-element.69), channel_id=1, source_target_pairs={{0,20},{4,16},{8,28},{12,24},{16,4},{20,0},{24,12},{28,8},{1,21},{... | collective-permute-start | bytes 147464 | tf_op jit(solution)/shard_map/ppermute | solution.py:480
  98.2 23.6 %collective-permute-start.18 = (bf16[48,512]{1,0:T(8,128)(2,1)S(1)}, bf16[48,512]{1,0:T(8,128)(2,1)S(1)}, u32[]{:S(2)}, u32[]{:S(2)}) collective-permute-start(bf16[48,512]{1,0:T(8,128)(2,1)S(1)} %get-tuple-element.70), channel_id=1, source_target_pairs={{0,24},{4,28},{8,16},{12,20},{16,8},{20,12},{24,0},{28,4},{1,25},{... | collective-permute-start | bytes 147464 | tf_op jit(solution)/shard_map/ppermute | solution.py:480
  100.2 21.6 %collective-permute-start.19 = (bf16[48,512]{1,0:T(8,128)(2,1)S(1)}, bf16[48,512]{1,0:T(8,128)(2,1)S(1)}, u32[]{:S(2)}, u32[]{:S(2)}) collective-permute-start(bf16[48,512]{1,0:T(8,128)(2,1)S(1)} %get-tuple-element.71), channel_id=1, source_target_pairs={{0,28},{4,24},{8,20},{12,16},{16,12},{20,8},{24,4},{28,0},{1,29},{... | collective-permute-start | bytes 147464 | tf_op jit(solution)/shard_map/ppermute | solution.py:480
  102.0 15.3 %copy-start.5 = (bf16[48,1664]{1,0:T(8,128)(2,1)S(1)}, bf16[48,1664]{1,0:T(8,128)(2,1)}, u32[]{:S(2)}) copy-start(bf16[48,1664]{1,0:T(8,128)(2,1)} %get-tuple-element.43.refs_0_.refs_1_) | copy-start | bytes 479236
  113.8 8.1 %collective-permute-start.13 = (bf16[48,512]{1,0:T(8,128)(2,1)S(1)}, bf16[48,512]{1,0:T(8,128)(2,1)S(1)}, u32[]{:S(2)}, u32[]{:S(2)}) collective-permute-start(bf16[48,512]{1,0:T(8,128)(2,1)S(1)} %get-tuple-element.65), channel_id=1, source_target_pairs={{0,4},{4,0},{8,12},{12,8},{16,20},{20,16},{24,28},{28,24},{1,5},{5... | collective-permute-start | bytes 147464 | tf_op jit(solution)/shard_map/ppermute | solution.py:480
  115.3 6.6 %collective-permute-start.14 = (bf16[48,512]{1,0:T(8,128)(2,1)S(1)}, bf16[48,512]{1,0:T(8,128)(2,1)S(1)}, u32[]{:S(2)}, u32[]{:S(2)}) collective-permute-start(bf16[48,512]{1,0:T(8,128)(2,1)S(1)} %get-tuple-element.66), channel_id=1, source_target_pairs={{0,8},{4,12},{8,0},{12,4},{16,24},{20,28},{24,16},{28,20},{1,9},{5... | collective-permute-start | bytes 147464 | tf_op jit(solution)/shard_map/ppermute | solution.py:480
  116.0 5.9 %collective-permute-start.15 = (bf16[48,512]{1,0:T(8,128)(2,1)S(1)}, bf16[48,512]{1,0:T(8,128)(2,1)S(1)}, u32[]{:S(2)}, u32[]{:S(2)}) collective-permute-start(bf16[48,512]{1,0:T(8,128)(2,1)S(1)} %get-tuple-element.67), channel_id=1, source_target_pairs={{0,12},{4,8},{8,4},{12,0},{16,28},{20,24},{24,20},{28,16},{1,13},{... | collective-permute-start | bytes 147464 | tf_op jit(solution)/shard_map/ppermute | solution.py:480
  117.3 4.5 %copy-start.2 = (s32[1,192]{1,0:T(1,128)S(1)}, s32[1,192]{1,0:T(1,128)}, u32[]{:S(2)}) copy-start(s32[1,192]{1,0:T(1,128)} %get-tuple-element.59.refs_0_) | copy-start | bytes 2308
  (2 other events, 1.8 us)

commit v4 on v3

--- a/solution.py
+++ b/solution.py
@@ -11,7 +11,7 @@
 TILE = 128
 GROUP = 8
 MXU_LANES = 256
-UNROLL = 6
+UNROLL = 12
 DEAD = 64.0
 MIDDLE = 64.0
 
@@ -179,13 +179,11 @@
     return stack_rows(rows, oz)
 
 
-def basis_kernel(sz, synthesis, analysis, spread_out, sample_out, spread_table, sample_table):
-    for basis, out in ((synthesis, spread_out), (analysis, sample_out)):
-        out[...] = jnp.zeros(out.shape, bf16)
-        for k in range(3):
-            out[:, k * sz.qw : k * sz.qw + sz.points] = dot(place_terms(sz, k), basis[...]).astype(bf16)
-    spread_table[...] = height_table(spread_table.shape, 1)
-    sample_table[...] = height_table(sample_table.shape, 0)
+def basis_kernel(sz, dim, basis, out, table):
+    out[...] = jnp.zeros(out.shape, bf16)
+    for k in range(3):
+        out[:, k * sz.qw : k * sz.qw + sz.points] = dot(place_terms(sz, k), basis[...]).astype(bf16)
+    table[...] = height_table(table.shape, dim)
 
 
 def in_turn(*works):
@@ -196,7 +194,7 @@
 
 def run_groups(count, prepare, use, slots):
     in_turn(prepare(0, *slots[0]))
-    turns = next(t for t in (UNROLL, 4, 2, 1) if count % t == 0)
+    turns = next(t for t in (UNROLL, 6, 4, 2, 1) if count % t == 0)
 
     def step(h, carry):
         for i in range(turns):
@@ -356,25 +354,62 @@
     last[gx * rows :] = jnp.zeros((last.shape[0] - gx * rows, TILE), f32)
 
 
-def sample_kernel(sz, gx, ny, nyb, layers, slabs, parts, begin, *refs):
-    lines_in, recv, (expand, table), refs = refs[:parts], refs[parts : 2 * parts], refs[2 * parts : 2 + 2 * parts], refs[2 + 2 * parts :]
+def sample_weights(sz, g, points, lines, table, w_ref, wz_ref):
+    cut = sz.qw // MXU_LANES * MXU_LANES
+    heights = (iota((TILE, TILE), 0).astype(f32) - MIDDLE) * math.sqrt(square)
+    line_weights(sz, g, points, lines, w_ref)
+    oz = points[pl.ds(pl.multiple_of(g * GROUP, GROUP), GROUP), 2 * sz.qw :]
+    right = height_factors(oz[:, :cut]) if cut else None
+    rest = oz[:, cut:] * math.sqrt(square)
+    yield
+    for u in range(GROUP):
+        if cut:
+            exponents = dot(table[u * TILE : (u + 1) * TILE], right)
+            wz_ref[u * TILE : (u + 1) * TILE, :cut] = jnp.exp2(exponents).astype(bf16)
+        for t in range(cut, sz.qw, TILE):
+            away = rest[u : u + 1, t - cut : t - cut + TILE] - heights
+            value = jnp.exp2(norm_bits - away * away).astype(bf16)
+            wz_ref[u * TILE : (u + 1) * TILE, t : t + TILE] = value
+        yield
+
+
+def weights_kernel(sz, parts, *refs):
+    recv, (table, w_out, wz_out, points, lines) = refs[:parts], refs[parts:]
+    load_records(sz, recv, points, lines)
+    count = w_out.shape[0]
+    turns = next(t for t in (4, 2, 1) if count % t == 0)
+
+    def step(h, carry):
+        groups = [turns * h + i for i in range(turns)]
+        for g in groups:
+            in_turn(sample_weights(sz, g, points, lines, table, w_out.at[g], wz_out.at[g]))
+        return carry
+
+    lax.fori_loop(0, count // turns, step, 0)
+
+
+def sample_kernel(sz, gx, ny, nyb, layers, slabs, parts, begin, halves, *refs):
+    lines_in, refs = refs[:parts], refs[parts:]
     if begin:
-        own, other, last, vnew = refs[:4]
-        back, (drive, state), refs = refs[4 : 4 + parts], refs[4 + parts : 6 + parts], refs[6 + parts :]
+        ready, refs = refs[: 2 * halves], refs[2 * halves :]
+        expand, own, other, last, vnew = refs[:5]
+        back, (drive, state, *refs) = refs[5 : 5 + parts], refs[5 + parts :]
     else:
-        last, back, refs = refs[0], refs[1 : 1 + parts], refs[1 + parts :]
-    points, lines, w0, wz0, w1, wz1, gathered, products, sampled, rows_s, sem = refs
+        recv, (expand, table, last), refs = refs[:parts], refs[parts : 3 + parts], refs[3 + parts :]
+        back, (points, lines, w0, wz0, w1, wz1, *refs) = refs[:parts], refs[parts:]
+    gathered, products, sampled, rows_s, sem = refs
     copies = []
     for i, part in enumerate(lines_in):
         size = part.shape[0]
         copies.append(pltpu.make_async_copy(part, rows_s.at[pl.ds(i * size, size)], sem.at[i]))
         copies[-1].start()
     stencil = sz.stencil
-    slots = points.shape[0]
+    slots = sampled.shape[0]
     count = slots // GROUP
     planes = 3 * layers
-    load_records(sz, recv, points, lines)
-    if begin:
+    if not begin:
+        load_records(sz, recv, points, lines)
+    else:
         relax(gx, ny, layers, slabs, own, other, drive, state, last)
         size = nyb * planes
         for x in range(gx):
@@ -386,25 +421,8 @@
 
     for copy in copies:
         copy.wait()
-    cut = sz.qw // MXU_LANES * MXU_LANES
-    heights = (iota((TILE, TILE), 0).astype(f32) - MIDDLE) * math.sqrt(square)
-
     def prepare(g, w_ref, wz_ref):
-        g = jnp.minimum(g, count - 1)
-        line_weights(sz, g, points, lines, w_ref)
-        oz = points[pl.ds(pl.multiple_of(g * GROUP, GROUP), GROUP), 2 * sz.qw :]
-        right = height_factors(oz[:, :cut]) if cut else None
-        rest = oz[:, cut:] * math.sqrt(square)
-        yield
-        for u in range(GROUP):
-            if cut:
-                exponents = dot(table[u * TILE : (u + 1) * TILE], right)
-                wz_ref[u * TILE : (u + 1) * TILE, :cut] = jnp.exp2(exponents).astype(bf16)
-            for t in range(cut, sz.qw, TILE):
-                away = rest[u : u + 1, t - cut : t - cut + TILE] - heights
-                value = jnp.exp2(norm_bits - away * away).astype(bf16)
-                wz_ref[u * TILE : (u + 1) * TILE, t : t + TILE] = value
-            yield
+        yield from sample_weights(sz, jnp.minimum(g, count - 1), points, lines, table, w_ref, wz_ref)
 
     def use(g, w_ref, wz_ref):
         first = pl.multiple_of(g * GROUP, GROUP)
@@ -426,7 +444,24 @@
         for k in range(3):
             sampled[pl.ds(first, GROUP), k * sz.qw : (k + 1) * sz.qw] = values[k * GROUP : (k + 1) * GROUP]
 
-    run_groups(count, prepare, use, ((w0, wz0), (w1, wz1)))
+    def use_ready(base, w_in, wz_in):
+        turns = next(t for t in (UNROLL, 6, 4, 2, 1) if w_in.shape[0] % t == 0)
+
+        def step(h, carry):
+            for i in range(turns):
+                g = turns * h + i
+                in_turn(use(base + g, w_in.at[g], wz_in.at[g]))
+            return carry
+
+        lax.fori_loop(0, w_in.shape[0] // turns, step, 0)
+
+    if begin:
+        base = 0
+        for w_in, wz_in in zip(ready[::2], ready[1::2]):
+            use_ready(base, w_in, wz_in)
+            base += w_in.shape[0]
+    else:
+        run_groups(count, prepare, use, ((w0, wz0), (w1, wz1)))
     base = 0
     for ref in back:
         size = ref.shape[0]
@@ -507,14 +542,18 @@
     recv = [exchange(send[p], p) for p in range(chunks)]
 
     expand_shape = shape((sz.cw, 3 * sz.qw), bf16)
-    spread_basis, sample_basis, spread_table, sample_table = pl.pallas_call(
-        lambda *refs: basis_kernel(sz, *refs),
-        out_shape=[expand_shape, expand_shape, shape((TILE, GROUP * TILE), bf16), shape((GROUP * TILE, TILE), bf16)],
-        in_specs=vmem(2),
-        out_specs=vmem(4),
-        compiler_params=params,
-        name="basis",
-    )(synthesis, analysis)
+    def basis(values, dim):
+        table = (TILE, GROUP * TILE) if dim else (GROUP * TILE, TILE)
+        return pl.pallas_call(
+            lambda *refs: basis_kernel(sz, dim, *refs),
+            out_shape=[expand_shape, shape(table, bf16)],
+            in_specs=vmem(1),
+            out_specs=vmem(2),
+            compiler_params=params,
+            name="basis",
+        )(values)
+
+    spread_basis, spread_table = basis(synthesis, 1)
 
     grid_shape = shape((grid_rows, TILE), f32)
     half_shape = shape((gx * planes * half, TILE), bf16)
@@ -556,6 +595,28 @@
         return (a.astype(f32) + b.astype(f32)).astype(bf16)
 
     mine = add(keep, lax.ppermute(send_half, "batch", pairs(1)))
+    def weights(values):
+        slots = len(values) * size
+        groups = slots // GROUP
+        return pl.pallas_call(
+            lambda *refs: weights_kernel(sz, len(values), *refs),
+            out_shape=[
+                shape((groups, GROUP * stencil, sz.qw), f32),
+                shape((groups, GROUP * TILE, sz.qw), bf16),
+            ],
+            in_specs=vmem(len(values) + 1),
+            out_specs=vmem(2),
+            scratch_shapes=[pltpu.VMEM((slots, 3 * sz.qw), f32), pltpu.VMEM((2, groups, TILE), f32)],
+            compiler_params=params,
+            cost_estimate=pl.CostEstimate(flops=50_000_000 * slots, bytes_accessed=4_000_000, transcendentals=0),
+            name="weights",
+        )(*values, sample_table)
+
+    first = back_stages[0]
+    late = [recv[p] for p in first]
+    mine, analysis, late = lax.optimization_barrier((mine, analysis, late))
+    sample_basis, sample_table = basis(analysis, 0)
+    ready = [weights(late[: (len(late) + 1) // 2])]
     halo = SWEEPS * planes * half
     low = lax.ppermute(mine[-halo:], "slab", [(i, i + 1) for i in range(slabs - 1)])
     high = lax.ppermute(mine[:halo], "slab", [(i + 1, i) for i in range(slabs - 1)])
@@ -563,11 +624,14 @@
     bit = 2
     while bit < batches:
         got = lax.ppermute(mine, "batch", pairs(bit))
-        edges, got = lax.optimization_barrier((edges, got))
+        edges, got, ready, late = lax.optimization_barrier((edges, got, ready, late))
         mine = add(mine, got)
         edges = add(edges, lax.ppermute(edges, "batch", pairs(bit)))
         bit *= 2
     mine = jnp.concatenate([edges[:halo], mine, edges[halo:]], axis=0)
+    if len(late) > 1:
+        ready.append(weights(late[(len(late) + 1) // 2 :]))
+        mine, ready = lax.optimization_barrier((mine, ready))
     other = lax.ppermute(mine, "batch", pairs(1))
 
     wide = gx + 2 * SWEEPS
@@ -578,21 +642,27 @@
         slots = parts * size
         begin = stage is back_stages[0]
         out = pl.pallas_call(
-            lambda *refs: sample_kernel(sz, gx, ny, nyb, layers, slabs, parts, begin, *refs),
+            lambda *refs: sample_kernel(sz, gx, ny, nyb, layers, slabs, parts, begin, len(ready), *refs),
             out_shape=([grid_shape, shape((gx * nyb * planes, TILE), f32)] if begin else [])
             + [shape((size, sz.cw), bf16)] * parts,
-            in_specs=vmem(2 * parts + 2) + vmem(2 if begin else 1),
+            in_specs=vmem(parts + 2 * len(ready) + 3 if begin else 2 * parts + 3),
             out_specs=vmem(2 * begin + parts),
-            scratch_shapes=([padded, padded] if begin else [])
-            + [pltpu.VMEM((slots, 3 * sz.qw), f32), pltpu.VMEM((2, slots // GROUP, TILE), f32)]
-            + [weights_xy, pltpu.VMEM((GROUP * TILE, sz.qw), bf16)] * 2
+            scratch_shapes=(
+                [padded, padded]
+                if begin
+                else [pltpu.VMEM((slots, 3 * sz.qw), f32), pltpu.VMEM((2, slots // GROUP, TILE), f32)]
+                + [weights_xy, pltpu.VMEM((GROUP * TILE, sz.qw), bf16)] * 2
+            )
             + [terms_shape]
             + [pltpu.VMEM((3 * GROUP * stencil, sz.qw), bf16), pltpu.VMEM((slots, 3 * sz.qw), f32)]
             + [pltpu.SMEM((slots, TILE), jnp.int32), pltpu.SemaphoreType.DMA((parts,))],
             compiler_params=params,
             cost_estimate=pl.CostEstimate(flops=50_000_000 * slots, bytes_accessed=4_000_000, transcendentals=0),
             name="sample",
-        )(*(rows[p] for p in stage), *(recv[p] for p in stage), sample_basis, sample_table, *((mine, other) if begin else (grid,)))
+        )(
+            *(rows[p] for p in stage),
+            *((*sum(map(list, ready), []), sample_basis, mine, other) if begin else (*(recv[p] for p in stage), sample_basis, sample_table, grid)),
+        )
         if begin:
             grid, vnew = out[:2]
         for p, back in zip(stage, out[2 * begin :]):

time: 124 us -> 121 us (0.976)
  waiting for transfers between devices: 14.9 us -> 7.78 us
  Pallas kernels: 70.4 us -> 73.4 us
  starting transfers between devices: 33.3 us -> 35 us
    pallas_call x1 -> x4, Pallas kernels: 1.26 us -> 9.27 us  [the longest x2 7.9 us: weights(): pl.pallas_call(lambda *refs: weights_kernel(sz, len(values), *refs), out_...]
    pallas_call x3, Pallas kernels: 34.4 us -> 29.7 us  [local(): pl.pallas_call(lambda *refs: sample_kernel(sz, gx, ny, nyb, layers, slabs...]
    ppermute x1, waiting for transfers between devices: 4.32 us -> 0.43 us  [local(): lax.ppermute(mine[:halo], 'slab', [(i + 1, i) for i in range(slabs - 1)])]
    ppermute x1, waiting for transfers between devices: 4.98 us -> 1.38 us  [local(): edges = add(edges, lax.ppermute(edges, 'batch', pairs(bit)))]
    ppermute x14, starting transfers between devices: 24.9 us -> 27.2 us  [exchange(): lax.ppermute(value, 'slab', [(i, i ^ p) for i in range(slabs)])]
    ppermute x14, waiting for transfers between devices: 0.96 us -> 2.26 us  [exchange(): lax.ppermute(value, 'slab', [(i, i ^ p) for i in range(slabs)])]
  transfers between devices with their start and end apart: 20 -> 20, of which waited for: 7 -> 6; matrix products, arithmetic and copies ran while one was open for 0% -> 0% of each run, Pallas kernels for 27% -> 34%
where the time goes in v4:
time: 121 us; the launch traced here: 120 us
  Pallas kernels  73.4 us (61%)
  starting transfers between devices  35 us (29%)
  waiting for transfers between devices  7.78 us (6%)
  local copies, waits for them, and re-layouts  2.86 us (2%)
    pallas_call x3, Pallas kernels, local(): pl.pallas_call(lambda *refs: sample_kernel(sz, gx, ny, nyb, layers, slabs...  29.7 us
    pallas_call x2, Pallas kernels, local(): pl.pallas_call(lambda *refs: spread_kernel(sz, gx, ny, nyb, layers, parts...  29.5 us
    ppermute x14, starting transfers between devices, exchange(): lax.ppermute(value, 'slab', [(i, i ^ p) for i in range(slabs)])  27.2 us
    pallas_call x2, Pallas kernels, weights(): pl.pallas_call(lambda *refs: weights_kernel(sz, len(values), *refs), out_...  7.9 us
    ppermute x1, starting transfers between devices, local(): lax.ppermute(mine[-halo:], 'slab', [(i, i + 1) for i in range(slabs - 1)])  3.97 us
    pallas_call x1, Pallas kernels, local(): pl.pallas_call(lambda *refs: pack_kernel(sz, slabs, cap, chunks, pairwise...  3.37 us
    unnamed x12, local copies, waits for them, and re-layouts  2.83 us
  transfers between devices with their start and end apart: 20, of which 6 were waited for; matrix products, arithmetic and copies ran while one was open for 0% of the time, Pallas kernels for 34%

profile of v4, /device:TPU:0, one launch (start us, length us, event | category | flops | bytes accessed | tf_op | source)
XLA Modules:
  0.0 120.3 jit_solution(9956575660480810313)
XLA Ops:
  0.6 3.4 %pack.1 = (bf16[48,1664]{1,0:T(8,128)(2,1)}, bf16[48,1664]{1,0:T(8,128)(2,1)}, bf16[48,1664]{1,0:T(8,128)(2,1)}, bf16[48,1664]{1,0:T(8,128)(2,1)}, bf16[48,1664]...) custom-call(s32[1,192]{1,0:T(1,128)} %bitcast.19, ...), custom_call_target="tpu_custom_call" | custom-call | tf_op jit(solution)/shard_map/pack/pallas_call | solution.py:531
  4.0 3.0 %collective-permute-start.4 = (bf16[48,1664]{1,0:T(8,128)(2,1)}, bf16[48,1664]{1,0:T(8,128)(2,1)S(1)}, u32[]{:S(2)}, u32[]{:S(2)}) collective-permute-start(bf16[48,1664]{1,0:T(8,128)(2,1)} %get-tuple-element.63), channel_id=1, source_target_pairs={{0,4},{4,0},{8,12},{12,8},{16,20},{20,16},{24,28},{28,24},{1,5},{5... | collective-permute-start | bytes 479240 | tf_op jit(solution)/shard_map/ppermute | solution.py:515
  7.0 1.6 %collective-permute-start.5 = (bf16[48,1664]{1,0:T(8,128)(2,1)}, bf16[48,1664]{1,0:T(8,128)(2,1)S(1)}, u32[]{:S(2)}, u32[]{:S(2)}) collective-permute-start(bf16[48,1664]{1,0:T(8,128)(2,1)} %get-tuple-element.64), channel_id=1, source_target_pairs={{0,8},{4,12},{8,0},{12,4},{16,24},{20,28},{24,16},{28,20},{1,9},{5... | collective-permute-start | bytes 479240 | tf_op jit(solution)/shard_map/ppermute | solution.py:515
  8.6 3.0 %collective-permute-start = (bf16[48,1664]{1,0:T(8,128)(2,1)}, bf16[48,1664]{1,0:T(8,128)(2,1)S(1)}, u32[]{:S(2)}, u32[]{:S(2)}) collective-permute-start(bf16[48,1664]{1,0:T(8,128)(2,1)} %get-tuple-element.56), channel_id=1, source_target_pairs={{0,16},{4,20},{8,24},{12,28},{16,0},{20,4},{24,8},{28,12},{1,17},{... | collective-permute-start | bytes 479240 | tf_op jit(solution)/shard_map/ppermute | solution.py:515
  14.3 3.7 %collective-permute-start.2 = (bf16[48,1664]{1,0:T(8,128)(2,1)}, bf16[48,1664]{1,0:T(8,128)(2,1)S(1)}, u32[]{:S(2)}, u32[]{:S(2)}) collective-permute-start(bf16[48,1664]{1,0:T(8,128)(2,1)} %get-tuple-element.58), channel_id=1, source_target_pairs={{0,24},{4,28},{8,16},{12,20},{16,8},{20,12},{24,0},{28,4},{1,25},{... | collective-permute-start | bytes 479240 | tf_op jit(solution)/shard_map/ppermute | solution.py:515
  18.0 2.0 %collective-permute-done.5.refs_2_.refs_4_ = bf16[48,1664]{1,0:T(8,128)(2,1)S(1)} collective-permute-done((bf16[48,1664]{1,0:T(8,128)(2,1)}, bf16[48,1664]{1,0:T(8,128)(2,1)S(1)}, u32[]{:S(2)}, u32[]{:S(2)}) %collective-permute-start.5) | collective-permute-done | bytes 159776 | tf_op jit(solution)/shard_map/ppermute | solution.py:515
  23.2 15.3 %spread.2 = (f32[3120,128]{1,0:T(8,128)S(1)}, s32[48,128]{1,0:T(8,128)S(1)}, s32[48,128]{1,0:T(8,128)S(1)}, s32[48,128]{1,0:T(8,128)S(1)}, s32[48,128]{1,0:T(8,128)S(1)}) custom-call(bf16[48,1664]{1,0:T(8,128)(2,1)S(1)} %copy-done.4, bf16[48,1664]{1,0:T(8,128)(2,1)S(1)} %collective-permute-done.4.refs_1_.refs_3_, ...), custom_call_target="tpu_custom_call" | custom-call | flops 19200000000 | bytes 4000000 | tf_op jit(solution)/shard_map/spread/pallas_call | solution.py:569
  38.6 14.1 %spread.3 = (f32[3120,128]{1,0:T(8,128)S(1)}, s32[48,128]{1,0:T(8,128)S(1)}, s32[48,128]{1,0:T(8,128)S(1)}, s32[48,128]{1,0:T(8,128)S(1)}, s32[48,128]{1,0:T(8,1...) custom-call(bf16[48,1664]{1,0:T(8,128)(2,1)S(1)} %collective-permute-done.r, ...), custom_call_target="tpu_custom_call", output_to_operand_aliasing={{0}: (6, {})} | custom-call | flops 19200000000 | bytes 4000000 | tf_op jit(solution)/shard_map/spread/pallas_call | solution.py:569
  52.9 1.7 %collective-permute-done.7 = bf16[1536,128]{1,0:T(8,128)(2,1)S(1)} collective-permute-done((bf16[1536,128]{1,0:T(8,128)(2,1)S(1)}, bf16[1536,128]{1,0:T(8,128)(2,1)S(1)}, u32[]{:S(2)}, u32[]{:S(2)}) %collective-permute-start.7) | collective-permute-done | bytes 393248 | tf_op jit(solution)/shard_map/ppermute | solution.py:597
  54.7 1.7 %collective-permute-start.10 = (bf16[1536,128]{1,0:T(8,128)(2,1)S(1)}, bf16[1536,128]{1,0:T(8,128)(2,1)S(1)}, u32[]{:S(2)}, u32[]{:S(2)}) collective-permute-start(bf16[1536,128]{1,0:T(8,128)(2,1)S(1)} %add_convert_fusion.1), channel_id=1, source_target_pairs={{0,2},{1,3},{2,0},{3,1},{4,6},{5,7},{6,4},{7,5},{8,10},{9,11},{10,... | collective-permute-start | bytes 1179656 | tf_op jit(solution)/shard_map/ppermute | solution.py:626
  56.4 4.0 %collective-permute-start.8 = (bf16[384,128]{1,0:T(8,128)(2,1)S(1)}, bf16[384,128]{1,0:T(8,128)(2,1)S(1)}, u32[]{:S(2)}, u32[]{:S(2)}) collective-permute-start(bf16[384,128]{1,0:T(8,128)(2,1)S(1)} %get-tuple-element.110), channel_id=1, source_target_pairs={{0,4},{4,8},{8,12},{12,16},{16,20},{20,24},{24,28},{1,5},{5,9},{9,... | collective-permute-start | bytes 294920 | tf_op jit(solution)/shard_map/ppermute | solution.py:621
  60.4 1.3 %collective-permute-start.9 = (bf16[384,128]{1,0:T(8,128)(2,1)S(1)}, bf16[384,128]{1,0:T(8,128)(2,1)S(1)}, u32[]{:S(2)}, u32[]{:S(2)}) collective-permute-start(bf16[384,128]{1,0:T(8,128)(2,1)S(1)} %get-tuple-element.111), channel_id=1, source_target_pairs={{4,0},{8,4},{12,8},{16,12},{20,16},{24,20},{28,24},{5,1},{9,5},{13... | collective-permute-start | bytes 294920 | tf_op jit(solution)/shard_map/ppermute | solution.py:622
  62.5 3.9 %weights.2 = (f32[12,128,384]{2,1,0:T(8,128)S(1)}, bf16[12,1024,384]{2,1,0:T(8,128)(2,1)S(1)}) custom-call(bf16[48,1664]{1,0:T(8,128)(2,1)S(1)} %collective-permute-done.refs_0_, bf16[48,1664]{1,0:T(8,128)(2,1)S(1)} %collective-permute-done.1.refs_1_, bf16[1024,128]{1,0:T(8,128)(2,1)S(1)} %get-tuple-element.77.refs_2_.refs_3_.refs_7_), custom_call_target="tpu_custom_call" | custom-call | flops 4800000000 | bytes 4000000 | tf_op jit(solution)/shard_map/weights/pallas_call | solution.py:601
  67.7 4.0 %weights.3 = (f32[12,128,384]{2,1,0:T(8,128)S(1)}, bf16[12,1024,384]{2,1,0:T(8,128)(2,1)S(1)}) custom-call(bf16[48,1664]{1,0:T(8,128)(2,1)S(1)} %collective-permute-done.2.refs_2_.refs_0_, bf16[48,1664]{1,0:T(8,128)(2,1)S(1)} %collective-permute-done.3.refs_3_.refs_1_, bf16[1024,128]{1,0:T(8,128)(2,1)S(1)} %get-tuple-element.77.refs_2_.refs_3_.refs_7_), custom_call_target="tpu_custom_call" | custom-call | flops 4800000000 | bytes 4000000 | tf_op jit(solution)/shard_map/weights/pallas_call | solution.py:601
  71.7 1.4 %collective-permute-done.11 = bf16[768,128]{1,0:T(8,128)(2,1)S(1)} collective-permute-done((bf16[768,128]{1,0:T(8,128)(2,1)S(1)}, bf16[768,128]{1,0:T(8,128)(2,1)S(1)}, u32[]{:S(2)}, u32[]{:S(2)}) %collective-permute-start.11) | collective-permute-done | bytes 196640 | tf_op jit(solution)/shard_map/ppermute | solution.py:629
  73.3 2.0 %collective-permute-done.12.refs_10_ = bf16[2304,128]{1,0:T(8,128)(2,1)S(1)} collective-permute-done((bf16[2304,128]{1,0:T(8,128)(2,1)S(1)}, bf16[2304,128]{1,0:T(8,128)(2,1)S(1)}, u32[]{:S(2)}, u32[]{:S(2)}) %collective-permute-start.12) | collective-permute-done | bytes 589856 | tf_op jit(solution)/shard_map/ppermute | solution.py:635
  75.3 13.3 %sample.3 = (f32[3120,128]{1,0:T(8,128)S(1)}, f32[768,128]{1,0:T(8,128)}, bf16[48,512]{1,0:T(8,128)(2,1)S(1)}, bf16[48,512]{1,0:T(8,128)(2,1)S(1)}, bf16[48,512]...) custom-call(s32[48,128]{1,0:T(8,128)S(1)} %get-tuple-element.67.refs_0_, s32[48,128]{1,0:T(8,128)S(1)} %get-tuple-element.68.refs_1_, ...), custom_call_target="tpu_custom_call" | custom-call | flops 9600000000 | bytes 4000000 | tf_op jit(solution)/shard_map/sample/pallas_call | solution.py:644
  88.6 5.2 %collective-permute-start.16 = (bf16[48,512]{1,0:T(8,128)(2,1)S(1)}, bf16[48,512]{1,0:T(8,128)(2,1)S(1)}, u32[]{:S(2)}, u32[]{:S(2)}) collective-permute-start(bf16[48,512]{1,0:T(8,128)(2,1)S(1)} %get-tuple-element.106), channel_id=1, source_target_pairs={{0,16},{4,20},{8,24},{12,28},{16,0},{20,4},{24,8},{28,12},{1,17},{... | collective-permute-start | bytes 147464 | tf_op jit(solution)/shard_map/ppermute | solution.py:515
  93.8 1.4 %collective-permute-start.18 = (bf16[48,512]{1,0:T(8,128)(2,1)S(1)}, bf16[48,512]{1,0:T(8,128)(2,1)S(1)}, u32[]{:S(2)}, u32[]{:S(2)}) collective-permute-start(bf16[48,512]{1,0:T(8,128)(2,1)S(1)} %get-tuple-element.108), channel_id=1, source_target_pairs={{0,24},{4,28},{8,16},{12,20},{16,8},{20,12},{24,0},{28,4},{1,25},{... | collective-permute-start | bytes 147464 | tf_op jit(solution)/shard_map/ppermute | solution.py:515
  95.2 3.4 %collective-permute-start.19 = (bf16[48,512]{1,0:T(8,128)(2,1)S(1)}, bf16[48,512]{1,0:T(8,128)(2,1)S(1)}, u32[]{:S(2)}, u32[]{:S(2)}) collective-permute-start(bf16[48,512]{1,0:T(8,128)(2,1)S(1)} %get-tuple-element.109), channel_id=1, source_target_pairs={{0,28},{4,24},{8,20},{12,16},{16,12},{20,8},{24,4},{28,0},{1,29},{... | collective-permute-start | bytes 147464 | tf_op jit(solution)/shard_map/ppermute | solution.py:515
  98.6 11.9 %sample.5 = (bf16[48,512]{1,0:T(8,128)(2,1)S(1)}, bf16[48,512]{1,0:T(8,128)(2,1)S(1)}, bf16[48,512]{1,0:T(8,128)(2,1)S(1)}) custom-call(s32[48,128]{1,0:T(8,128)S(1)} %get-tuple-element.100.refs_0_, s32[48,128]{1,0:T(8,128)S(1)} %get-tuple-element.101.refs_1_, s32[48,128]{1,0:T(8,128)S(1)} %get-tuple-element.102.refs_2_, ...), custom_call_target="tpu_custom_call" | custom-call | flops 7200000000 | bytes 4000000 | tf_op jit(solution)/shard_map/sample/pallas_call | solution.py:644
  111.1 3.0 %collective-permute-start.15 = (bf16[48,512]{1,0:T(8,128)(2,1)S(1)}, bf16[48,512]{1,0:T(8,128)(2,1)S(1)}, u32[]{:S(2)}, u32[]{:S(2)}) collective-permute-start(bf16[48,512]{1,0:T(8,128)(2,1)S(1)} %get-tuple-element.105), channel_id=1, source_target_pairs={{0,12},{4,8},{8,4},{12,0},{16,28},{20,24},{24,20},{28,16},{1,13},{... | collective-permute-start | bytes 147464 | tf_op jit(solution)/shard_map/ppermute | solution.py:515
  114.1 4.5 %sample.4.refs_1_ = bf16[48,512]{1,0:T(8,128)(2,1)S(1)} custom-call(s32[48,128]{1,0:T(8,128)S(1)} %get-tuple-element.98.refs_0_, bf16[48,1664]{1,0:T(8,128)(2,1)S(1)} %copy-done.5, bf16[512,1152]{1,0:T(8,128)(2,1)S(1)} %get-tuple-element.94.refs_8_.refs_2_.refs_6_, bf16[1024,128]{1,0:T(8,128)(2,1)S(1)} %get-tuple-element.77.refs_2_.refs_3_.refs_7_, ...), custom_call_target="tpu_custom_call" | custom-call | flops 2400000000 | bytes 4000000 | tf_op jit(solution)/shard_map/sample/pallas_call | solution.py:644
  118.6 1.6 %unpack.1 = bf16[3,169,192]{2,1,0:T(8,128)(2,1)} custom-call(s32[1,192]{1,0:T(1,128)S(1)} %copy-done.2, bf16[48,512]{1,0:T(8,128)(2,1)S(1)} %sample.4.refs_1_, bf16[48,512]{1,0:T(8,128)(2,1)S(1)} %collective-permute-done.13.refs_2_, bf16[48,512]{1,0:T(8,128)(2,1)S(1)} %collective-permute-done.14.refs_3_, ...), custom_call_target="tpu_custom_call" | custom-call | tf_op jit(solution)/shard_map/unpack/pallas_call | solution.py:672
  (46 shorter events, 9.0 us)
Async XLA Ops:
  4.0 10.3 %collective-permute-start.4 = (bf16[48,1664]{1,0:T(8,128)(2,1)}, bf16[48,1664]{1,0:T(8,128)(2,1)S(1)}, u32[]{:S(2)}, u32[]{:S(2)}) collective-permute-start(bf16[48,1664]{1,0:T(8,128)(2,1)} %get-tuple-element.63), channel_id=1, source_target_pairs={{0,4},{4,0},{8,12},{12,8},{16,20},{20,16},{24,28},{28,24},{1,5},{5... | collective-permute-start | bytes 479240 | tf_op jit(solution)/shard_map/ppermute | solution.py:515
  7.0 13.0 %collective-permute-start.5 = (bf16[48,1664]{1,0:T(8,128)(2,1)}, bf16[48,1664]{1,0:T(8,128)(2,1)S(1)}, u32[]{:S(2)}, u32[]{:S(2)}) collective-permute-start(bf16[48,1664]{1,0:T(8,128)(2,1)} %get-tuple-element.64), channel_id=1, source_target_pairs={{0,8},{4,12},{8,0},{12,4},{16,24},{20,28},{24,16},{28,20},{1,9},{5... | collective-permute-start | bytes 479240 | tf_op jit(solution)/shard_map/ppermute | solution.py:515
  8.5 12.8 %collective-permute-start.6 = (bf16[48,1664]{1,0:T(8,128)(2,1)}, bf16[48,1664]{1,0:T(8,128)(2,1)S(1)}, u32[]{:S(2)}, u32[]{:S(2)}) collective-permute-start(bf16[48,1664]{1,0:T(8,128)(2,1)} %get-tuple-element.65), channel_id=1, source_target_pairs={{0,12},{4,8},{8,4},{12,0},{16,28},{20,24},{24,20},{28,16},{1,13},{... | collective-permute-start | bytes 479240 | tf_op jit(solution)/shard_map/ppermute | solution.py:515
  8.6 30.1 %collective-permute-start = (bf16[48,1664]{1,0:T(8,128)(2,1)}, bf16[48,1664]{1,0:T(8,128)(2,1)S(1)}, u32[]{:S(2)}, u32[]{:S(2)}) collective-permute-start(bf16[48,1664]{1,0:T(8,128)(2,1)} %get-tuple-element.56), channel_id=1, source_target_pairs={{0,16},{4,20},{8,24},{12,28},{16,0},{20,4},{24,8},{28,12},{1,17},{... | collective-permute-start | bytes 479240 | tf_op jit(solution)/shard_map/ppermute | solution.py:515
  11.5 27.1 %collective-permute-start.1 = (bf16[48,1664]{1,0:T(8,128)(2,1)}, bf16[48,1664]{1,0:T(8,128)(2,1)S(1)}, u32[]{:S(2)}, u32[]{:S(2)}) collective-permute-start(bf16[48,1664]{1,0:T(8,128)(2,1)} %get-tuple-element.57), channel_id=1, source_target_pairs={{0,20},{4,16},{8,28},{12,24},{16,4},{20,0},{24,12},{28,8},{1,21},{... | collective-permute-start | bytes 479240 | tf_op jit(solution)/shard_map/ppermute | solution.py:515
  14.3 24.3 %collective-permute-start.2 = (bf16[48,1664]{1,0:T(8,128)(2,1)}, bf16[48,1664]{1,0:T(8,128)(2,1)S(1)}, u32[]{:S(2)}, u32[]{:S(2)}) collective-permute-start(bf16[48,1664]{1,0:T(8,128)(2,1)} %get-tuple-element.58), channel_id=1, source_target_pairs={{0,24},{4,28},{8,16},{12,20},{16,8},{20,12},{24,0},{28,4},{1,25},{... | collective-permute-start | bytes 479240 | tf_op jit(solution)/shard_map/ppermute | solution.py:515
  20.0 18.6 %collective-permute-start.3 = (bf16[48,1664]{1,0:T(8,128)(2,1)}, bf16[48,1664]{1,0:T(8,128)(2,1)S(1)}, u32[]{:S(2)}, u32[]{:S(2)}) collective-permute-start(bf16[48,1664]{1,0:T(8,128)(2,1)} %get-tuple-element.59), channel_id=1, source_target_pairs={{0,28},{4,24},{8,20},{12,16},{16,12},{20,8},{24,4},{28,0},{1,29},{... | collective-permute-start | bytes 479240 | tf_op jit(solution)/shard_map/ppermute | solution.py:515
  21.3 1.0 copy-start.3
  52.8 8.9 %copy-start.1 = (bf16[169,338]{1,0:T(8,128)(2,1)S(1)}, bf16[169,338]{1,0:T(8,128)(2,1)}, u32[]{:S(2)}) copy-start(bf16[169,338]{1,0:T(8,128)(2,1)} %refs_0_.2) | copy-start | bytes 342736
  52.8 1.8 %collective-permute-start.7 = (bf16[1536,128]{1,0:T(8,128)(2,1)S(1)}, bf16[1536,128]{1,0:T(8,128)(2,1)S(1)}, u32[]{:S(2)}, u32[]{:S(2)}) collective-permute-start(bf16[1536,128]{1,0:T(8,128)(2,1)S(1)} %get-tuple-element.72), channel_id=1, source_target_pairs={{0,1},{1,0},{2,3},{3,2},{4,5},{5,4},{6,7},{7,6},{8,9},{9,8},{10,11... | collective-permute-start | bytes 1179656 | tf_op jit(solution)/shard_map/ppermute | solution.py:597
  54.7 12.2 %collective-permute-start.10 = (bf16[1536,128]{1,0:T(8,128)(2,1)S(1)}, bf16[1536,128]{1,0:T(8,128)(2,1)S(1)}, u32[]{:S(2)}, u32[]{:S(2)}) collective-permute-start(bf16[1536,128]{1,0:T(8,128)(2,1)S(1)} %add_convert_fusion.1), channel_id=1, source_target_pairs={{0,2},{1,3},{2,0},{3,1},{4,6},{5,7},{6,4},{7,5},{8,10},{9,11},{10,... | collective-permute-start | bytes 1179656 | tf_op jit(solution)/shard_map/ppermute | solution.py:626
  56.4 10.0 %collective-permute-start.8 = (bf16[384,128]{1,0:T(8,128)(2,1)S(1)}, bf16[384,128]{1,0:T(8,128)(2,1)S(1)}, u32[]{:S(2)}, u32[]{:S(2)}) collective-permute-start(bf16[384,128]{1,0:T(8,128)(2,1)S(1)} %get-tuple-element.110), channel_id=1, source_target_pairs={{0,4},{4,8},{8,12},{12,16},{16,20},{20,24},{24,28},{1,5},{5,9},{9,... | collective-permute-start | bytes 294920 | tf_op jit(solution)/shard_map/ppermute | solution.py:621
  60.4 6.5 %collective-permute-start.9 = (bf16[384,128]{1,0:T(8,128)(2,1)S(1)}, bf16[384,128]{1,0:T(8,128)(2,1)S(1)}, u32[]{:S(2)}, u32[]{:S(2)}) collective-permute-start(bf16[384,128]{1,0:T(8,128)(2,1)S(1)} %get-tuple-element.111), channel_id=1, source_target_pairs={{4,0},{8,4},{12,8},{16,12},{20,16},{24,20},{28,24},{5,1},{9,5},{13... | collective-permute-start | bytes 294920 | tf_op jit(solution)/shard_map/ppermute | solution.py:622
  67.0 6.0 %collective-permute-start.11 = (bf16[768,128]{1,0:T(8,128)(2,1)S(1)}, bf16[768,128]{1,0:T(8,128)(2,1)S(1)}, u32[]{:S(2)}, u32[]{:S(2)}) collective-permute-start(bf16[768,128]{1,0:T(8,128)(2,1)S(1)} %pad_maximum_fusion.1), channel_id=1, source_target_pairs={{0,2},{1,3},{2,0},{3,1},{4,6},{5,7},{6,4},{7,5},{8,10},{9,11},{10,... | collective-permute-start | bytes 589832 | tf_op jit(solution)/shard_map/ppermute | solution.py:629
  73.2 2.1 %collective-permute-start.12 = (bf16[2304,128]{1,0:T(8,128)(2,1)S(1)}, bf16[2304,128]{1,0:T(8,128)(2,1)S(1)}, u32[]{:S(2)}, u32[]{:S(2)}) collective-permute-start(bf16[2304,128]{1,0:T(8,128)(2,1)S(1)} %pad_maximum_fusion.refs_9_), channel_id=1, source_target_pairs={{0,1},{1,0},{2,3},{3,2},{4,5},{5,4},{6,7},{7,6},{8,9},{9,8},{10,11... | collective-permute-start | bytes 1769480 | tf_op jit(solution)/shard_map/ppermute | solution.py:635
  88.6 22.5 %collective-permute-start.16 = (bf16[48,512]{1,0:T(8,128)(2,1)S(1)}, bf16[48,512]{1,0:T(8,128)(2,1)S(1)}, u32[]{:S(2)}, u32[]{:S(2)}) collective-permute-start(bf16[48,512]{1,0:T(8,128)(2,1)S(1)} %get-tuple-element.106), channel_id=1, source_target_pairs={{0,16},{4,20},{8,24},{12,28},{16,0},{20,4},{24,8},{28,12},{1,17},{... | collective-permute-start | bytes 147464 | tf_op jit(solution)/shard_map/ppermute | solution.py:515
  93.8 17.3 %collective-permute-start.17 = (bf16[48,512]{1,0:T(8,128)(2,1)S(1)}, bf16[48,512]{1,0:T(8,128)(2,1)S(1)}, u32[]{:S(2)}, u32[]{:S(2)}) collective-permute-start(bf16[48,512]{1,0:T(8,128)(2,1)S(1)} %get-tuple-element.107), channel_id=1, source_target_pairs={{0,20},{4,16},{8,28},{12,24},{16,4},{20,0},{24,12},{28,8},{1,21},{... | collective-permute-start | bytes 147464 | tf_op jit(solution)/shard_map/ppermute | solution.py:515
  93.8 24.8 %collective-permute-start.18 = (bf16[48,512]{1,0:T(8,128)(2,1)S(1)}, bf16[48,512]{1,0:T(8,128)(2,1)S(1)}, u32[]{:S(2)}, u32[]{:S(2)}) collective-permute-start(bf16[48,512]{1,0:T(8,128)(2,1)S(1)} %get-tuple-element.108), channel_id=1, source_target_pairs={{0,24},{4,28},{8,16},{12,20},{16,8},{20,12},{24,0},{28,4},{1,25},{... | collective-permute-start | bytes 147464 | tf_op jit(solution)/shard_map/ppermute | solution.py:515
  95.2 23.3 %collective-permute-start.19 = (bf16[48,512]{1,0:T(8,128)(2,1)S(1)}, bf16[48,512]{1,0:T(8,128)(2,1)S(1)}, u32[]{:S(2)}, u32[]{:S(2)}) collective-permute-start(bf16[48,512]{1,0:T(8,128)(2,1)S(1)} %get-tuple-element.109), channel_id=1, source_target_pairs={{0,28},{4,24},{8,20},{12,16},{16,12},{20,8},{24,4},{28,0},{1,29},{... | collective-permute-start | bytes 147464 | tf_op jit(solution)/shard_map/ppermute | solution.py:515
  98.6 15.5 %copy-start.5 = (bf16[48,1664]{1,0:T(8,128)(2,1)S(1)}, bf16[48,1664]{1,0:T(8,128)(2,1)}, u32[]{:S(2)}) copy-start(bf16[48,1664]{1,0:T(8,128)(2,1)} %get-tuple-element.62.refs_0_.refs_1_) | copy-start | bytes 479236
  110.5 8.1 %collective-permute-start.13 = (bf16[48,512]{1,0:T(8,128)(2,1)S(1)}, bf16[48,512]{1,0:T(8,128)(2,1)S(1)}, u32[]{:S(2)}, u32[]{:S(2)}) collective-permute-start(bf16[48,512]{1,0:T(8,128)(2,1)S(1)} %get-tuple-element.103), channel_id=1, source_target_pairs={{0,4},{4,0},{8,12},{12,8},{16,20},{20,16},{24,28},{28,24},{1,5},{5... | collective-permute-start | bytes 147464 | tf_op jit(solution)/shard_map/ppermute | solution.py:515
  111.1 7.5 %collective-permute-start.14 = (bf16[48,512]{1,0:T(8,128)(2,1)S(1)}, bf16[48,512]{1,0:T(8,128)(2,1)S(1)}, u32[]{:S(2)}, u32[]{:S(2)}) collective-permute-start(bf16[48,512]{1,0:T(8,128)(2,1)S(1)} %get-tuple-element.104), channel_id=1, source_target_pairs={{0,8},{4,12},{8,0},{12,4},{16,24},{20,28},{24,16},{28,20},{1,9},{5... | collective-permute-start | bytes 147464 | tf_op jit(solution)/shard_map/ppermute | solution.py:515
  111.1 7.5 %collective-permute-start.15 = (bf16[48,512]{1,0:T(8,128)(2,1)S(1)}, bf16[48,512]{1,0:T(8,128)(2,1)S(1)}, u32[]{:S(2)}, u32[]{:S(2)}) collective-permute-start(bf16[48,512]{1,0:T(8,128)(2,1)S(1)} %get-tuple-element.105), channel_id=1, source_target_pairs={{0,12},{4,8},{8,4},{12,0},{16,28},{20,24},{24,20},{28,16},{1,13},{... | collective-permute-start | bytes 147464 | tf_op jit(solution)/shard_map/ppermute | solution.py:515
  114.1 4.5 %copy-start.2 = (s32[1,192]{1,0:T(1,128)S(1)}, s32[1,192]{1,0:T(1,128)}, u32[]{:S(2)}) copy-start(s32[1,192]{1,0:T(1,128)} %get-tuple-element.97.refs_0_) | copy-start | bytes 2308
  (2 other events, 1.8 us)

commit v5 on v4

--- a/solution.py
+++ b/solution.py
@@ -182,7 +182,11 @@
 def basis_kernel(sz, dim, basis, out, table):
     out[...] = jnp.zeros(out.shape, bf16)
     for k in range(3):
-        out[:, k * sz.qw : k * sz.qw + sz.points] = dot(place_terms(sz, k), basis[...]).astype(bf16)
+        points = slice(k * sz.qw, k * sz.qw + sz.points)
+        if dim:
+            out[:, points] = dot(place_terms(sz, k), basis[...]).astype(bf16)
+        else:
+            out[points] = dot(basis[...], place_terms(sz, k), 0, 1).astype(bf16)
     table[...] = height_table(table.shape, dim)
 
 
@@ -240,11 +244,7 @@
         copies.append(pltpu.make_async_copy(rows_out[i], rows_s.at[pl.ds(i * size, size)], sem.at[i]))
         copies[-1].start()
     load_records(sz, recv, points, lines)
-    base = 0
-    for part in recv:
-        size = part.shape[0]
-        forces[base : base + size] = dot(part[:, 3 * sz.qw :], expand[...])
-        base += size
+    forces[...] = dot(jnp.concatenate([part[:, 3 * sz.qw :] for part in recv], axis=0), expand[...])
     if begin:
         grid[...] = jnp.zeros(grid.shape, f32)
         size = nyb * planes
@@ -462,11 +462,11 @@
             base += w_in.shape[0]
     else:
         run_groups(count, prepare, use, ((w0, wz0), (w1, wz1)))
+    coef = dot(sampled[...].astype(bf16), expand[...]).astype(bf16)
     base = 0
     for ref in back:
-        size = ref.shape[0]
-        ref[...] = dot(sampled[base : base + size].astype(bf16), expand[...], 1, 1).astype(bf16)
-        base += size
+        ref[...] = coef[base : base + ref.shape[0]]
+        base += ref.shape[0]
 
 
 def unpack_kernel(sz, *refs):
@@ -541,12 +541,11 @@
     slot = send[chunks]
     recv = [exchange(send[p], p) for p in range(chunks)]
 
-    expand_shape = shape((sz.cw, 3 * sz.qw), bf16)
     def basis(values, dim):
         table = (TILE, GROUP * TILE) if dim else (GROUP * TILE, TILE)
         return pl.pallas_call(
             lambda *refs: basis_kernel(sz, dim, *refs),
-            out_shape=[expand_shape, shape(table, bf16)],
+            out_shape=[shape((sz.cw, 3 * sz.qw) if dim else (3 * sz.qw, sz.cw), bf16), shape(table, bf16)],
             in_specs=vmem(1),
             out_specs=vmem(2),
             compiler_params=params,

time: 121 us -> 118 us (0.975)
  Pallas kernels: 73.4 us -> 70.7 us
    pallas_call x3, Pallas kernels: 29.7 us -> 27.6 us  [local(): pl.pallas_call(lambda *refs: sample_kernel(sz, gx, ny, nyb, layers, slabs...]
where the time goes in v5:
time: 118 us
  Pallas kernels  70.7 us (60%)
  starting transfers between devices  35.5 us (30%)
  waiting for transfers between devices  7.83 us (7%)
  local copies, waits for them, and re-layouts  2.86 us (2%)
    pallas_call x2, Pallas kernels, local(): pl.pallas_call(lambda *refs: spread_kernel(sz, gx, ny, nyb, layers, parts...  28.9 us
    pallas_call x3, Pallas kernels, local(): pl.pallas_call(lambda *refs: sample_kernel(sz, gx, ny, nyb, layers, slabs...  27.6 us
    ppermute x14, starting transfers between devices, exchange(): lax.ppermute(value, 'slab', [(i, i ^ p) for i in range(slabs)])  27.5 us
    pallas_call x2, Pallas kernels, weights(): pl.pallas_call(lambda *refs: weights_kernel(sz, len(values), *refs), out_...  7.9 us
    ppermute x1, starting transfers between devices, local(): lax.ppermute(mine[-halo:], 'slab', [(i, i + 1) for i in range(slabs - 1)])  4.02 us
    pallas_call x1, Pallas kernels, local(): pl.pallas_call(lambda *refs: pack_kernel(sz, slabs, cap, chunks, pairwise...  3.37 us
    unnamed x12, local copies, waits for them, and re-layouts  2.83 us
  transfers between devices with their start and end apart: 20, of which 6 were waited for; matrix products, arithmetic and copies ran while one was open for 0% of the time, Pallas kernels for 34%

profile of v5, /device:TPU:0, one launch (start us, length us, event | category | flops | bytes accessed | tf_op | source)
XLA Modules:
  0.0 118.1 jit_solution(7666871948651362618)
XLA Ops:
  0.6 3.4 %pack.1 = (bf16[48,1664]{1,0:T(8,128)(2,1)}, bf16[48,1664]{1,0:T(8,128)(2,1)}, bf16[48,1664]{1,0:T(8,128)(2,1)}, bf16[48,1664]{1,0:T(8,128)(2,1)}, bf16[48,1664]...) custom-call(s32[1,192]{1,0:T(1,128)} %bitcast.19, ...), custom_call_target="tpu_custom_call" | custom-call | tf_op jit(solution)/shard_map/pack/pallas_call | solution.py:531
  4.0 3.0 %collective-permute-start.4 = (bf16[48,1664]{1,0:T(8,128)(2,1)}, bf16[48,1664]{1,0:T(8,128)(2,1)S(1)}, u32[]{:S(2)}, u32[]{:S(2)}) collective-permute-start(bf16[48,1664]{1,0:T(8,128)(2,1)} %get-tuple-element.63), channel_id=1, source_target_pairs={{0,4},{4,0},{8,12},{12,8},{16,20},{20,16},{24,28},{28,24},{1,5},{5... | collective-permute-start | bytes 479240 | tf_op jit(solution)/shard_map/ppermute | solution.py:515
  7.0 1.6 %collective-permute-start.5 = (bf16[48,1664]{1,0:T(8,128)(2,1)}, bf16[48,1664]{1,0:T(8,128)(2,1)S(1)}, u32[]{:S(2)}, u32[]{:S(2)}) collective-permute-start(bf16[48,1664]{1,0:T(8,128)(2,1)} %get-tuple-element.64), channel_id=1, source_target_pairs={{0,8},{4,12},{8,0},{12,4},{16,24},{20,28},{24,16},{28,20},{1,9},{5... | collective-permute-start | bytes 479240 | tf_op jit(solution)/shard_map/ppermute | solution.py:515
  8.6 3.0 %collective-permute-start = (bf16[48,1664]{1,0:T(8,128)(2,1)}, bf16[48,1664]{1,0:T(8,128)(2,1)S(1)}, u32[]{:S(2)}, u32[]{:S(2)}) collective-permute-start(bf16[48,1664]{1,0:T(8,128)(2,1)} %get-tuple-element.56), channel_id=1, source_target_pairs={{0,16},{4,20},{8,24},{12,28},{16,0},{20,4},{24,8},{28,12},{1,17},{... | collective-permute-start | bytes 479240 | tf_op jit(solution)/shard_map/ppermute | solution.py:515
  11.5 1.3 %collective-permute-start.1 = (bf16[48,1664]{1,0:T(8,128)(2,1)}, bf16[48,1664]{1,0:T(8,128)(2,1)S(1)}, u32[]{:S(2)}, u32[]{:S(2)}) collective-permute-start(bf16[48,1664]{1,0:T(8,128)(2,1)} %get-tuple-element.57), channel_id=1, source_target_pairs={{0,20},{4,16},{8,28},{12,24},{16,4},{20,0},{24,12},{28,8},{1,21},{... | collective-permute-start | bytes 479240 | tf_op jit(solution)/shard_map/ppermute | solution.py:515
  14.3 3.7 %collective-permute-start.2 = (bf16[48,1664]{1,0:T(8,128)(2,1)}, bf16[48,1664]{1,0:T(8,128)(2,1)S(1)}, u32[]{:S(2)}, u32[]{:S(2)}) collective-permute-start(bf16[48,1664]{1,0:T(8,128)(2,1)} %get-tuple-element.58), channel_id=1, source_target_pairs={{0,24},{4,28},{8,16},{12,20},{16,8},{20,12},{24,0},{28,4},{1,25},{... | collective-permute-start | bytes 479240 | tf_op jit(solution)/shard_map/ppermute | solution.py:515
  18.0 2.0 %collective-permute-done.5.refs_2_.refs_4_ = bf16[48,1664]{1,0:T(8,128)(2,1)S(1)} collective-permute-done((bf16[48,1664]{1,0:T(8,128)(2,1)}, bf16[48,1664]{1,0:T(8,128)(2,1)S(1)}, u32[]{:S(2)}, u32[]{:S(2)}) %collective-permute-start.5) | collective-permute-done | bytes 159776 | tf_op jit(solution)/shard_map/ppermute | solution.py:515
  23.2 14.9 %spread.2 = (f32[3120,128]{1,0:T(8,128)S(1)}, s32[48,128]{1,0:T(8,128)S(1)}, s32[48,128]{1,0:T(8,128)S(1)}, s32[48,128]{1,0:T(8,128)S(1)}, s32[48,128]{1,0:T(8,128)S(1)}) custom-call(bf16[48,1664]{1,0:T(8,128)(2,1)S(1)} %copy-done.4, bf16[48,1664]{1,0:T(8,128)(2,1)S(1)} %collective-permute-done.4.refs_1_.refs_3_, ...), custom_call_target="tpu_custom_call" | custom-call | flops 19200000000 | bytes 4000000 | tf_op jit(solution)/shard_map/spread/pallas_call | solution.py:568
  38.2 13.9 %spread.3 = (f32[3120,128]{1,0:T(8,128)S(1)}, s32[48,128]{1,0:T(8,128)S(1)}, s32[48,128]{1,0:T(8,128)S(1)}, s32[48,128]{1,0:T(8,128)S(1)}, s32[48,128]{1,0:T(8,1...) custom-call(bf16[48,1664]{1,0:T(8,128)(2,1)S(1)} %collective-permute-done.r, ...), custom_call_target="tpu_custom_call", output_to_operand_aliasing={{0}: (6, {})} | custom-call | flops 19200000000 | bytes 4000000 | tf_op jit(solution)/shard_map/spread/pallas_call | solution.py:568
  52.3 1.7 %collective-permute-done.7 = bf16[1536,128]{1,0:T(8,128)(2,1)S(1)} collective-permute-done((bf16[1536,128]{1,0:T(8,128)(2,1)S(1)}, bf16[1536,128]{1,0:T(8,128)(2,1)S(1)}, u32[]{:S(2)}, u32[]{:S(2)}) %collective-permute-start.7) | collective-permute-done | bytes 393248 | tf_op jit(solution)/shard_map/ppermute | solution.py:596
  54.1 1.7 %collective-permute-start.10 = (bf16[1536,128]{1,0:T(8,128)(2,1)S(1)}, bf16[1536,128]{1,0:T(8,128)(2,1)S(1)}, u32[]{:S(2)}, u32[]{:S(2)}) collective-permute-start(bf16[1536,128]{1,0:T(8,128)(2,1)S(1)} %add_convert_fusion.1), channel_id=1, source_target_pairs={{0,2},{1,3},{2,0},{3,1},{4,6},{5,7},{6,4},{7,5},{8,10},{9,11},{10,... | collective-permute-start | bytes 1179656 | tf_op jit(solution)/shard_map/ppermute | solution.py:625
  55.8 4.0 %collective-permute-start.8 = (bf16[384,128]{1,0:T(8,128)(2,1)S(1)}, bf16[384,128]{1,0:T(8,128)(2,1)S(1)}, u32[]{:S(2)}, u32[]{:S(2)}) collective-permute-start(bf16[384,128]{1,0:T(8,128)(2,1)S(1)} %get-tuple-element.110), channel_id=1, source_target_pairs={{0,4},{4,8},{8,12},{12,16},{16,20},{20,24},{24,28},{1,5},{5,9},{9,... | collective-permute-start | bytes 294920 | tf_op jit(solution)/shard_map/ppermute | solution.py:620
  59.8 1.5 %collective-permute-start.9 = (bf16[384,128]{1,0:T(8,128)(2,1)S(1)}, bf16[384,128]{1,0:T(8,128)(2,1)S(1)}, u32[]{:S(2)}, u32[]{:S(2)}) collective-permute-start(bf16[384,128]{1,0:T(8,128)(2,1)S(1)} %get-tuple-element.111), channel_id=1, source_target_pairs={{4,0},{8,4},{12,8},{16,12},{20,16},{24,20},{28,24},{5,1},{9,5},{13... | collective-permute-start | bytes 294920 | tf_op jit(solution)/shard_map/ppermute | solution.py:621
  62.1 3.9 %weights.2 = (f32[12,128,384]{2,1,0:T(8,128)S(1)}, bf16[12,1024,384]{2,1,0:T(8,128)(2,1)S(1)}) custom-call(bf16[48,1664]{1,0:T(8,128)(2,1)S(1)} %collective-permute-done.refs_0_, bf16[48,1664]{1,0:T(8,128)(2,1)S(1)} %collective-permute-done.1.refs_1_, bf16[1024,128]{1,0:T(8,128)(2,1)S(1)} %get-tuple-element.77.refs_2_.refs_3_.refs_7_), custom_call_target="tpu_custom_call" | custom-call | flops 4800000000 | bytes 4000000 | tf_op jit(solution)/shard_map/weights/pallas_call | solution.py:600
  67.1 4.0 %weights.3 = (f32[12,128,384]{2,1,0:T(8,128)S(1)}, bf16[12,1024,384]{2,1,0:T(8,128)(2,1)S(1)}) custom-call(bf16[48,1664]{1,0:T(8,128)(2,1)S(1)} %collective-permute-done.2.refs_2_.refs_0_, bf16[48,1664]{1,0:T(8,128)(2,1)S(1)} %collective-permute-done.3.refs_3_.refs_1_, bf16[1024,128]{1,0:T(8,128)(2,1)S(1)} %get-tuple-element.77.refs_2_.refs_3_.refs_7_), custom_call_target="tpu_custom_call" | custom-call | flops 4800000000 | bytes 4000000 | tf_op jit(solution)/shard_map/weights/pallas_call | solution.py:600
  71.1 1.6 %collective-permute-done.11 = bf16[768,128]{1,0:T(8,128)(2,1)S(1)} collective-permute-done((bf16[768,128]{1,0:T(8,128)(2,1)S(1)}, bf16[768,128]{1,0:T(8,128)(2,1)S(1)}, u32[]{:S(2)}, u32[]{:S(2)}) %collective-permute-start.11) | collective-permute-done | bytes 196640 | tf_op jit(solution)/shard_map/ppermute | solution.py:628
  72.9 2.0 %collective-permute-done.12.refs_10_ = bf16[2304,128]{1,0:T(8,128)(2,1)S(1)} collective-permute-done((bf16[2304,128]{1,0:T(8,128)(2,1)S(1)}, bf16[2304,128]{1,0:T(8,128)(2,1)S(1)}, u32[]{:S(2)}, u32[]{:S(2)}) %collective-permute-start.12) | collective-permute-done | bytes 589856 | tf_op jit(solution)/shard_map/ppermute | solution.py:634
  74.9 12.1 %sample.3 = (f32[3120,128]{1,0:T(8,128)S(1)}, f32[768,128]{1,0:T(8,128)}, bf16[48,512]{1,0:T(8,128)(2,1)S(1)}, bf16[48,512]{1,0:T(8,128)(2,1)S(1)}, bf16[48,512]...) custom-call(s32[48,128]{1,0:T(8,128)S(1)} %get-tuple-element.67.refs_0_, s32[48,128]{1,0:T(8,128)S(1)} %get-tuple-element.68.refs_1_, ...), custom_call_target="tpu_custom_call" | custom-call | flops 9600000000 | bytes 4000000 | tf_op jit(solution)/shard_map/sample/pallas_call | solution.py:643
  87.0 5.5 %collective-permute-start.16 = (bf16[48,512]{1,0:T(8,128)(2,1)S(1)}, bf16[48,512]{1,0:T(8,128)(2,1)S(1)}, u32[]{:S(2)}, u32[]{:S(2)}) collective-permute-start(bf16[48,512]{1,0:T(8,128)(2,1)S(1)} %get-tuple-element.106), channel_id=1, source_target_pairs={{0,16},{4,20},{8,24},{12,28},{16,0},{20,4},{24,8},{28,12},{1,17},{... | collective-permute-start | bytes 147464 | tf_op jit(solution)/shard_map/ppermute | solution.py:515
  93.8 3.5 %collective-permute-start.19 = (bf16[48,512]{1,0:T(8,128)(2,1)S(1)}, bf16[48,512]{1,0:T(8,128)(2,1)S(1)}, u32[]{:S(2)}, u32[]{:S(2)}) collective-permute-start(bf16[48,512]{1,0:T(8,128)(2,1)S(1)} %get-tuple-element.109), channel_id=1, source_target_pairs={{0,28},{4,24},{8,20},{12,16},{16,12},{20,8},{24,4},{28,0},{1,29},{... | collective-permute-start | bytes 147464 | tf_op jit(solution)/shard_map/ppermute | solution.py:515
  97.3 11.1 %sample.5 = (bf16[48,512]{1,0:T(8,128)(2,1)S(1)}, bf16[48,512]{1,0:T(8,128)(2,1)S(1)}, bf16[48,512]{1,0:T(8,128)(2,1)S(1)}) custom-call(s32[48,128]{1,0:T(8,128)S(1)} %get-tuple-element.100.refs_0_, s32[48,128]{1,0:T(8,128)S(1)} %get-tuple-element.101.refs_1_, s32[48,128]{1,0:T(8,128)S(1)} %get-tuple-element.102.refs_2_, ...), custom_call_target="tpu_custom_call" | custom-call | flops 7200000000 | bytes 4000000 | tf_op jit(solution)/shard_map/sample/pallas_call | solution.py:643
  109.0 3.0 %collective-permute-start.15 = (bf16[48,512]{1,0:T(8,128)(2,1)S(1)}, bf16[48,512]{1,0:T(8,128)(2,1)S(1)}, u32[]{:S(2)}, u32[]{:S(2)}) collective-permute-start(bf16[48,512]{1,0:T(8,128)(2,1)S(1)} %get-tuple-element.105), channel_id=1, source_target_pairs={{0,12},{4,8},{8,4},{12,0},{16,28},{20,24},{24,20},{28,16},{1,13},{... | collective-permute-start | bytes 147464 | tf_op jit(solution)/shard_map/ppermute | solution.py:515
  112.0 4.4 %sample.4.refs_1_ = bf16[48,512]{1,0:T(8,128)(2,1)S(1)} custom-call(s32[48,128]{1,0:T(8,128)S(1)} %get-tuple-element.98.refs_0_, bf16[48,1664]{1,0:T(8,128)(2,1)S(1)} %copy-done.5, bf16[1152,512]{1,0:T(8,128)(2,1)S(1)} %get-tuple-element.94.refs_8_.refs_2_.refs_6_, bf16[1024,128]{1,0:T(8,128)(2,1)S(1)} %get-tuple-element.77.refs_2_.refs_3_.refs_7_, ...), custom_call_target="tpu_custom_call" | custom-call | flops 2400000000 | bytes 4000000 | tf_op jit(solution)/shard_map/sample/pallas_call | solution.py:643
  116.5 1.6 %unpack.1 = bf16[3,169,192]{2,1,0:T(8,128)(2,1)} custom-call(s32[1,192]{1,0:T(1,128)S(1)} %copy-done.2, bf16[48,512]{1,0:T(8,128)(2,1)S(1)} %sample.4.refs_1_, bf16[48,512]{1,0:T(8,128)(2,1)S(1)} %collective-permute-done.13.refs_2_, bf16[48,512]{1,0:T(8,128)(2,1)S(1)} %collective-permute-done.14.refs_3_, ...), custom_call_target="tpu_custom_call" | custom-call | tf_op jit(solution)/shard_map/unpack/pallas_call | solution.py:671
  (46 shorter events, 8.8 us)
Async XLA Ops:
  4.0 10.3 %collective-permute-start.4 = (bf16[48,1664]{1,0:T(8,128)(2,1)}, bf16[48,1664]{1,0:T(8,128)(2,1)S(1)}, u32[]{:S(2)}, u32[]{:S(2)}) collective-permute-start(bf16[48,1664]{1,0:T(8,128)(2,1)} %get-tuple-element.63), channel_id=1, source_target_pairs={{0,4},{4,0},{8,12},{12,8},{16,20},{20,16},{24,28},{28,24},{1,5},{5... | collective-permute-start | bytes 479240 | tf_op jit(solution)/shard_map/ppermute | solution.py:515
  7.0 13.0 %collective-permute-start.5 = (bf16[48,1664]{1,0:T(8,128)(2,1)}, bf16[48,1664]{1,0:T(8,128)(2,1)S(1)}, u32[]{:S(2)}, u32[]{:S(2)}) collective-permute-start(bf16[48,1664]{1,0:T(8,128)(2,1)} %get-tuple-element.64), channel_id=1, source_target_pairs={{0,8},{4,12},{8,0},{12,4},{16,24},{20,28},{24,16},{28,20},{1,9},{5... | collective-permute-start | bytes 479240 | tf_op jit(solution)/shard_map/ppermute | solution.py:515
  8.5 12.8 %collective-permute-start.6 = (bf16[48,1664]{1,0:T(8,128)(2,1)}, bf16[48,1664]{1,0:T(8,128)(2,1)S(1)}, u32[]{:S(2)}, u32[]{:S(2)}) collective-permute-start(bf16[48,1664]{1,0:T(8,128)(2,1)} %get-tuple-element.65), channel_id=1, source_target_pairs={{0,12},{4,8},{8,4},{12,0},{16,28},{20,24},{24,20},{28,16},{1,13},{... | collective-permute-start | bytes 479240 | tf_op jit(solution)/shard_map/ppermute | solution.py:515
  8.6 29.6 %collective-permute-start = (bf16[48,1664]{1,0:T(8,128)(2,1)}, bf16[48,1664]{1,0:T(8,128)(2,1)S(1)}, u32[]{:S(2)}, u32[]{:S(2)}) collective-permute-start(bf16[48,1664]{1,0:T(8,128)(2,1)} %get-tuple-element.56), channel_id=1, source_target_pairs={{0,16},{4,20},{8,24},{12,28},{16,0},{20,4},{24,8},{28,12},{1,17},{... | collective-permute-start | bytes 479240 | tf_op jit(solution)/shard_map/ppermute | solution.py:515
  11.5 26.7 %collective-permute-start.1 = (bf16[48,1664]{1,0:T(8,128)(2,1)}, bf16[48,1664]{1,0:T(8,128)(2,1)S(1)}, u32[]{:S(2)}, u32[]{:S(2)}) collective-permute-start(bf16[48,1664]{1,0:T(8,128)(2,1)} %get-tuple-element.57), channel_id=1, source_target_pairs={{0,20},{4,16},{8,28},{12,24},{16,4},{20,0},{24,12},{28,8},{1,21},{... | collective-permute-start | bytes 479240 | tf_op jit(solution)/shard_map/ppermute | solution.py:515
  14.3 23.9 %collective-permute-start.2 = (bf16[48,1664]{1,0:T(8,128)(2,1)}, bf16[48,1664]{1,0:T(8,128)(2,1)S(1)}, u32[]{:S(2)}, u32[]{:S(2)}) collective-permute-start(bf16[48,1664]{1,0:T(8,128)(2,1)} %get-tuple-element.58), channel_id=1, source_target_pairs={{0,24},{4,28},{8,16},{12,20},{16,8},{20,12},{24,0},{28,4},{1,25},{... | collective-permute-start | bytes 479240 | tf_op jit(solution)/shard_map/ppermute | solution.py:515
  20.0 18.2 %collective-permute-start.3 = (bf16[48,1664]{1,0:T(8,128)(2,1)}, bf16[48,1664]{1,0:T(8,128)(2,1)S(1)}, u32[]{:S(2)}, u32[]{:S(2)}) collective-permute-start(bf16[48,1664]{1,0:T(8,128)(2,1)} %get-tuple-element.59), channel_id=1, source_target_pairs={{0,28},{4,24},{8,20},{12,16},{16,12},{20,8},{24,4},{28,0},{1,29},{... | collective-permute-start | bytes 479240 | tf_op jit(solution)/shard_map/ppermute | solution.py:515
  21.3 1.0 copy-start.3
  52.2 9.2 %copy-start.1 = (bf16[169,338]{1,0:T(8,128)(2,1)S(1)}, bf16[169,338]{1,0:T(8,128)(2,1)}, u32[]{:S(2)}) copy-start(bf16[169,338]{1,0:T(8,128)(2,1)} %refs_0_.2) | copy-start | bytes 342736
  52.2 1.8 %collective-permute-start.7 = (bf16[1536,128]{1,0:T(8,128)(2,1)S(1)}, bf16[1536,128]{1,0:T(8,128)(2,1)S(1)}, u32[]{:S(2)}, u32[]{:S(2)}) collective-permute-start(bf16[1536,128]{1,0:T(8,128)(2,1)S(1)} %get-tuple-element.72), channel_id=1, source_target_pairs={{0,1},{1,0},{2,3},{3,2},{4,5},{5,4},{6,7},{7,6},{8,9},{9,8},{10,11... | collective-permute-start | bytes 1179656 | tf_op jit(solution)/shard_map/ppermute | solution.py:596
  54.1 12.3 %collective-permute-start.10 = (bf16[1536,128]{1,0:T(8,128)(2,1)S(1)}, bf16[1536,128]{1,0:T(8,128)(2,1)S(1)}, u32[]{:S(2)}, u32[]{:S(2)}) collective-permute-start(bf16[1536,128]{1,0:T(8,128)(2,1)S(1)} %add_convert_fusion.1), channel_id=1, source_target_pairs={{0,2},{1,3},{2,0},{3,1},{4,6},{5,7},{6,4},{7,5},{8,10},{9,11},{10,... | collective-permute-start | bytes 1179656 | tf_op jit(solution)/shard_map/ppermute | solution.py:625
  55.8 10.2 %collective-permute-start.8 = (bf16[384,128]{1,0:T(8,128)(2,1)S(1)}, bf16[384,128]{1,0:T(8,128)(2,1)S(1)}, u32[]{:S(2)}, u32[]{:S(2)}) collective-permute-start(bf16[384,128]{1,0:T(8,128)(2,1)S(1)} %get-tuple-element.110), channel_id=1, source_target_pairs={{0,4},{4,8},{8,12},{12,16},{16,20},{20,24},{24,28},{1,5},{5,9},{9,... | collective-permute-start | bytes 294920 | tf_op jit(solution)/shard_map/ppermute | solution.py:620
  59.8 6.5 %collective-permute-start.9 = (bf16[384,128]{1,0:T(8,128)(2,1)S(1)}, bf16[384,128]{1,0:T(8,128)(2,1)S(1)}, u32[]{:S(2)}, u32[]{:S(2)}) collective-permute-start(bf16[384,128]{1,0:T(8,128)(2,1)S(1)} %get-tuple-element.111), channel_id=1, source_target_pairs={{4,0},{8,4},{12,8},{16,12},{20,16},{24,20},{28,24},{5,1},{9,5},{13... | collective-permute-start | bytes 294920 | tf_op jit(solution)/shard_map/ppermute | solution.py:621
  66.5 6.2 %collective-permute-start.11 = (bf16[768,128]{1,0:T(8,128)(2,1)S(1)}, bf16[768,128]{1,0:T(8,128)(2,1)S(1)}, u32[]{:S(2)}, u32[]{:S(2)}) collective-permute-start(bf16[768,128]{1,0:T(8,128)(2,1)S(1)} %pad_maximum_fusion.1), channel_id=1, source_target_pairs={{0,2},{1,3},{2,0},{3,1},{4,6},{5,7},{6,4},{7,5},{8,10},{9,11},{10,... | collective-permute-start | bytes 589832 | tf_op jit(solution)/shard_map/ppermute | solution.py:628
  72.8 2.1 %collective-permute-start.12 = (bf16[2304,128]{1,0:T(8,128)(2,1)S(1)}, bf16[2304,128]{1,0:T(8,128)(2,1)S(1)}, u32[]{:S(2)}, u32[]{:S(2)}) collective-permute-start(bf16[2304,128]{1,0:T(8,128)(2,1)S(1)} %pad_maximum_fusion.refs_9_), channel_id=1, source_target_pairs={{0,1},{1,0},{2,3},{3,2},{4,5},{5,4},{6,7},{7,6},{8,9},{9,8},{10,11... | collective-permute-start | bytes 1769480 | tf_op jit(solution)/shard_map/ppermute | solution.py:634
  87.0 22.0 %collective-permute-start.16 = (bf16[48,512]{1,0:T(8,128)(2,1)S(1)}, bf16[48,512]{1,0:T(8,128)(2,1)S(1)}, u32[]{:S(2)}, u32[]{:S(2)}) collective-permute-start(bf16[48,512]{1,0:T(8,128)(2,1)S(1)} %get-tuple-element.106), channel_id=1, source_target_pairs={{0,16},{4,20},{8,24},{12,28},{16,0},{20,4},{24,8},{28,12},{1,17},{... | collective-permute-start | bytes 147464 | tf_op jit(solution)/shard_map/ppermute | solution.py:515
  92.5 16.5 %collective-permute-start.17 = (bf16[48,512]{1,0:T(8,128)(2,1)S(1)}, bf16[48,512]{1,0:T(8,128)(2,1)S(1)}, u32[]{:S(2)}, u32[]{:S(2)}) collective-permute-start(bf16[48,512]{1,0:T(8,128)(2,1)S(1)} %get-tuple-element.107), channel_id=1, source_target_pairs={{0,20},{4,16},{8,28},{12,24},{16,4},{20,0},{24,12},{28,8},{1,21},{... | collective-permute-start | bytes 147464 | tf_op jit(solution)/shard_map/ppermute | solution.py:515
  92.5 23.9 %collective-permute-start.18 = (bf16[48,512]{1,0:T(8,128)(2,1)S(1)}, bf16[48,512]{1,0:T(8,128)(2,1)S(1)}, u32[]{:S(2)}, u32[]{:S(2)}) collective-permute-start(bf16[48,512]{1,0:T(8,128)(2,1)S(1)} %get-tuple-element.108), channel_id=1, source_target_pairs={{0,24},{4,28},{8,16},{12,20},{16,8},{20,12},{24,0},{28,4},{1,25},{... | collective-permute-start | bytes 147464 | tf_op jit(solution)/shard_map/ppermute | solution.py:515
  93.8 22.6 %collective-permute-start.19 = (bf16[48,512]{1,0:T(8,128)(2,1)S(1)}, bf16[48,512]{1,0:T(8,128)(2,1)S(1)}, u32[]{:S(2)}, u32[]{:S(2)}) collective-permute-start(bf16[48,512]{1,0:T(8,128)(2,1)S(1)} %get-tuple-element.109), channel_id=1, source_target_pairs={{0,28},{4,24},{8,20},{12,16},{16,12},{20,8},{24,4},{28,0},{1,29},{... | collective-permute-start | bytes 147464 | tf_op jit(solution)/shard_map/ppermute | solution.py:515
  97.3 14.7 %copy-start.5 = (bf16[48,1664]{1,0:T(8,128)(2,1)S(1)}, bf16[48,1664]{1,0:T(8,128)(2,1)}, u32[]{:S(2)}) copy-start(bf16[48,1664]{1,0:T(8,128)(2,1)} %get-tuple-element.62.refs_0_.refs_1_) | copy-start | bytes 479236
  108.5 8.0 %collective-permute-start.13 = (bf16[48,512]{1,0:T(8,128)(2,1)S(1)}, bf16[48,512]{1,0:T(8,128)(2,1)S(1)}, u32[]{:S(2)}, u32[]{:S(2)}) collective-permute-start(bf16[48,512]{1,0:T(8,128)(2,1)S(1)} %get-tuple-element.103), channel_id=1, source_target_pairs={{0,4},{4,0},{8,12},{12,8},{16,20},{20,16},{24,28},{28,24},{1,5},{5... | collective-permute-start | bytes 147464 | tf_op jit(solution)/shard_map/ppermute | solution.py:515
  109.0 7.4 %collective-permute-start.14 = (bf16[48,512]{1,0:T(8,128)(2,1)S(1)}, bf16[48,512]{1,0:T(8,128)(2,1)S(1)}, u32[]{:S(2)}, u32[]{:S(2)}) collective-permute-start(bf16[48,512]{1,0:T(8,128)(2,1)S(1)} %get-tuple-element.104), channel_id=1, source_target_pairs={{0,8},{4,12},{8,0},{12,4},{16,24},{20,28},{24,16},{28,20},{1,9},{5... | collective-permute-start | bytes 147464 | tf_op jit(solution)/shard_map/ppermute | solution.py:515
  109.0 7.4 %collective-permute-start.15 = (bf16[48,512]{1,0:T(8,128)(2,1)S(1)}, bf16[48,512]{1,0:T(8,128)(2,1)S(1)}, u32[]{:S(2)}, u32[]{:S(2)}) collective-permute-start(bf16[48,512]{1,0:T(8,128)(2,1)S(1)} %get-tuple-element.105), channel_id=1, source_target_pairs={{0,12},{4,8},{8,4},{12,0},{16,28},{20,24},{24,20},{28,16},{1,13},{... | collective-permute-start | bytes 147464 | tf_op jit(solution)/shard_map/ppermute | solution.py:515
  112.0 4.4 %copy-start.2 = (s32[1,192]{1,0:T(1,128)S(1)}, s32[1,192]{1,0:T(1,128)}, u32[]{:S(2)}) copy-start(s32[1,192]{1,0:T(1,128)} %get-tuple-element.97.refs_0_) | copy-start | bytes 2308
  (2 other events, 1.8 us)

commit v6 on v5

--- a/solution.py
+++ b/solution.py
@@ -472,11 +472,9 @@
 def unpack_kernel(sz, *refs):
     slot, out = refs[0], refs[-1]
     parts = refs[1:-1]
-    cells, size = slot.shape[1], parts[0].shape[0]
-    coef = jnp.zeros((cells, sz.cw), f32)
-    for c, back in enumerate(parts):
-        place = one_hot(slot[...] == iota((size, cells), 0) + c * size)
-        coef = coef + dot(place, back[...], 0, 0)
+    back = jnp.concatenate([part[...] for part in parts], axis=0)
+    place = one_hot(slot[...] == iota((back.shape[0], slot.shape[1]), 0))
+    coef = dot(place, back, 0, 0)
     coef = coef.astype(bf16)
     for k in range(3):
         shape = (sz.terms, sz.cw)

time: 118 us -> 118 us (level)
  no operation moved by 1% of the time
where the time goes in v6:
time: 118 us
  Pallas kernels  70.3 us (60%)
  starting transfers between devices  35.6 us (30%)
  waiting for transfers between devices  7.81 us (7%)
  local copies, waits for them, and re-layouts  2.86 us (2%)
    pallas_call x2, Pallas kernels, local(): pl.pallas_call(lambda *refs: spread_kernel(sz, gx, ny, nyb, layers, parts...  28.8 us
    pallas_call x3, Pallas kernels, local(): pl.pallas_call(lambda *refs: sample_kernel(sz, gx, ny, nyb, layers, slabs...  27.6 us
    ppermute x14, starting transfers between devices, exchange(): lax.ppermute(value, 'slab', [(i, i ^ p) for i in range(slabs)])  27.5 us
    pallas_call x2, Pallas kernels, weights(): pl.pallas_call(lambda *refs: weights_kernel(sz, len(values), *refs), out_...  7.91 us
    ppermute x1, starting transfers between devices, local(): lax.ppermute(mine[-halo:], 'slab', [(i, i + 1) for i in range(slabs - 1)])  4.1 us
    pallas_call x1, Pallas kernels, local(): pl.pallas_call(lambda *refs: pack_kernel(sz, slabs, cap, chunks, pairwise...  3.37 us
    unnamed x12, local copies, waits for them, and re-layouts  2.83 us
  transfers between devices with their start and end apart: 20, of which 6 were waited for; matrix products, arithmetic and copies ran while one was open for 0% of the time, Pallas kernels for 34%

profile of v6, /device:TPU:0, one launch (start us, length us, event | category | flops | bytes accessed | tf_op | source)
XLA Modules:
  0.0 117.9 jit_solution(11991833588974540061)
XLA Ops:
  0.6 3.4 %pack.1 = (bf16[48,1664]{1,0:T(8,128)(2,1)}, bf16[48,1664]{1,0:T(8,128)(2,1)}, bf16[48,1664]{1,0:T(8,128)(2,1)}, bf16[48,1664]{1,0:T(8,128)(2,1)}, bf16[48,1664]...) custom-call(s32[1,192]{1,0:T(1,128)} %bitcast.19, ...), custom_call_target="tpu_custom_call" | custom-call | tf_op jit(solution)/shard_map/pack/pallas_call | solution.py:529
  4.0 3.0 %collective-permute-start.4 = (bf16[48,1664]{1,0:T(8,128)(2,1)}, bf16[48,1664]{1,0:T(8,128)(2,1)S(1)}, u32[]{:S(2)}, u32[]{:S(2)}) collective-permute-start(bf16[48,1664]{1,0:T(8,128)(2,1)} %get-tuple-element.63), channel_id=1, source_target_pairs={{0,4},{4,0},{8,12},{12,8},{16,20},{20,16},{24,28},{28,24},{1,5},{5... | collective-permute-start | bytes 479240 | tf_op jit(solution)/shard_map/ppermute | solution.py:513
  7.0 1.6 %collective-permute-start.5 = (bf16[48,1664]{1,0:T(8,128)(2,1)}, bf16[48,1664]{1,0:T(8,128)(2,1)S(1)}, u32[]{:S(2)}, u32[]{:S(2)}) collective-permute-start(bf16[48,1664]{1,0:T(8,128)(2,1)} %get-tuple-element.64), channel_id=1, source_target_pairs={{0,8},{4,12},{8,0},{12,4},{16,24},{20,28},{24,16},{28,20},{1,9},{5... | collective-permute-start | bytes 479240 | tf_op jit(solution)/shard_map/ppermute | solution.py:513
  8.6 3.0 %collective-permute-start = (bf16[48,1664]{1,0:T(8,128)(2,1)}, bf16[48,1664]{1,0:T(8,128)(2,1)S(1)}, u32[]{:S(2)}, u32[]{:S(2)}) collective-permute-start(bf16[48,1664]{1,0:T(8,128)(2,1)} %get-tuple-element.56), channel_id=1, source_target_pairs={{0,16},{4,20},{8,24},{12,28},{16,0},{20,4},{24,8},{28,12},{1,17},{... | collective-permute-start | bytes 479240 | tf_op jit(solution)/shard_map/ppermute | solution.py:513
  11.5 1.3 %collective-permute-start.1 = (bf16[48,1664]{1,0:T(8,128)(2,1)}, bf16[48,1664]{1,0:T(8,128)(2,1)S(1)}, u32[]{:S(2)}, u32[]{:S(2)}) collective-permute-start(bf16[48,1664]{1,0:T(8,128)(2,1)} %get-tuple-element.57), channel_id=1, source_target_pairs={{0,20},{4,16},{8,28},{12,24},{16,4},{20,0},{24,12},{28,8},{1,21},{... | collective-permute-start | bytes 479240 | tf_op jit(solution)/shard_map/ppermute | solution.py:513
  14.3 3.7 %collective-permute-start.2 = (bf16[48,1664]{1,0:T(8,128)(2,1)}, bf16[48,1664]{1,0:T(8,128)(2,1)S(1)}, u32[]{:S(2)}, u32[]{:S(2)}) collective-permute-start(bf16[48,1664]{1,0:T(8,128)(2,1)} %get-tuple-element.58), channel_id=1, source_target_pairs={{0,24},{4,28},{8,16},{12,20},{16,8},{20,12},{24,0},{28,4},{1,25},{... | collective-permute-start | bytes 479240 | tf_op jit(solution)/shard_map/ppermute | solution.py:513
  18.0 2.0 %collective-permute-done.5.refs_2_.refs_4_ = bf16[48,1664]{1,0:T(8,128)(2,1)S(1)} collective-permute-done((bf16[48,1664]{1,0:T(8,128)(2,1)}, bf16[48,1664]{1,0:T(8,128)(2,1)S(1)}, u32[]{:S(2)}, u32[]{:S(2)}) %collective-permute-start.5) | collective-permute-done | bytes 159776 | tf_op jit(solution)/shard_map/ppermute | solution.py:513
  23.2 14.9 %spread.2 = (f32[3120,128]{1,0:T(8,128)S(1)}, s32[48,128]{1,0:T(8,128)S(1)}, s32[48,128]{1,0:T(8,128)S(1)}, s32[48,128]{1,0:T(8,128)S(1)}, s32[48,128]{1,0:T(8,128)S(1)}) custom-call(bf16[48,1664]{1,0:T(8,128)(2,1)S(1)} %copy-done.4, bf16[48,1664]{1,0:T(8,128)(2,1)S(1)} %collective-permute-done.4.refs_1_.refs_3_, ...), custom_call_target="tpu_custom_call" | custom-call | flops 19200000000 | bytes 4000000 | tf_op jit(solution)/shard_map/spread/pallas_call | solution.py:566
  38.2 13.9 %spread.3 = (f32[3120,128]{1,0:T(8,128)S(1)}, s32[48,128]{1,0:T(8,128)S(1)}, s32[48,128]{1,0:T(8,128)S(1)}, s32[48,128]{1,0:T(8,128)S(1)}, s32[48,128]{1,0:T(8,1...) custom-call(bf16[48,1664]{1,0:T(8,128)(2,1)S(1)} %collective-permute-done.r, ...), custom_call_target="tpu_custom_call", output_to_operand_aliasing={{0}: (6, {})} | custom-call | flops 19200000000 | bytes 4000000 | tf_op jit(solution)/shard_map/spread/pallas_call | solution.py:566
  52.2 1.7 %collective-permute-done.7 = bf16[1536,128]{1,0:T(8,128)(2,1)S(1)} collective-permute-done((bf16[1536,128]{1,0:T(8,128)(2,1)S(1)}, bf16[1536,128]{1,0:T(8,128)(2,1)S(1)}, u32[]{:S(2)}, u32[]{:S(2)}) %collective-permute-start.7) | collective-permute-done | bytes 393248 | tf_op jit(solution)/shard_map/ppermute | solution.py:594
  54.0 1.7 %collective-permute-start.10 = (bf16[1536,128]{1,0:T(8,128)(2,1)S(1)}, bf16[1536,128]{1,0:T(8,128)(2,1)S(1)}, u32[]{:S(2)}, u32[]{:S(2)}) collective-permute-start(bf16[1536,128]{1,0:T(8,128)(2,1)S(1)} %add_convert_fusion.1), channel_id=1, source_target_pairs={{0,2},{1,3},{2,0},{3,1},{4,6},{5,7},{6,4},{7,5},{8,10},{9,11},{10,... | collective-permute-start | bytes 1179656 | tf_op jit(solution)/shard_map/ppermute | solution.py:623
  55.7 4.1 %collective-permute-start.8 = (bf16[384,128]{1,0:T(8,128)(2,1)S(1)}, bf16[384,128]{1,0:T(8,128)(2,1)S(1)}, u32[]{:S(2)}, u32[]{:S(2)}) collective-permute-start(bf16[384,128]{1,0:T(8,128)(2,1)S(1)} %get-tuple-element.110), channel_id=1, source_target_pairs={{0,4},{4,8},{8,12},{12,16},{16,20},{20,24},{24,28},{1,5},{5,9},{9,... | collective-permute-start | bytes 294920 | tf_op jit(solution)/shard_map/ppermute | solution.py:618
  59.8 1.5 %collective-permute-start.9 = (bf16[384,128]{1,0:T(8,128)(2,1)S(1)}, bf16[384,128]{1,0:T(8,128)(2,1)S(1)}, u32[]{:S(2)}, u32[]{:S(2)}) collective-permute-start(bf16[384,128]{1,0:T(8,128)(2,1)S(1)} %get-tuple-element.111), channel_id=1, source_target_pairs={{4,0},{8,4},{12,8},{16,12},{20,16},{24,20},{28,24},{5,1},{9,5},{13... | collective-permute-start | bytes 294920 | tf_op jit(solution)/shard_map/ppermute | solution.py:619
  62.1 3.9 %weights.2 = (f32[12,128,384]{2,1,0:T(8,128)S(1)}, bf16[12,1024,384]{2,1,0:T(8,128)(2,1)S(1)}) custom-call(bf16[48,1664]{1,0:T(8,128)(2,1)S(1)} %collective-permute-done.refs_0_, bf16[48,1664]{1,0:T(8,128)(2,1)S(1)} %collective-permute-done.1.refs_1_, bf16[1024,128]{1,0:T(8,128)(2,1)S(1)} %get-tuple-element.77.refs_2_.refs_3_.refs_7_), custom_call_target="tpu_custom_call" | custom-call | flops 4800000000 | bytes 4000000 | tf_op jit(solution)/shard_map/weights/pallas_call | solution.py:598
  67.2 4.0 %weights.3 = (f32[12,128,384]{2,1,0:T(8,128)S(1)}, bf16[12,1024,384]{2,1,0:T(8,128)(2,1)S(1)}) custom-call(bf16[48,1664]{1,0:T(8,128)(2,1)S(1)} %collective-permute-done.2.refs_2_.refs_0_, bf16[48,1664]{1,0:T(8,128)(2,1)S(1)} %collective-permute-done.3.refs_3_.refs_1_, bf16[1024,128]{1,0:T(8,128)(2,1)S(1)} %get-tuple-element.77.refs_2_.refs_3_.refs_7_), custom_call_target="tpu_custom_call" | custom-call | flops 4800000000 | bytes 4000000 | tf_op jit(solution)/shard_map/weights/pallas_call | solution.py:598
  71.1 1.6 %collective-permute-done.11 = bf16[768,128]{1,0:T(8,128)(2,1)S(1)} collective-permute-done((bf16[768,128]{1,0:T(8,128)(2,1)S(1)}, bf16[768,128]{1,0:T(8,128)(2,1)S(1)}, u32[]{:S(2)}, u32[]{:S(2)}) %collective-permute-start.11) | collective-permute-done | bytes 196640 | tf_op jit(solution)/shard_map/ppermute | solution.py:626
  72.9 2.0 %collective-permute-done.12.refs_10_ = bf16[2304,128]{1,0:T(8,128)(2,1)S(1)} collective-permute-done((bf16[2304,128]{1,0:T(8,128)(2,1)S(1)}, bf16[2304,128]{1,0:T(8,128)(2,1)S(1)}, u32[]{:S(2)}, u32[]{:S(2)}) %collective-permute-start.12) | collective-permute-done | bytes 589856 | tf_op jit(solution)/shard_map/ppermute | solution.py:632
  74.9 12.1 %sample.3 = (f32[3120,128]{1,0:T(8,128)S(1)}, f32[768,128]{1,0:T(8,128)}, bf16[48,512]{1,0:T(8,128)(2,1)S(1)}, bf16[48,512]{1,0:T(8,128)(2,1)S(1)}, bf16[48,512]...) custom-call(s32[48,128]{1,0:T(8,128)S(1)} %get-tuple-element.67.refs_0_, s32[48,128]{1,0:T(8,128)S(1)} %get-tuple-element.68.refs_1_, ...), custom_call_target="tpu_custom_call" | custom-call | flops 9600000000 | bytes 4000000 | tf_op jit(solution)/shard_map/sample/pallas_call | solution.py:641
  87.0 5.5 %collective-permute-start.16 = (bf16[48,512]{1,0:T(8,128)(2,1)S(1)}, bf16[48,512]{1,0:T(8,128)(2,1)S(1)}, u32[]{:S(2)}, u32[]{:S(2)}) collective-permute-start(bf16[48,512]{1,0:T(8,128)(2,1)S(1)} %get-tuple-element.106), channel_id=1, source_target_pairs={{0,16},{4,20},{8,24},{12,28},{16,0},{20,4},{24,8},{28,12},{1,17},{... | collective-permute-start | bytes 147464 | tf_op jit(solution)/shard_map/ppermute | solution.py:513
  93.8 3.5 %collective-permute-start.19 = (bf16[48,512]{1,0:T(8,128)(2,1)S(1)}, bf16[48,512]{1,0:T(8,128)(2,1)S(1)}, u32[]{:S(2)}, u32[]{:S(2)}) collective-permute-start(bf16[48,512]{1,0:T(8,128)(2,1)S(1)} %get-tuple-element.109), channel_id=1, source_target_pairs={{0,28},{4,24},{8,20},{12,16},{16,12},{20,8},{24,4},{28,0},{1,29},{... | collective-permute-start | bytes 147464 | tf_op jit(solution)/shard_map/ppermute | solution.py:513
  97.4 11.1 %sample.5 = (bf16[48,512]{1,0:T(8,128)(2,1)S(1)}, bf16[48,512]{1,0:T(8,128)(2,1)S(1)}, bf16[48,512]{1,0:T(8,128)(2,1)S(1)}) custom-call(s32[48,128]{1,0:T(8,128)S(1)} %get-tuple-element.100.refs_0_, s32[48,128]{1,0:T(8,128)S(1)} %get-tuple-element.101.refs_1_, s32[48,128]{1,0:T(8,128)S(1)} %get-tuple-element.102.refs_2_, ...), custom_call_target="tpu_custom_call" | custom-call | flops 7200000000 | bytes 4000000 | tf_op jit(solution)/shard_map/sample/pallas_call | solution.py:641
  109.1 3.0 %collective-permute-start.15 = (bf16[48,512]{1,0:T(8,128)(2,1)S(1)}, bf16[48,512]{1,0:T(8,128)(2,1)S(1)}, u32[]{:S(2)}, u32[]{:S(2)}) collective-permute-start(bf16[48,512]{1,0:T(8,128)(2,1)S(1)} %get-tuple-element.105), channel_id=1, source_target_pairs={{0,12},{4,8},{8,4},{12,0},{16,28},{20,24},{24,20},{28,16},{1,13},{... | collective-permute-start | bytes 147464 | tf_op jit(solution)/shard_map/ppermute | solution.py:513
  112.1 4.4 %sample.4.refs_1_ = bf16[48,512]{1,0:T(8,128)(2,1)S(1)} custom-call(s32[48,128]{1,0:T(8,128)S(1)} %get-tuple-element.98.refs_0_, bf16[48,1664]{1,0:T(8,128)(2,1)S(1)} %copy-done.5, bf16[1152,512]{1,0:T(8,128)(2,1)S(1)} %get-tuple-element.94.refs_8_.refs_2_.refs_6_, bf16[1024,128]{1,0:T(8,128)(2,1)S(1)} %get-tuple-element.77.refs_2_.refs_3_.refs_7_, ...), custom_call_target="tpu_custom_call" | custom-call | flops 2400000000 | bytes 4000000 | tf_op jit(solution)/shard_map/sample/pallas_call | solution.py:641
  116.5 1.3 %unpack.1 = bf16[3,169,192]{2,1,0:T(8,128)(2,1)} custom-call(s32[1,192]{1,0:T(1,128)S(1)} %copy-done.2, bf16[48,512]{1,0:T(8,128)(2,1)S(1)} %sample.4.refs_1_, bf16[48,512]{1,0:T(8,128)(2,1)S(1)} %collective-permute-done.13.refs_2_, bf16[48,512]{1,0:T(8,128)(2,1)S(1)} %collective-permute-done.14.refs_3_, ...), custom_call_target="tpu_custom_call" | custom-call | tf_op jit(solution)/shard_map/unpack/pallas_call | solution.py:669
  (46 shorter events, 8.8 us)
Async XLA Ops:
  4.0 10.3 %collective-permute-start.4 = (bf16[48,1664]{1,0:T(8,128)(2,1)}, bf16[48,1664]{1,0:T(8,128)(2,1)S(1)}, u32[]{:S(2)}, u32[]{:S(2)}) collective-permute-start(bf16[48,1664]{1,0:T(8,128)(2,1)} %get-tuple-element.63), channel_id=1, source_target_pairs={{0,4},{4,0},{8,12},{12,8},{16,20},{20,16},{24,28},{28,24},{1,5},{5... | collective-permute-start | bytes 479240 | tf_op jit(solution)/shard_map/ppermute | solution.py:513
  7.0 13.0 %collective-permute-start.5 = (bf16[48,1664]{1,0:T(8,128)(2,1)}, bf16[48,1664]{1,0:T(8,128)(2,1)S(1)}, u32[]{:S(2)}, u32[]{:S(2)}) collective-permute-start(bf16[48,1664]{1,0:T(8,128)(2,1)} %get-tuple-element.64), channel_id=1, source_target_pairs={{0,8},{4,12},{8,0},{12,4},{16,24},{20,28},{24,16},{28,20},{1,9},{5... | collective-permute-start | bytes 479240 | tf_op jit(solution)/shard_map/ppermute | solution.py:513
  8.5 12.8 %collective-permute-start.6 = (bf16[48,1664]{1,0:T(8,128)(2,1)}, bf16[48,1664]{1,0:T(8,128)(2,1)S(1)}, u32[]{:S(2)}, u32[]{:S(2)}) collective-permute-start(bf16[48,1664]{1,0:T(8,128)(2,1)} %get-tuple-element.65), channel_id=1, source_target_pairs={{0,12},{4,8},{8,4},{12,0},{16,28},{20,24},{24,20},{28,16},{1,13},{... | collective-permute-start | bytes 479240 | tf_op jit(solution)/shard_map/ppermute | solution.py:513
  8.6 29.6 %collective-permute-start = (bf16[48,1664]{1,0:T(8,128)(2,1)}, bf16[48,1664]{1,0:T(8,128)(2,1)S(1)}, u32[]{:S(2)}, u32[]{:S(2)}) collective-permute-start(bf16[48,1664]{1,0:T(8,128)(2,1)} %get-tuple-element.56), channel_id=1, source_target_pairs={{0,16},{4,20},{8,24},{12,28},{16,0},{20,4},{24,8},{28,12},{1,17},{... | collective-permute-start | bytes 479240 | tf_op jit(solution)/shard_map/ppermute | solution.py:513
  11.5 26.6 %collective-permute-start.1 = (bf16[48,1664]{1,0:T(8,128)(2,1)}, bf16[48,1664]{1,0:T(8,128)(2,1)S(1)}, u32[]{:S(2)}, u32[]{:S(2)}) collective-permute-start(bf16[48,1664]{1,0:T(8,128)(2,1)} %get-tuple-element.57), channel_id=1, source_target_pairs={{0,20},{4,16},{8,28},{12,24},{16,4},{20,0},{24,12},{28,8},{1,21},{... | collective-permute-start | bytes 479240 | tf_op jit(solution)/shard_map/ppermute | solution.py:513
  14.3 23.9 %collective-permute-start.2 = (bf16[48,1664]{1,0:T(8,128)(2,1)}, bf16[48,1664]{1,0:T(8,128)(2,1)S(1)}, u32[]{:S(2)}, u32[]{:S(2)}) collective-permute-start(bf16[48,1664]{1,0:T(8,128)(2,1)} %get-tuple-element.58), channel_id=1, source_target_pairs={{0,24},{4,28},{8,16},{12,20},{16,8},{20,12},{24,0},{28,4},{1,25},{... | collective-permute-start | bytes 479240 | tf_op jit(solution)/shard_map/ppermute | solution.py:513
  20.0 18.2 %collective-permute-start.3 = (bf16[48,1664]{1,0:T(8,128)(2,1)}, bf16[48,1664]{1,0:T(8,128)(2,1)S(1)}, u32[]{:S(2)}, u32[]{:S(2)}) collective-permute-start(bf16[48,1664]{1,0:T(8,128)(2,1)} %get-tuple-element.59), channel_id=1, source_target_pairs={{0,28},{4,24},{8,20},{12,16},{16,12},{20,8},{24,4},{28,0},{1,29},{... | collective-permute-start | bytes 479240 | tf_op jit(solution)/shard_map/ppermute | solution.py:513
  21.3 1.0 copy-start.3
  52.1 9.3 %copy-start.1 = (bf16[169,338]{1,0:T(8,128)(2,1)S(1)}, bf16[169,338]{1,0:T(8,128)(2,1)}, u32[]{:S(2)}) copy-start(bf16[169,338]{1,0:T(8,128)(2,1)} %refs_0_.2) | copy-start | bytes 342736
  52.1 1.8 %collective-permute-start.7 = (bf16[1536,128]{1,0:T(8,128)(2,1)S(1)}, bf16[1536,128]{1,0:T(8,128)(2,1)S(1)}, u32[]{:S(2)}, u32[]{:S(2)}) collective-permute-start(bf16[1536,128]{1,0:T(8,128)(2,1)S(1)} %get-tuple-element.72), channel_id=1, source_target_pairs={{0,1},{1,0},{2,3},{3,2},{4,5},{5,4},{6,7},{7,6},{8,9},{9,8},{10,11... | collective-permute-start | bytes 1179656 | tf_op jit(solution)/shard_map/ppermute | solution.py:594
  54.0 12.4 %collective-permute-start.10 = (bf16[1536,128]{1,0:T(8,128)(2,1)S(1)}, bf16[1536,128]{1,0:T(8,128)(2,1)S(1)}, u32[]{:S(2)}, u32[]{:S(2)}) collective-permute-start(bf16[1536,128]{1,0:T(8,128)(2,1)S(1)} %add_convert_fusion.1), channel_id=1, source_target_pairs={{0,2},{1,3},{2,0},{3,1},{4,6},{5,7},{6,4},{7,5},{8,10},{9,11},{10,... | collective-permute-start | bytes 1179656 | tf_op jit(solution)/shard_map/ppermute | solution.py:623
  55.7 10.3 %collective-permute-start.8 = (bf16[384,128]{1,0:T(8,128)(2,1)S(1)}, bf16[384,128]{1,0:T(8,128)(2,1)S(1)}, u32[]{:S(2)}, u32[]{:S(2)}) collective-permute-start(bf16[384,128]{1,0:T(8,128)(2,1)S(1)} %get-tuple-element.110), channel_id=1, source_target_pairs={{0,4},{4,8},{8,12},{12,16},{16,20},{20,24},{24,28},{1,5},{5,9},{9,... | collective-permute-start | bytes 294920 | tf_op jit(solution)/shard_map/ppermute | solution.py:618
  59.8 6.5 %collective-permute-start.9 = (bf16[384,128]{1,0:T(8,128)(2,1)S(1)}, bf16[384,128]{1,0:T(8,128)(2,1)S(1)}, u32[]{:S(2)}, u32[]{:S(2)}) collective-permute-start(bf16[384,128]{1,0:T(8,128)(2,1)S(1)} %get-tuple-element.111), channel_id=1, source_target_pairs={{4,0},{8,4},{12,8},{16,12},{20,16},{24,20},{28,24},{5,1},{9,5},{13... | collective-permute-start | bytes 294920 | tf_op jit(solution)/shard_map/ppermute | solution.py:619
  66.5 6.2 %collective-permute-start.11 = (bf16[768,128]{1,0:T(8,128)(2,1)S(1)}, bf16[768,128]{1,0:T(8,128)(2,1)S(1)}, u32[]{:S(2)}, u32[]{:S(2)}) collective-permute-start(bf16[768,128]{1,0:T(8,128)(2,1)S(1)} %pad_maximum_fusion.1), channel_id=1, source_target_pairs={{0,2},{1,3},{2,0},{3,1},{4,6},{5,7},{6,4},{7,5},{8,10},{9,11},{10,... | collective-permute-start | bytes 589832 | tf_op jit(solution)/shard_map/ppermute | solution.py:626
  72.8 2.1 %collective-permute-start.12 = (bf16[2304,128]{1,0:T(8,128)(2,1)S(1)}, bf16[2304,128]{1,0:T(8,128)(2,1)S(1)}, u32[]{:S(2)}, u32[]{:S(2)}) collective-permute-start(bf16[2304,128]{1,0:T(8,128)(2,1)S(1)} %pad_maximum_fusion.refs_9_), channel_id=1, source_target_pairs={{0,1},{1,0},{2,3},{3,2},{4,5},{5,4},{6,7},{7,6},{8,9},{9,8},{10,11... | collective-permute-start | bytes 1769480 | tf_op jit(solution)/shard_map/ppermute | solution.py:632
  87.0 22.0 %collective-permute-start.16 = (bf16[48,512]{1,0:T(8,128)(2,1)S(1)}, bf16[48,512]{1,0:T(8,128)(2,1)S(1)}, u32[]{:S(2)}, u32[]{:S(2)}) collective-permute-start(bf16[48,512]{1,0:T(8,128)(2,1)S(1)} %get-tuple-element.106), channel_id=1, source_target_pairs={{0,16},{4,20},{8,24},{12,28},{16,0},{20,4},{24,8},{28,12},{1,17},{... | collective-permute-start | bytes 147464 | tf_op jit(solution)/shard_map/ppermute | solution.py:513
  92.6 16.5 %collective-permute-start.17 = (bf16[48,512]{1,0:T(8,128)(2,1)S(1)}, bf16[48,512]{1,0:T(8,128)(2,1)S(1)}, u32[]{:S(2)}, u32[]{:S(2)}) collective-permute-start(bf16[48,512]{1,0:T(8,128)(2,1)S(1)} %get-tuple-element.107), channel_id=1, source_target_pairs={{0,20},{4,16},{8,28},{12,24},{16,4},{20,0},{24,12},{28,8},{1,21},{... | collective-permute-start | bytes 147464 | tf_op jit(solution)/shard_map/ppermute | solution.py:513
  92.6 23.9 %collective-permute-start.18 = (bf16[48,512]{1,0:T(8,128)(2,1)S(1)}, bf16[48,512]{1,0:T(8,128)(2,1)S(1)}, u32[]{:S(2)}, u32[]{:S(2)}) collective-permute-start(bf16[48,512]{1,0:T(8,128)(2,1)S(1)} %get-tuple-element.108), channel_id=1, source_target_pairs={{0,24},{4,28},{8,16},{12,20},{16,8},{20,12},{24,0},{28,4},{1,25},{... | collective-permute-start | bytes 147464 | tf_op jit(solution)/shard_map/ppermute | solution.py:513
  93.8 22.6 %collective-permute-start.19 = (bf16[48,512]{1,0:T(8,128)(2,1)S(1)}, bf16[48,512]{1,0:T(8,128)(2,1)S(1)}, u32[]{:S(2)}, u32[]{:S(2)}) collective-permute-start(bf16[48,512]{1,0:T(8,128)(2,1)S(1)} %get-tuple-element.109), channel_id=1, source_target_pairs={{0,28},{4,24},{8,20},{12,16},{16,12},{20,8},{24,4},{28,0},{1,29},{... | collective-permute-start | bytes 147464 | tf_op jit(solution)/shard_map/ppermute | solution.py:513
  97.4 14.7 %copy-start.5 = (bf16[48,1664]{1,0:T(8,128)(2,1)S(1)}, bf16[48,1664]{1,0:T(8,128)(2,1)}, u32[]{:S(2)}) copy-start(bf16[48,1664]{1,0:T(8,128)(2,1)} %get-tuple-element.62.refs_0_.refs_1_) | copy-start | bytes 479236
  108.5 8.0 %collective-permute-start.13 = (bf16[48,512]{1,0:T(8,128)(2,1)S(1)}, bf16[48,512]{1,0:T(8,128)(2,1)S(1)}, u32[]{:S(2)}, u32[]{:S(2)}) collective-permute-start(bf16[48,512]{1,0:T(8,128)(2,1)S(1)} %get-tuple-element.103), channel_id=1, source_target_pairs={{0,4},{4,0},{8,12},{12,8},{16,20},{20,16},{24,28},{28,24},{1,5},{5... | collective-permute-start | bytes 147464 | tf_op jit(solution)/shard_map/ppermute | solution.py:513
  109.1 7.4 %collective-permute-start.14 = (bf16[48,512]{1,0:T(8,128)(2,1)S(1)}, bf16[48,512]{1,0:T(8,128)(2,1)S(1)}, u32[]{:S(2)}, u32[]{:S(2)}) collective-permute-start(bf16[48,512]{1,0:T(8,128)(2,1)S(1)} %get-tuple-element.104), channel_id=1, source_target_pairs={{0,8},{4,12},{8,0},{12,4},{16,24},{20,28},{24,16},{28,20},{1,9},{5... | collective-permute-start | bytes 147464 | tf_op jit(solution)/shard_map/ppermute | solution.py:513
  109.1 7.4 %collective-permute-start.15 = (bf16[48,512]{1,0:T(8,128)(2,1)S(1)}, bf16[48,512]{1,0:T(8,128)(2,1)S(1)}, u32[]{:S(2)}, u32[]{:S(2)}) collective-permute-start(bf16[48,512]{1,0:T(8,128)(2,1)S(1)} %get-tuple-element.105), channel_id=1, source_target_pairs={{0,12},{4,8},{8,4},{12,0},{16,28},{20,24},{24,20},{28,16},{1,13},{... | collective-permute-start | bytes 147464 | tf_op jit(solution)/shard_map/ppermute | solution.py:513
  112.1 4.4 %copy-start.2 = (s32[1,192]{1,0:T(1,128)S(1)}, s32[1,192]{1,0:T(1,128)}, u32[]{:S(2)}) copy-start(s32[1,192]{1,0:T(1,128)} %get-tuple-element.97.refs_0_) | copy-start | bytes 2308
  (2 other events, 1.8 us)
